TPU v7x, 32 devices: a whole 2x2x4 slice. The times are simulated.
32 devices in a mesh: grp: 2 (over y), blk: 4 (over z), walk: 2 (over x), sub: 2 (over core).
Axes of the slice: x: 2, y: 2, z: 4, core: 2. Of those that a mesh axis runs over, the one named last changes fastest.
Arguments:
- walker_mats: bfloat16 [8, 2048, 2048], P(('grp', 'blk'), 'walk'), parts along dimension 0, may hold values from -0.0029296875 to 0.0029296875
- vertex: int32 [8, 2048], P(('grp', 'blk')), parts along dimension 0, may hold values from 0 to 8191
- weights: float32 [8], P('grp'), parts along dimension 0, may hold values from 0.5 to 1.5
- transfer_table: int32 [16, 2560], replicated, may hold values from 0 to 2559, each once within a row
- g4_old: float32 [32, 16, 2560], P(('grp', 'blk', 'walk', 'sub')), parts along dimension 0, may hold values from -2 to 2
Outputs:
- g4_new: float32 [32, 16, 2560], P(('grp', 'blk', 'walk', 'sub')), parts along dimension 0
There are 2 independent parts, one for each index of `grp`. A program takes and returns all parts, laid end to end along the dimension named above; an argument that names none is the same for every part. Nothing has to cross between parts.
All inputs are finite; a program needn't handle non-finite values.
Results may differ from a plain program's by a relative error of at most 0.0041.
Values may be sent and summed in bfloat16 or wider, within the bound.
No kernel may reach another device: no remote copies, remote signals or barrier semaphores. Data moves between devices by JAX's collectives and lax.ppermute only.
A program may use at most 64 MiB of HBM per device.

v0:
```python
import functools
import itertools
import math

import jax
import jax.numpy as jnp
from jax import lax
from jax.experimental import pallas as pl
from jax.experimental.pallas import tpu as pltpu
from jax.sharding import PartitionSpec as P

TQ = 4
RSTEPS = 4


phase_period = 8192
quarter_bits = 11
lanes = 128
lane_bits = 7
sublanes = 8
code_limit = 32767.0
smallest_peak = 1e-30


def toward(index, distance, count):
    if count & (count - 1) == 0:
        return index ^ distance
    return (index + distance) % count


def back(index, distance, count):
    if count & (count - 1) == 0:
        return index ^ distance
    return (index + count - distance) % count


def cos_sin(product):
    residue = product & (phase_period - 1)
    quarter = (residue + phase_period // 8) >> quarter_bits
    angle = (residue - (quarter << quarter_bits)).astype(jnp.float32) * (2.0 * math.pi / phase_period)
    square = angle * angle
    sine = angle + angle * square * (
        -1.0 / 6.0 + square * (1.0 / 120.0 + square * (-1.0 / 5040.0 + square * (1.0 / 362880.0)))
    )
    cosine = 1.0 + square * (
        -0.5 + square * (1.0 / 24.0 + square * (-1.0 / 720.0 + square * (1.0 / 40320.0)))
    )
    odd = (quarter & 1) == 1
    cosine_out = jnp.where(odd, sine, cosine)
    sine_out = jnp.where(odd, cosine, sine)
    cosine_out = jnp.where(((quarter + 1) & 2) == 2, -cosine_out, cosine_out)
    sine_out = jnp.where((quarter & 2) == 2, -sine_out, sine_out)
    return cosine_out, sine_out


def row_ids(count):
    return lax.broadcasted_iota(jnp.int32, (count, lanes), 0)


def split_by(ids, size):
    if size & (size - 1) == 0:
        return ids >> (size.bit_length() - 1), ids & (size - 1)
    return ids // size, ids % size


def table_kernel(sizes, vertex_ref, table_ref, left_ref):
    blk_count, walk_count, sub_count, rows_own = sizes
    walk_index = lax.axis_index("walk")
    sub_index = lax.axis_index("sub")
    columns, vertices = table_ref.shape
    window_rows, rows_local = left_ref.shape

    ids, inner = split_by(row_ids(window_rows), rows_own)
    ids, blk_part = split_by(ids, blk_count)
    walk_part, sub_part = split_by(ids, sub_count)
    sub_part = toward(sub_index, sub_part, sub_count)
    walk_part = toward(walk_index, walk_part, walk_count)
    window = ((blk_part * walk_count + walk_part) * sub_count + sub_part) * rows_own + inner
    own_start = pl.multiple_of(walk_index * rows_local, lanes)
    for start in range(0, rows_local, lanes):
        own_vertex = vertex_ref[:, pl.ds(own_start + start, lanes)]
        cosine, sine = cos_sin(own_vertex * window)
        left_ref[:, start : start + lanes] = (cosine + sine).astype(jnp.bfloat16)

    blocks = columns // lanes
    half_blocks = blocks // 2
    coarse_rows = -(-max(half_blocks, 1) // sublanes) * sublanes
    middle_count = lanes // sublanes
    center = sub_index * columns + (blocks - 1) * (lanes // 2)

    def angles(step):
        vertex = vertex_ref[:, pl.ds(pl.multiple_of(step * lanes, lanes), lanes)]
        cosine, sine = cos_sin(vertex * (row_ids(sublanes) + center))
        return (
            cosine + sine,
            cosine - sine,
            *cos_sin(vertex * (row_ids(middle_count) * sublanes)),
            *cos_sin(vertex * ((blocks - 1 - 2 * row_ids(coarse_rows)) * (lanes // 2))),
        )

    def table_step(step, carried):
        following = angles(jnp.minimum(step + 1, steps - 1))
        cas_fine, cam_fine, cos_middle, sin_middle, cos_coarse, sin_coarse = carried
        here = pl.ds(pl.multiple_of(step * lanes, lanes), lanes)
        for pair in range(middle_count // 2):
            cas, cam = [], []
            for middle in (2 * pair, 2 * pair + 1):
                c, s = cos_middle[middle : middle + 1], sin_middle[middle : middle + 1]
                cas.append(c * cas_fine + s * cam_fine)
                cam.append(c * cam_fine - s * cas_fine)
            cas, cam = jnp.concatenate(cas, axis=0), jnp.concatenate(cam, axis=0)
            start = pair * 2 * sublanes
            for low in range(half_blocks):
                high = blocks - 1 - low
                even = cos_coarse[low : low + 1] * cas
                odd = sin_coarse[low : low + 1] * cam
                for block, value in ((low, even - odd), (high, even + odd)):
                    first = block * lanes + start
                    table_ref[first : first + 2 * sublanes, here] = value.astype(jnp.bfloat16)
            if blocks % 2:
                first = half_blocks * lanes + start
                table_ref[first : first + 2 * sublanes, here] = cas.astype(jnp.bfloat16)
        return following

    steps = vertices // lanes
    lax.fori_loop(0, steps, table_step, angles(0))


def product_kernel(sizes, matrix_ref, table_ref, left_ref, *rest):
    *sent_refs, weight_ref = rest
    blk_count, _, _, rows_own = sizes
    vertices = matrix_ref.shape[2]
    window_rows = left_ref.shape[0]

    chunk = 4 * lanes
    for start in range(0, vertices, chunk):
        left_product = jnp.dot(
            left_ref[...], matrix_ref[0, :, start : start + chunk], preferred_element_type=jnp.float32
        )
        high = left_product.astype(jnp.bfloat16)
        weight_ref[:window_rows, start : start + chunk] = high
        weight_ref[window_rows:, start : start + chunk] = (
            left_product - high.astype(jnp.float32)
        ).astype(jnp.bfloat16)
    green = lax.dot_general(
        weight_ref[...], table_ref[...], (((1,), (1,)), ((), ())), preferred_element_type=jnp.float32
    )
    green = green[:window_rows] + green[window_rows:]
    rows_each = blk_count * rows_own
    for place, sent_ref in enumerate(sent_refs):
        sent_ref[...] = green[place * rows_each : (place + 1) * rows_each]


def pick_rows(rows, wanted):
    ids = lax.broadcasted_iota(jnp.int32, (wanted.shape[0], rows.shape[0]), 1)
    chosen = jnp.where(ids == wanted, 1.0, 0.0).astype(jnp.bfloat16)
    return jnp.dot(chosen, rows, preferred_element_type=jnp.float32)


def combine_kernel(sizes, *refs):
    blk_count, walk_count, sub_count, rows_own = sizes
    blk_index = lax.axis_index("blk")
    sub_index = lax.axis_index("sub")
    part_refs, whole_refs = refs[: walk_count * sub_count], refs[walk_count * sub_count :]
    columns_part = part_refs[0].shape[1]
    for distance in range(sub_count):
        sub_part = back(sub_index, distance, sub_count)
        here = pl.ds(pl.multiple_of(sub_part * columns_part, lanes), columns_part)
        total = sum(
            part_refs[walk_part * sub_count + distance][...] for walk_part in range(walk_count)
        ).astype(jnp.bfloat16)
        if len(whole_refs) == 1:
            whole_refs[0][:, here] = total
            continue
        for place, whole_ref in enumerate(whole_refs):
            ids = lax.broadcasted_iota(jnp.int32, (whole_ref.shape[0], 1), 0)
            step, inner = split_by(ids, rows_own)
            _, blk_part = split_by(toward(blk_index, place, blk_count) + RSTEPS * blk_count - step, blk_count)
            whole_ref[:, here] = pick_rows(total, blk_part * rows_own + inner).astype(whole_ref.dtype)


def accumulate_kernel(sizes, distances, weights_ref, transfer_ref, old_ref, *rest):
    *arrived_refs, new_ref, source_ref, left_ref, unit_ref = rest
    blk_count, _, _, rows_own = sizes
    blk_index = lax.axis_index("blk")
    transfers, columns = transfer_ref.shape
    half = columns // 2
    groups = transfers // sublanes
    tiles = columns // lanes
    weights = weights_ref[...] * (1.0 / blk_count)
    walker_ids = lax.broadcasted_iota(jnp.int32, weights.shape, 1)

    ids = lax.broadcasted_iota(jnp.int32, (transfers, 1), 0)
    step, _ = split_by(ids, TQ)
    if arrived_refs[0].shape[0] == blk_count * rows_own:
        _, step = split_by(blk_index + RSTEPS * blk_count - step, blk_count)

    for own in range(rows_own):
        for place, distance in enumerate(distances):
            rows = pick_rows(arrived_refs[place][...], step * rows_own + own)
            walker = back(blk_index, distance, blk_count)
            weight = jnp.sum(jnp.where(walker_ids == walker, weights, 0.0), axis=1, keepdims=True)
            left_ref[place] = rows[:1] * weight
            peak = jnp.maximum(jnp.max(jnp.abs(rows), axis=1, keepdims=True), smallest_peak)
            codes = jnp.floor(rows * (code_limit / peak) + 0.5).astype(jnp.int32)
            unit_ref[place] = jnp.broadcast_to(peak * (1.0 / code_limit), (transfers, lanes))
            source_ref[place] = (codes[:, :half] << 16) | (codes[:, half:] & 0xFFFF)

        together = len(distances) if len(distances) <= 4 else math.gcd(len(distances), 4)

        @pl.loop(0, tiles, unroll=math.gcd(tiles, 10))
        def _(tile):
            here = pl.ds(pl.multiple_of(tile * lanes, lanes), lanes)
            for group in range(groups):
                rows = slice(group * sublanes, (group + 1) * sublanes)
                index = transfer_ref[rows, here]
                index_lane = index & (lanes - 1)
                in_first = index < half
                index_tile = jnp.where(in_first, index, index - half) >> lane_bits

                def add_walkers(first, total):
                    picked = [jnp.zeros((sublanes, lanes), jnp.int32)] * together
                    for source in range(half // lanes):
                        match = index_tile == source
                        for k in range(together):
                            words = source_ref[
                                first + k, rows, source * lanes : (source + 1) * lanes
                            ]
                            words = jnp.take_along_axis(
                                words, index_lane, axis=1, mode="promise_in_bounds"
                            )
                            picked[k] = jnp.where(match, words, picked[k])
                    for k in range(together):
                        code = jnp.where(in_first, picked[k], picked[k] << 16) >> 16
                        total = total + left_ref[first + k, :, here] * (
                            unit_ref[first + k, rows] * code.astype(jnp.float32)
                        )
                    return total

                total = old_ref[own, rows, here]
                if len(distances) == together:
                    total = add_walkers(0, total)
                else:
                    total = lax.fori_loop(
                        0, len(distances) // together, lambda i, t: add_walkers(i * together, t), total
                    )
                new_ref[own, rows, here] = total


def exchange(pieces, axes, counts):
    positions = list(itertools.product(*map(range, counts)))
    place = {position: i for i, position in enumerate(positions)}
    arrived = [pieces[0]] * len(positions)
    for i in range(1, len(positions)):
        route = [
            (place[position], place[tuple(map(toward, position, positions[i], counts))])
            for position in positions
        ]
        arrived[i] = lax.ppermute(pieces[i], axes, route)
    return arrived


def local(walker_mats, vertex, weights, transfer_table, g4_old):
    blk_count = lax.axis_size("blk")
    walk_count = lax.axis_size("walk")
    sub_count = lax.axis_size("sub")
    rows_local, vertices = walker_mats.shape[1:]
    rows_own, transfers, columns = g4_old.shape
    columns_local = columns // sub_count
    devices = blk_count * walk_count * sub_count
    sizes = (blk_count, walk_count, sub_count, rows_own)
    vmem = pl.BlockSpec(memory_space=pltpu.VMEM)
    table, left = pl.pallas_call(
        functools.partial(table_kernel, sizes),
        out_shape=[
            jax.ShapeDtypeStruct((columns_local, vertices), jnp.bfloat16),
            jax.ShapeDtypeStruct((devices * rows_own, rows_local), jnp.bfloat16),
        ],
        in_specs=[vmem],
        out_specs=[vmem] * 2,
        compiler_params=pltpu.CompilerParams(vmem_limit_bytes=24 * 2**20),
        cost_estimate=pl.CostEstimate(
            flops=2000 * columns_local * vertices,
            bytes_accessed=6 * columns_local * vertices,
            transcendentals=0,
        ),
        name="table",
    )(vertex)
    sent = pl.pallas_call(
        functools.partial(product_kernel, sizes),
        out_shape=[jax.ShapeDtypeStruct((blk_count * rows_own, columns_local), jnp.float32)]
        * (walk_count * sub_count),
        in_specs=[vmem] * 3,
        out_specs=[vmem] * (walk_count * sub_count),
        scratch_shapes=[pltpu.VMEM((2 * devices * rows_own, vertices), jnp.bfloat16)],
        compiler_params=pltpu.CompilerParams(vmem_limit_bytes=24 * 2**20),
        name="product",
    )(walker_mats, table, left)
    parts = exchange(sent, ("walk", "sub"), (walk_count, sub_count))
    shared = blk_count <= RSTEPS
    rows_each = (blk_count if shared else RSTEPS) * rows_own
    whole_count = 1 if shared else blk_count
    whole = pl.pallas_call(
        functools.partial(combine_kernel, sizes),
        out_shape=[jax.ShapeDtypeStruct((rows_each, columns), jnp.bfloat16)] * whole_count,
        in_specs=[vmem] * len(parts),
        out_specs=[vmem] * whole_count,
        compiler_params=pltpu.CompilerParams(vmem_limit_bytes=24 * 2**20),
        name="combine",
    )(*parts)
    arrived = exchange(whole * blk_count if shared else whole, ("blk",), (blk_count,))
    far = blk_count // 2
    totals = g4_old
    for places in ([0, *range(far + 1, blk_count)], [*range(1, far)], [far]):
        totals = pl.pallas_call(
            functools.partial(accumulate_kernel, sizes, places),
            out_shape=jax.ShapeDtypeStruct(g4_old.shape, jnp.float32),
            in_specs=[vmem] * (3 + len(places)),
            out_specs=vmem,
            scratch_shapes=[
                pltpu.VMEM((len(places), transfers, columns // 2), jnp.int32),
                pltpu.VMEM((len(places), 1, columns), jnp.float32),
                pltpu.VMEM((len(places), transfers, lanes), jnp.float32),
            ],
            compiler_params=pltpu.CompilerParams(vmem_limit_bytes=24 * 2**20),
            cost_estimate=pl.CostEstimate(
                flops=1000 * len(places) * transfers * columns,
                bytes_accessed=12 * transfers * columns,
                transcendentals=0,
            ),
            name="accumulate",
        )(weights[None], transfer_table, totals, *[arrived[place] for place in places])
    return totals


def solution(mesh):
    in_specs = (
        P(("grp", "blk"), "walk", None),
        P(("grp", "blk"), None),
        P("grp"),
        P(),
        P(("grp", "blk", "walk", "sub"), None, None),
    )
    out_specs = P(("grp", "blk", "walk", "sub"), None, None)
    return jax.shard_map(local, mesh=mesh, in_specs=in_specs, out_specs=out_specs, check_vma=False)
```

profile of v0, /device:TPU:0, one launch (start us, length us, event | category | flops | bytes accessed | tf_op | source)
XLA Modules:
  0.0 21.7 jit_solution(860553884010257997)
XLA Ops:
  0.0 0.8 %copy-done.4 = s32[1,2048]{1,0:T(1,128)S(1)} copy-done((s32[1,2048]{1,0:T(1,128)S(1)}, s32[1,2048]{1,0:T(1,128)}, u32[]{:S(2)}) %copy-start.4) | copy-done | bytes 8216
  0.8 2.1 %table.1 = (bf16[1280,2048]{1,0:T(8,128)(2,1)S(1)}, bf16[16,1024]{1,0:T(8,128)(2,1)S(1)}) custom-call(s32[1,2048]{1,0:T(1,128)S(1)} %copy-done.4), custom_call_target="tpu_custom_call" | custom-call | flops 5242880000 | bytes 15728640 | tf_op jit(solution)/shard_map/table/pallas_call | solution.py:273
  3.0 0.0 copy-start.1
  3.0 0.0 copy-start.2
  3.0 0.0 copy-start.3
  3.0 0.0 copy-done
  3.0 2.2 %product.1 = (f32[4,1280]{1,0:T(4,128)S(1)}, f32[4,1280]{1,0:T(4,128)S(1)}, f32[4,1280]{1,0:T(4,128)S(1)}, f32[4,1280]{1,0:T(4,128)S(1)}) custom-call(bf16[1,1024,2048]{2,1,0:T(8,128)(2,1)S(1)} %copy-done, bf16[1280,2048]{1,0:T(8,128)(2,1)S(1)} %get-tuple-element.11.table_ref, bf16[16,1024]{1,0:T(8,128)(2,1)S(1)} %get-tuple-element.12.left_ref), custom_call_target="tpu_custom_call" | custom-call | tf_op jit(solution)/shard_map/product/pallas_call | solution.py:289
  5.2 0.5 %collective-permute-start = (f32[4,1280]{1,0:T(4,128)S(1)}, f32[4,1280]{1,0:T(4,128)S(1)}, u32[]{:S(2)}, u32[]{:S(2)}) collective-permute-start(f32[4,1280]{1,0:T(4,128)S(1)} %get-tuple-element.14), channel_id=1, source_target_pairs={{0,1},{1,0},{2,3},{3,2},{4,5},{5,4},{6,7},{7,6},{8,9},{9,8},{10,11... | collective-permute-start | bytes 61448 | tf_op jit(solution)/shard_map/ppermute | solution.py:259
  5.7 2.5 %collective-permute-start.1 = (f32[4,1280]{1,0:T(4,128)S(1)}, f32[4,1280]{1,0:T(4,128)S(1)}, u32[]{:S(2)}, u32[]{:S(2)}) collective-permute-start(f32[4,1280]{1,0:T(4,128)S(1)} %get-tuple-element.15), channel_id=1, source_target_pairs={{0,2},{1,3},{2,0},{3,1},{4,6},{5,7},{6,4},{7,5},{8,10},{9,11},{10,... | collective-permute-start | bytes 61448 | tf_op jit(solution)/shard_map/ppermute | solution.py:259
  8.2 0.1 collective-permute-start.2
  8.3 0.0 collective-permute-done.refs_1_
  8.3 1.6 %collective-permute-done.1.refs_2_ = f32[4,1280]{1,0:T(4,128)S(1)} collective-permute-done((f32[4,1280]{1,0:T(4,128)S(1)}, f32[4,1280]{1,0:T(4,128)S(1)}, u32[]{:S(2)}, u32[]{:S(2)}) %collective-permute-start.1) | collective-permute-done | bytes 20512 | tf_op jit(solution)/shard_map/ppermute | solution.py:259
  10.0 1.4 %collective-permute-done.2.refs_3_ = f32[4,1280]{1,0:T(4,128)S(1)} collective-permute-done((f32[4,1280]{1,0:T(4,128)S(1)}, f32[4,1280]{1,0:T(4,128)S(1)}, u32[]{:S(2)}, u32[]{:S(2)}) %collective-permute-start.2) | collective-permute-done | bytes 20512 | tf_op jit(solution)/shard_map/ppermute | solution.py:259
  11.4 3.7 %collective-permute-start.3 = (bf16[4,2560]{1,0:T(4,128)(2,1)S(1)}, bf16[4,2560]{1,0:T(4,128)(2,1)S(1)}, u32[]{:S(2)}, u32[]{:S(2)}) collective-permute-start(bf16[4,2560]{1,0:T(4,128)(2,1)S(1)} %combine.1.rest_0_), channel_id=1, source_target_pairs={{0,12},{4,8},{8,4},{12,0},{1,13},{5,9},{9,5},{13,1},{2,14},{6,10},... | collective-permute-start | bytes 61448 | tf_op jit(solution)/shard_map/ppermute | solution.py:259
  15.1 0.0 collective-permute-start.4
  15.1 0.8 %collective-permute-start.5 = (bf16[4,2560]{1,0:T(4,128)(2,1)S(1)}, bf16[4,2560]{1,0:T(4,128)(2,1)S(1)}, u32[]{:S(2)}, u32[]{:S(2)}) collective-permute-start(bf16[4,2560]{1,0:T(4,128)(2,1)S(1)} %combine.1.rest_0_), channel_id=1, source_target_pairs={{0,8},{4,12},{8,0},{12,4},{1,9},{5,13},{9,1},{13,5},{2,10},{6,14},... | collective-permute-start | bytes 61448 | tf_op jit(solution)/shard_map/ppermute | solution.py:259
  15.9 1.2 %collective-permute-done.3.rest_1_ = bf16[4,2560]{1,0:T(4,128)(2,1)S(1)} collective-permute-done((bf16[4,2560]{1,0:T(4,128)(2,1)S(1)}, bf16[4,2560]{1,0:T(4,128)(2,1)S(1)}, u32[]{:S(2)}, u32[]{:S(2)}) %collective-permute-start.3) | collective-permute-done | bytes 20512 | tf_op jit(solution)/shard_map/ppermute | solution.py:259
  17.1 0.0 copy-done.1
  17.1 0.0 copy-done.2
  17.1 1.5 %accumulate.3.old_ref = f32[1,16,2560]{2,1,0:T(8,128)S(1)} custom-call(f32[1,4]{1,0:T(1,128)S(1)} %bitcast.1, s32[16,2560]{1,0:T(8,128)S(1)} %copy-done.1, f32[1,16,2560]{2,1,0:T(8,128)S(1)} %copy-done.2, bf16[4,2560]{1,0:T(4,128)(2,1)S(1)} %combine.1.rest_0_, bf16[4,2560]{1,0:T(4,128)(2,1)S(1)} %collective-permute-done.3.rest_1_), custom_call_target="tpu_custom_call" | custom-call | flops 81920000 | bytes 491520 | tf_op jit(solution)/shard_map/accumulate/pallas_call | solution.py:315
  18.5 0.4 %collective-permute-done.4.rest_0_ = bf16[4,2560]{1,0:T(4,128)(2,1)S(1)} collective-permute-done((bf16[4,2560]{1,0:T(4,128)(2,1)S(1)}, bf16[4,2560]{1,0:T(4,128)(2,1)S(1)}, u32[]{:S(2)}, u32[]{:S(2)}) %collective-permute-start.4) | collective-permute-done | bytes 20512 | tf_op jit(solution)/shard_map/ppermute | solution.py:259
  18.9 1.0 %accumulate.4.old_ref = f32[1,16,2560]{2,1,0:T(8,128)S(1)} custom-call(f32[1,4]{1,0:T(1,128)S(1)} %bitcast.2, s32[16,2560]{1,0:T(8,128)S(1)} %copy-done.1, f32[1,16,2560]{2,1,0:T(8,128)S(1)} %accumulate.3.old_ref, bf16[4,2560]{1,0:T(4,128)(2,1)S(1)} %collective-permute-done.4.rest_0_), custom_call_target="tpu_custom_call" | custom-call | flops 40960000 | bytes 491520 | tf_op jit(solution)/shard_map/accumulate/pallas_call | solution.py:315
  20.0 0.0 collective-permute-done.5.rest_0_
  20.0 1.7 %accumulate.5 = f32[1,16,2560]{2,1,0:T(8,128)} custom-call(f32[1,4]{1,0:T(1,128)S(1)} %bitcast.3, s32[16,2560]{1,0:T(8,128)S(1)} %copy-done.1, f32[1,16,2560]{2,1,0:T(8,128)S(1)} %accumulate.4.old_ref, bf16[4,2560]{1,0:T(4,128)(2,1)S(1)} %collective-permute-done.5.rest_0_), custom_call_target="tpu_custom_call" | custom-call | flops 40960000 | bytes 491520 | tf_op jit(solution)/shard_map/accumulate/pallas_call | solution.py:315
  (4 shorter events, 0.0 us)
Async XLA Ops:
  0.0 3.0 %copy-start = (bf16[1,1024,2048]{2,1,0:T(8,128)(2,1)S(1)}, bf16[1,1024,2048]{2,1,0:T(8,128)(2,1)}, u32[]{:S(2)}) copy-start(bf16[1,1024,2048]{2,1,0:T(8,128)(2,1)} %matrix_ref.1) | copy-start | bytes 12582916
  0.0 0.8 %copy-start.4 = (s32[1,2048]{1,0:T(1,128)S(1)}, s32[1,2048]{1,0:T(1,128)}, u32[]{:S(2)}) copy-start(s32[1,2048]{1,0:T(1,128)} %vertex_ref.1) | copy-start | bytes 24580
  3.0 14.1 %copy-start.1 = (s32[16,2560]{1,0:T(8,128)S(1)}, s32[16,2560]{1,0:T(8,128)}, u32[]{:S(2)}) copy-start(s32[16,2560]{1,0:T(8,128)} %transfer_ref.5) | copy-start | bytes 491524
  3.0 14.1 %copy-start.2 = (f32[1,16,2560]{2,1,0:T(8,128)S(1)}, f32[1,16,2560]{2,1,0:T(8,128)}, u32[]{:S(2)}) copy-start(f32[1,16,2560]{2,1,0:T(8,128)} %old_ref.1) | copy-start | bytes 491524
  3.0 14.0 %copy-start.3 = (f32[4]{0:T(128)S(1)}, f32[4]{0:T(128)}, u32[]{:S(2)}) copy-start(f32[4]{0:T(128)} %param.7) | copy-start | bytes 52
  5.2 3.1 %collective-permute-start = (f32[4,1280]{1,0:T(4,128)S(1)}, f32[4,1280]{1,0:T(4,128)S(1)}, u32[]{:S(2)}, u32[]{:S(2)}) collective-permute-start(f32[4,1280]{1,0:T(4,128)S(1)} %get-tuple-element.14), channel_id=1, source_target_pairs={{0,1},{1,0},{2,3},{3,2},{4,5},{5,4},{6,7},{7,6},{8,9},{9,8},{10,11... | collective-permute-start | bytes 61448 | tf_op jit(solution)/shard_map/ppermute | solution.py:259
  5.7 4.3 %collective-permute-start.1 = (f32[4,1280]{1,0:T(4,128)S(1)}, f32[4,1280]{1,0:T(4,128)S(1)}, u32[]{:S(2)}, u32[]{:S(2)}) collective-permute-start(f32[4,1280]{1,0:T(4,128)S(1)} %get-tuple-element.15), channel_id=1, source_target_pairs={{0,2},{1,3},{2,0},{3,1},{4,6},{5,7},{6,4},{7,5},{8,10},{9,11},{10,... | collective-permute-start | bytes 61448 | tf_op jit(solution)/shard_map/ppermute | solution.py:259
  8.2 3.2 %collective-permute-start.2 = (f32[4,1280]{1,0:T(4,128)S(1)}, f32[4,1280]{1,0:T(4,128)S(1)}, u32[]{:S(2)}, u32[]{:S(2)}) collective-permute-start(f32[4,1280]{1,0:T(4,128)S(1)} %get-tuple-element.16), channel_id=1, source_target_pairs={{0,3},{1,2},{2,1},{3,0},{4,7},{5,6},{6,5},{7,4},{8,11},{9,10},{10,... | collective-permute-start | bytes 61448 | tf_op jit(solution)/shard_map/ppermute | solution.py:259
  11.4 5.6 %collective-permute-start.3 = (bf16[4,2560]{1,0:T(4,128)(2,1)S(1)}, bf16[4,2560]{1,0:T(4,128)(2,1)S(1)}, u32[]{:S(2)}, u32[]{:S(2)}) collective-permute-start(bf16[4,2560]{1,0:T(4,128)(2,1)S(1)} %combine.1.rest_0_), channel_id=1, source_target_pairs={{0,12},{4,8},{8,4},{12,0},{1,13},{5,9},{9,5},{13,1},{2,14},{6,10},... | collective-permute-start | bytes 61448 | tf_op jit(solution)/shard_map/ppermute | solution.py:259
  15.1 3.9 %collective-permute-start.4 = (bf16[4,2560]{1,0:T(4,128)(2,1)S(1)}, bf16[4,2560]{1,0:T(4,128)(2,1)S(1)}, u32[]{:S(2)}, u32[]{:S(2)}) collective-permute-start(bf16[4,2560]{1,0:T(4,128)(2,1)S(1)} %combine.1.rest_0_), channel_id=1, source_target_pairs={{0,4},{4,0},{8,12},{12,8},{1,5},{5,1},{9,13},{13,9},{2,6},{6,2},{1... | collective-permute-start | bytes 61448 | tf_op jit(solution)/shard_map/ppermute | solution.py:259
  15.1 4.9 %collective-permute-start.5 = (bf16[4,2560]{1,0:T(4,128)(2,1)S(1)}, bf16[4,2560]{1,0:T(4,128)(2,1)S(1)}, u32[]{:S(2)}, u32[]{:S(2)}) collective-permute-start(bf16[4,2560]{1,0:T(4,128)(2,1)S(1)} %combine.1.rest_0_), channel_id=1, source_target_pairs={{0,8},{4,12},{8,0},{12,4},{1,9},{5,13},{9,1},{13,5},{2,10},{6,14},... | collective-permute-start | bytes 61448 | tf_op jit(solution)/shard_map/ppermute | solution.py:259
where the time goes:
time: 21.9 us; the launch traced here: 21.7 us
  Pallas kernels  8.46 us (39%)
  starting transfers between devices  7.57 us (35%)
  waiting for transfers between devices  4.67 us (21%)
  local copies, waits for them, and re-layouts  0.87 us (4%)
    ppermute x6, starting transfers between devices, exchange(): arrived[i] = lax.ppermute(pieces[i], axes, route)  7.57 us
    ppermute x6, waiting for transfers between devices, exchange(): arrived[i] = lax.ppermute(pieces[i], axes, route)  4.67 us
    pallas_call x3, Pallas kernels, local(): pl.pallas_call(functools.partial(accumulate_kernel, sizes, places), out_s...  4.16 us
    pallas_call x1, Pallas kernels, local(): pl.pallas_call(functools.partial(product_kernel, sizes), out_shape=[jax.S...  2.16 us
    pallas_call x1, Pallas kernels, local(): pl.pallas_call(functools.partial(table_kernel, sizes), out_shape=[jax.Sha...  2.14 us
    unnamed x10, local copies, waits for them, and re-layouts  0.87 us
  transfers between devices with their start and end apart: 6, of which 4 were waited for; matrix products, arithmetic and copies ran while one was open for 0% of the time, Pallas kernels for 11%

commit v1 on v0

--- a/solution.py
+++ b/solution.py
@@ -63,11 +63,49 @@
     return ids // size, ids % size
 
 
+def tile_of(start):
+    return pl.ds(start if isinstance(start, int) else pl.multiple_of(start, lanes), lanes)
+
+
+def make_table(vertex_ref, table_ref, first, place, sub_index):
+    columns = table_ref.shape[0]
+    blocks = columns // lanes
+    half_blocks = blocks // 2
+    coarse_rows = -(-max(half_blocks, 1) // sublanes) * sublanes
+    middle_count = lanes // sublanes
+    center = sub_index * columns + (blocks - 1) * (lanes // 2)
+    here = tile_of(place)
+    vertex = vertex_ref[:, tile_of(first)]
+    cosine, sine = cos_sin(vertex * (row_ids(sublanes) + center))
+    cas_fine, cam_fine = cosine + sine, cosine - sine
+    cos_middle, sin_middle = cos_sin(vertex * (row_ids(middle_count) * sublanes))
+    cos_coarse, sin_coarse = cos_sin(
+        vertex * ((blocks - 1 - 2 * row_ids(coarse_rows)) * (lanes // 2))
+    )
+    for pair in range(middle_count // 2):
+        cas, cam = [], []
+        for middle in (2 * pair, 2 * pair + 1):
+            c, s = cos_middle[middle : middle + 1], sin_middle[middle : middle + 1]
+            cas.append(c * cas_fine + s * cam_fine)
+            cam.append(c * cam_fine - s * cas_fine)
+        cas, cam = jnp.concatenate(cas, axis=0), jnp.concatenate(cam, axis=0)
+        start = pair * 2 * sublanes
+        for low in range(half_blocks):
+            high = blocks - 1 - low
+            even = cos_coarse[low : low + 1] * cas
+            odd = sin_coarse[low : low + 1] * cam
+            for block, value in ((low, even - odd), (high, even + odd)):
+                row = block * lanes + start
+                table_ref[row : row + 2 * sublanes, here] = value.astype(jnp.bfloat16)
+        if blocks % 2:
+            row = half_blocks * lanes + start
+            table_ref[row : row + 2 * sublanes, here] = cas.astype(jnp.bfloat16)
+
+
 def table_kernel(sizes, vertex_ref, table_ref, left_ref):
     blk_count, walk_count, sub_count, rows_own = sizes
     walk_index = lax.axis_index("walk")
     sub_index = lax.axis_index("sub")
-    columns, vertices = table_ref.shape
     window_rows, rows_local = left_ref.shape
 
     ids, inner = split_by(row_ids(window_rows), rows_own)
@@ -82,68 +120,41 @@
         cosine, sine = cos_sin(own_vertex * window)
         left_ref[:, start : start + lanes] = (cosine + sine).astype(jnp.bfloat16)
 
-    blocks = columns // lanes
-    half_blocks = blocks // 2
-    coarse_rows = -(-max(half_blocks, 1) // sublanes) * sublanes
-    middle_count = lanes // sublanes
-    center = sub_index * columns + (blocks - 1) * (lanes // 2)
-
-    def angles(step):
-        vertex = vertex_ref[:, pl.ds(pl.multiple_of(step * lanes, lanes), lanes)]
-        cosine, sine = cos_sin(vertex * (row_ids(sublanes) + center))
-        return (
-            cosine + sine,
-            cosine - sine,
-            *cos_sin(vertex * (row_ids(middle_count) * sublanes)),
-            *cos_sin(vertex * ((blocks - 1 - 2 * row_ids(coarse_rows)) * (lanes // 2))),
-        )
-
-    def table_step(step, carried):
-        following = angles(jnp.minimum(step + 1, steps - 1))
-        cas_fine, cam_fine, cos_middle, sin_middle, cos_coarse, sin_coarse = carried
-        here = pl.ds(pl.multiple_of(step * lanes, lanes), lanes)
-        for pair in range(middle_count // 2):
-            cas, cam = [], []
-            for middle in (2 * pair, 2 * pair + 1):
-                c, s = cos_middle[middle : middle + 1], sin_middle[middle : middle + 1]
-                cas.append(c * cas_fine + s * cam_fine)
-                cam.append(c * cam_fine - s * cas_fine)
-            cas, cam = jnp.concatenate(cas, axis=0), jnp.concatenate(cam, axis=0)
-            start = pair * 2 * sublanes
-            for low in range(half_blocks):
-                high = blocks - 1 - low
-                even = cos_coarse[low : low + 1] * cas
-                odd = sin_coarse[low : low + 1] * cam
-                for block, value in ((low, even - odd), (high, even + odd)):
-                    first = block * lanes + start
-                    table_ref[first : first + 2 * sublanes, here] = value.astype(jnp.bfloat16)
-            if blocks % 2:
-                first = half_blocks * lanes + start
-                table_ref[first : first + 2 * sublanes, here] = cas.astype(jnp.bfloat16)
-        return following
-
-    steps = vertices // lanes
-    lax.fori_loop(0, steps, table_step, angles(0))
-
-
-def product_kernel(sizes, matrix_ref, table_ref, left_ref, *rest):
-    *sent_refs, weight_ref = rest
+    @pl.loop(0, table_ref.shape[1] // lanes)
+    def _(step):
+        make_table(vertex_ref, table_ref, step * lanes, step * lanes, sub_index)
+
+
+def product_kernel(sizes, matrix_ref, vertex_ref, early_ref, left_ref, *rest):
+    *sent_refs, late_ref, weight_ref = rest
     blk_count, _, _, rows_own = sizes
+    sub_index = lax.axis_index("sub")
     vertices = matrix_ref.shape[2]
     window_rows = left_ref.shape[0]
+    early = early_ref.shape[1]
 
     chunk = 4 * lanes
-    for start in range(0, vertices, chunk):
+    tiles = list(range(0, vertices - early, lanes))
+    chunks = list(range(0, vertices, chunk))
+    for i, start in enumerate(chunks):
         left_product = jnp.dot(
             left_ref[...], matrix_ref[0, :, start : start + chunk], preferred_element_type=jnp.float32
         )
+        for tile in tiles[i * len(tiles) // len(chunks) : (i + 1) * len(tiles) // len(chunks)]:
+            make_table(vertex_ref, late_ref, early + tile, tile, sub_index)
         high = left_product.astype(jnp.bfloat16)
         weight_ref[:window_rows, start : start + chunk] = high
         weight_ref[window_rows:, start : start + chunk] = (
             left_product - high.astype(jnp.float32)
         ).astype(jnp.bfloat16)
-    green = lax.dot_general(
-        weight_ref[...], table_ref[...], (((1,), (1,)), ((), ())), preferred_element_type=jnp.float32
+    green = sum(
+        lax.dot_general(
+            weight_ref[:, start : start + table_ref.shape[1]],
+            table_ref[...],
+            (((1,), (1,)), ((), ())),
+            preferred_element_type=jnp.float32,
+        )
+        for start, table_ref in ((0, early_ref), (early, late_ref))
     )
     green = green[:window_rows] + green[window_rows:]
     rows_each = blk_count * rows_own
@@ -208,7 +219,7 @@
 
         together = len(distances) if len(distances) <= 4 else math.gcd(len(distances), 4)
 
-        @pl.loop(0, tiles, unroll=math.gcd(tiles, 10))
+        @pl.loop(0, tiles, unroll=math.gcd(tiles, 20))
         def _(tile):
             here = pl.ds(pl.multiple_of(tile * lanes, lanes), lanes)
             for group in range(groups):
@@ -270,10 +281,11 @@
     devices = blk_count * walk_count * sub_count
     sizes = (blk_count, walk_count, sub_count, rows_own)
     vmem = pl.BlockSpec(memory_space=pltpu.VMEM)
+    early = 5 * vertices // (8 * 2 * lanes) * 2 * lanes
     table, left = pl.pallas_call(
         functools.partial(table_kernel, sizes),
         out_shape=[
-            jax.ShapeDtypeStruct((columns_local, vertices), jnp.bfloat16),
+            jax.ShapeDtypeStruct((columns_local, early), jnp.bfloat16),
             jax.ShapeDtypeStruct((devices * rows_own, rows_local), jnp.bfloat16),
         ],
         in_specs=[vmem],
@@ -290,12 +302,15 @@
         functools.partial(product_kernel, sizes),
         out_shape=[jax.ShapeDtypeStruct((blk_count * rows_own, columns_local), jnp.float32)]
         * (walk_count * sub_count),
-        in_specs=[vmem] * 3,
+        in_specs=[vmem] * 4,
         out_specs=[vmem] * (walk_count * sub_count),
-        scratch_shapes=[pltpu.VMEM((2 * devices * rows_own, vertices), jnp.bfloat16)],
+        scratch_shapes=[
+            pltpu.VMEM((columns_local, vertices - early), jnp.bfloat16),
+            pltpu.VMEM((2 * devices * rows_own, vertices), jnp.bfloat16),
+        ],
         compiler_params=pltpu.CompilerParams(vmem_limit_bytes=24 * 2**20),
         name="product",
-    )(walker_mats, table, left)
+    )(walker_mats, vertex, table, left)
     parts = exchange(sent, ("walk", "sub"), (walk_count, sub_count))
     shared = blk_count <= RSTEPS
     rows_each = (blk_count if shared else RSTEPS) * rows_own

time: 21.9 us -> 21 us (0.959)
  Pallas kernels: 8.46 us -> 7.46 us
    pallas_call x1, Pallas kernels: 2.14 us -> 1.29 us  [local(): pl.pallas_call(functools.partial(table_kernel, sizes), out_shape=[jax.Sha...]
    pallas_call x3, Pallas kernels: 4.16 us -> 3.79 us  [local(): pl.pallas_call(functools.partial(accumulate_kernel, sizes, places), out_s...]
where the time goes in v1:
time: 21 us; the launch traced here: 20.8 us
  starting transfers between devices  7.59 us (36%)
  Pallas kernels  7.46 us (36%)
  waiting for transfers between devices  4.8 us (23%)
  local copies, waits for them, and re-layouts  0.89 us (4%)
    ppermute x6, starting transfers between devices, exchange(): arrived[i] = lax.ppermute(pieces[i], axes, route)  7.59 us
    ppermute x6, waiting for transfers between devices, exchange(): arrived[i] = lax.ppermute(pieces[i], axes, route)  4.8 us
    pallas_call x3, Pallas kernels, local(): pl.pallas_call(functools.partial(accumulate_kernel, sizes, places), out_s...  3.79 us
    pallas_call x1, Pallas kernels, local(): pl.pallas_call(functools.partial(product_kernel, sizes), out_shape=[jax.S...  2.37 us
    pallas_call x1, Pallas kernels, local(): pl.pallas_call(functools.partial(table_kernel, sizes), out_shape=[jax.Sha...  1.29 us
    unnamed x10, local copies, waits for them, and re-layouts  0.89 us
  transfers between devices with their start and end apart: 6, of which 4 were waited for; matrix products, arithmetic and copies ran while one was open for 0% of the time, Pallas kernels for 11%

profile of v1, /device:TPU:0, one launch (start us, length us, event | category | flops | bytes accessed | tf_op | source)
XLA Modules:
  0.0 20.8 jit_solution(9115382673067065416)
XLA Ops:
  0.0 0.8 %copy-done.3 = s32[1,2048]{1,0:T(1,128)S(1)} copy-done((s32[1,2048]{1,0:T(1,128)S(1)}, s32[1,2048]{1,0:T(1,128)}, u32[]{:S(2)}) %copy-start.3) | copy-done | bytes 8216
  0.8 1.3 %table.1 = (bf16[1280,1280]{1,0:T(8,128)(2,1)S(1)}, bf16[16,1024]{1,0:T(8,128)(2,1)S(1)}) custom-call(s32[1,2048]{1,0:T(1,128)S(1)} %copy-done.3), custom_call_target="tpu_custom_call" | custom-call | flops 5242880000 | bytes 15728640 | tf_op jit(solution)/shard_map/table/pallas_call | solution.py:285
  2.1 0.0 copy-start.1
  2.2 0.0 copy-start.2
  2.2 0.0 copy-start.4
  2.2 0.0 copy-done
  2.2 2.4 %product.1 = (f32[4,1280]{1,0:T(4,128)S(1)}, f32[4,1280]{1,0:T(4,128)S(1)}, f32[4,1280]{1,0:T(4,128)S(1)}, f32[4,1280]{1,0:T(4,128)S(1)}) custom-call(bf16[1,1024,2048]{2,1,0:T(8,128)(2,1)S(1)} %copy-done, s32[1,2048]{1,0:T(1,128)S(1)} %copy-done.3, bf16[1280,1280]{1,0:T(8,128)(2,1)S(1)} %get-tuple-element.11.early_ref, ...), custom_call_target="tpu_custom_call" | custom-call | tf_op jit(solution)/shard_map/product/pallas_call | solution.py:301
  4.6 0.5 %collective-permute-start = (f32[4,1280]{1,0:T(4,128)S(1)}, f32[4,1280]{1,0:T(4,128)S(1)}, u32[]{:S(2)}, u32[]{:S(2)}) collective-permute-start(f32[4,1280]{1,0:T(4,128)S(1)} %get-tuple-element.14), channel_id=1, source_target_pairs={{0,1},{1,0},{2,3},{3,2},{4,5},{5,4},{6,7},{7,6},{8,9},{9,8},{10,11... | collective-permute-start | bytes 61448 | tf_op jit(solution)/shard_map/ppermute | solution.py:270
  5.1 2.5 %collective-permute-start.1 = (f32[4,1280]{1,0:T(4,128)S(1)}, f32[4,1280]{1,0:T(4,128)S(1)}, u32[]{:S(2)}, u32[]{:S(2)}) collective-permute-start(f32[4,1280]{1,0:T(4,128)S(1)} %get-tuple-element.15), channel_id=1, source_target_pairs={{0,2},{1,3},{2,0},{3,1},{4,6},{5,7},{6,4},{7,5},{8,10},{9,11},{10,... | collective-permute-start | bytes 61448 | tf_op jit(solution)/shard_map/ppermute | solution.py:270
  7.6 0.1 collective-permute-start.2
  7.7 0.0 collective-permute-done.refs_1_
  7.7 1.6 %collective-permute-done.1.refs_2_ = f32[4,1280]{1,0:T(4,128)S(1)} collective-permute-done((f32[4,1280]{1,0:T(4,128)S(1)}, f32[4,1280]{1,0:T(4,128)S(1)}, u32[]{:S(2)}, u32[]{:S(2)}) %collective-permute-start.1) | collective-permute-done | bytes 20512 | tf_op jit(solution)/shard_map/ppermute | solution.py:270
  9.4 1.4 %collective-permute-done.2.refs_3_ = f32[4,1280]{1,0:T(4,128)S(1)} collective-permute-done((f32[4,1280]{1,0:T(4,128)S(1)}, f32[4,1280]{1,0:T(4,128)S(1)}, u32[]{:S(2)}, u32[]{:S(2)}) %collective-permute-start.2) | collective-permute-done | bytes 20512 | tf_op jit(solution)/shard_map/ppermute | solution.py:270
  10.8 3.7 %collective-permute-start.3 = (bf16[4,2560]{1,0:T(4,128)(2,1)S(1)}, bf16[4,2560]{1,0:T(4,128)(2,1)S(1)}, u32[]{:S(2)}, u32[]{:S(2)}) collective-permute-start(bf16[4,2560]{1,0:T(4,128)(2,1)S(1)} %combine.1.rest_0_), channel_id=1, source_target_pairs={{0,12},{4,8},{8,4},{12,0},{1,13},{5,9},{9,5},{13,1},{2,14},{6,10},... | collective-permute-start | bytes 61448 | tf_op jit(solution)/shard_map/ppermute | solution.py:270
  14.5 0.0 collective-permute-start.4
  14.5 0.8 %collective-permute-start.5 = (bf16[4,2560]{1,0:T(4,128)(2,1)S(1)}, bf16[4,2560]{1,0:T(4,128)(2,1)S(1)}, u32[]{:S(2)}, u32[]{:S(2)}) collective-permute-start(bf16[4,2560]{1,0:T(4,128)(2,1)S(1)} %combine.1.rest_0_), channel_id=1, source_target_pairs={{0,8},{4,12},{8,0},{12,4},{1,9},{5,13},{9,1},{13,5},{2,10},{6,14},... | collective-permute-start | bytes 61448 | tf_op jit(solution)/shard_map/ppermute | solution.py:270
  15.3 1.2 %collective-permute-done.3.rest_1_ = bf16[4,2560]{1,0:T(4,128)(2,1)S(1)} collective-permute-done((bf16[4,2560]{1,0:T(4,128)(2,1)S(1)}, bf16[4,2560]{1,0:T(4,128)(2,1)S(1)}, u32[]{:S(2)}, u32[]{:S(2)}) %collective-permute-start.3) | collective-permute-done | bytes 20512 | tf_op jit(solution)/shard_map/ppermute | solution.py:270
  16.4 0.0 copy-done.1
  16.4 0.0 copy-done.2
  16.5 1.3 %accumulate.3.old_ref = f32[1,16,2560]{2,1,0:T(8,128)S(1)} custom-call(f32[1,4]{1,0:T(1,128)S(1)} %bitcast.1, s32[16,2560]{1,0:T(8,128)S(1)} %copy-done.1, f32[1,16,2560]{2,1,0:T(8,128)S(1)} %copy-done.2, bf16[4,2560]{1,0:T(4,128)(2,1)S(1)} %combine.1.rest_0_, bf16[4,2560]{1,0:T(4,128)(2,1)S(1)} %collective-permute-done.3.rest_1_), custom_call_target="tpu_custom_call" | custom-call | flops 81920000 | bytes 491520 | tf_op jit(solution)/shard_map/accumulate/pallas_call | solution.py:330
  17.8 0.5 %collective-permute-done.4.rest_0_ = bf16[4,2560]{1,0:T(4,128)(2,1)S(1)} collective-permute-done((bf16[4,2560]{1,0:T(4,128)(2,1)S(1)}, bf16[4,2560]{1,0:T(4,128)(2,1)S(1)}, u32[]{:S(2)}, u32[]{:S(2)}) %collective-permute-start.4) | collective-permute-done | bytes 20512 | tf_op jit(solution)/shard_map/ppermute | solution.py:270
  18.3 0.9 %accumulate.4.old_ref = f32[1,16,2560]{2,1,0:T(8,128)S(1)} custom-call(f32[1,4]{1,0:T(1,128)S(1)} %bitcast.2, s32[16,2560]{1,0:T(8,128)S(1)} %copy-done.1, f32[1,16,2560]{2,1,0:T(8,128)S(1)} %accumulate.3.old_ref, bf16[4,2560]{1,0:T(4,128)(2,1)S(1)} %collective-permute-done.4.rest_0_), custom_call_target="tpu_custom_call" | custom-call | flops 40960000 | bytes 491520 | tf_op jit(solution)/shard_map/accumulate/pallas_call | solution.py:330
  19.2 0.0 collective-permute-done.5.rest_0_
  19.2 1.6 %accumulate.5 = f32[1,16,2560]{2,1,0:T(8,128)} custom-call(f32[1,4]{1,0:T(1,128)S(1)} %bitcast.3, s32[16,2560]{1,0:T(8,128)S(1)} %copy-done.1, f32[1,16,2560]{2,1,0:T(8,128)S(1)} %accumulate.4.old_ref, bf16[4,2560]{1,0:T(4,128)(2,1)S(1)} %collective-permute-done.5.rest_0_), custom_call_target="tpu_custom_call" | custom-call | flops 40960000 | bytes 491520 | tf_op jit(solution)/shard_map/accumulate/pallas_call | solution.py:330
  (4 shorter events, 0.0 us)
Async XLA Ops:
  0.0 2.2 %copy-start = (bf16[1,1024,2048]{2,1,0:T(8,128)(2,1)S(1)}, bf16[1,1024,2048]{2,1,0:T(8,128)(2,1)}, u32[]{:S(2)}) copy-start(bf16[1,1024,2048]{2,1,0:T(8,128)(2,1)} %matrix_ref.1) | copy-start | bytes 12582916
  0.0 0.8 %copy-start.3 = (s32[1,2048]{1,0:T(1,128)S(1)}, s32[1,2048]{1,0:T(1,128)}, u32[]{:S(2)}) copy-start(s32[1,2048]{1,0:T(1,128)} %vertex_ref.3) | copy-start | bytes 24580
  2.1 14.3 %copy-start.1 = (s32[16,2560]{1,0:T(8,128)S(1)}, s32[16,2560]{1,0:T(8,128)}, u32[]{:S(2)}) copy-start(s32[16,2560]{1,0:T(8,128)} %transfer_ref.5) | copy-start | bytes 491524
  2.2 14.3 %copy-start.2 = (f32[1,16,2560]{2,1,0:T(8,128)S(1)}, f32[1,16,2560]{2,1,0:T(8,128)}, u32[]{:S(2)}) copy-start(f32[1,16,2560]{2,1,0:T(8,128)} %old_ref.1) | copy-start | bytes 491524
  2.2 14.3 %copy-start.4 = (f32[4]{0:T(128)S(1)}, f32[4]{0:T(128)}, u32[]{:S(2)}) copy-start(f32[4]{0:T(128)} %param.7) | copy-start | bytes 52
  4.6 3.1 %collective-permute-start = (f32[4,1280]{1,0:T(4,128)S(1)}, f32[4,1280]{1,0:T(4,128)S(1)}, u32[]{:S(2)}, u32[]{:S(2)}) collective-permute-start(f32[4,1280]{1,0:T(4,128)S(1)} %get-tuple-element.14), channel_id=1, source_target_pairs={{0,1},{1,0},{2,3},{3,2},{4,5},{5,4},{6,7},{7,6},{8,9},{9,8},{10,11... | collective-permute-start | bytes 61448 | tf_op jit(solution)/shard_map/ppermute | solution.py:270
  5.1 4.3 %collective-permute-start.1 = (f32[4,1280]{1,0:T(4,128)S(1)}, f32[4,1280]{1,0:T(4,128)S(1)}, u32[]{:S(2)}, u32[]{:S(2)}) collective-permute-start(f32[4,1280]{1,0:T(4,128)S(1)} %get-tuple-element.15), channel_id=1, source_target_pairs={{0,2},{1,3},{2,0},{3,1},{4,6},{5,7},{6,4},{7,5},{8,10},{9,11},{10,... | collective-permute-start | bytes 61448 | tf_op jit(solution)/shard_map/ppermute | solution.py:270
  7.6 3.2 %collective-permute-start.2 = (f32[4,1280]{1,0:T(4,128)S(1)}, f32[4,1280]{1,0:T(4,128)S(1)}, u32[]{:S(2)}, u32[]{:S(2)}) collective-permute-start(f32[4,1280]{1,0:T(4,128)S(1)} %get-tuple-element.16), channel_id=1, source_target_pairs={{0,3},{1,2},{2,1},{3,0},{4,7},{5,6},{6,5},{7,4},{8,11},{9,10},{10,... | collective-permute-start | bytes 61448 | tf_op jit(solution)/shard_map/ppermute | solution.py:270
  10.8 5.6 %collective-permute-start.3 = (bf16[4,2560]{1,0:T(4,128)(2,1)S(1)}, bf16[4,2560]{1,0:T(4,128)(2,1)S(1)}, u32[]{:S(2)}, u32[]{:S(2)}) collective-permute-start(bf16[4,2560]{1,0:T(4,128)(2,1)S(1)} %combine.1.rest_0_), channel_id=1, source_target_pairs={{0,12},{4,8},{8,4},{12,0},{1,13},{5,9},{9,5},{13,1},{2,14},{6,10},... | collective-permute-start | bytes 61448 | tf_op jit(solution)/shard_map/ppermute | solution.py:270
  14.5 3.9 %collective-permute-start.4 = (bf16[4,2560]{1,0:T(4,128)(2,1)S(1)}, bf16[4,2560]{1,0:T(4,128)(2,1)S(1)}, u32[]{:S(2)}, u32[]{:S(2)}) collective-permute-start(bf16[4,2560]{1,0:T(4,128)(2,1)S(1)} %combine.1.rest_0_), channel_id=1, source_target_pairs={{0,4},{4,0},{8,12},{12,8},{1,5},{5,1},{9,13},{13,9},{2,6},{6,2},{1... | collective-permute-start | bytes 61448 | tf_op jit(solution)/shard_map/ppermute | solution.py:270
  14.5 4.8 %collective-permute-start.5 = (bf16[4,2560]{1,0:T(4,128)(2,1)S(1)}, bf16[4,2560]{1,0:T(4,128)(2,1)S(1)}, u32[]{:S(2)}, u32[]{:S(2)}) collective-permute-start(bf16[4,2560]{1,0:T(4,128)(2,1)S(1)} %combine.1.rest_0_), channel_id=1, source_target_pairs={{0,8},{4,12},{8,0},{12,4},{1,9},{5,13},{9,1},{13,5},{2,10},{6,14},... | collective-permute-start | bytes 61448 | tf_op jit(solution)/shard_map/ppermute | solution.py:270

commit v2 on v1

--- a/solution.py
+++ b/solution.py
@@ -190,8 +190,11 @@
             whole_ref[:, here] = pick_rows(total, blk_part * rows_own + inner).astype(whole_ref.dtype)
 
 
-def accumulate_kernel(sizes, distances, weights_ref, transfer_ref, old_ref, *rest):
-    *arrived_refs, new_ref, source_ref, left_ref, unit_ref = rest
+def accumulate_kernel(sizes, distances, last, weights_ref, transfer_ref, old_ref, *rest):
+    if last:
+        *arrived_refs, out_ref, source_ref, left_ref, unit_ref, new_ref, out_sems = rest
+    else:
+        *arrived_refs, new_ref, source_ref, left_ref, unit_ref = rest
     blk_count, _, _, rows_own = sizes
     blk_index = lax.axis_index("blk")
     transfers, columns = transfer_ref.shape
@@ -206,22 +209,40 @@
     if arrived_refs[0].shape[0] == blk_count * rows_own:
         _, step = split_by(blk_index + RSTEPS * blk_count - step, blk_count)
 
+    def out_copy(own, part):
+        here = slice(part * half, (part + 1) * half)
+        return pltpu.make_async_copy(
+            new_ref.at[own, :, here], out_ref.at[own, :, here], out_sems.at[own, part]
+        )
+
+    def spread(rows, own):
+        wide = (transfers, rows.shape[1])
+        picked = jnp.broadcast_to(rows[own : own + 1], wide)
+        for place in range(1, rows.shape[0] // rows_own):
+            row = place * rows_own + own
+            picked = jnp.where(step == place, jnp.broadcast_to(rows[row : row + 1], wide), picked)
+        return picked
+
     for own in range(rows_own):
         for place, distance in enumerate(distances):
-            rows = pick_rows(arrived_refs[place][...], step * rows_own + own)
+            rows = arrived_refs[place][...].astype(jnp.float32)
             walker = back(blk_index, distance, blk_count)
             weight = jnp.sum(jnp.where(walker_ids == walker, weights, 0.0), axis=1, keepdims=True)
-            left_ref[place] = rows[:1] * weight
+            left = rows[own : own + 1]
+            for blk_part in range(1, rows.shape[0] // rows_own):
+                row = blk_part * rows_own + own
+                left = jnp.where(step[:1] == blk_part, rows[row : row + 1], left)
+            left_ref[place] = left * weight
             peak = jnp.maximum(jnp.max(jnp.abs(rows), axis=1, keepdims=True), smallest_peak)
             codes = jnp.floor(rows * (code_limit / peak) + 0.5).astype(jnp.int32)
-            unit_ref[place] = jnp.broadcast_to(peak * (1.0 / code_limit), (transfers, lanes))
-            source_ref[place] = (codes[:, :half] << 16) | (codes[:, half:] & 0xFFFF)
+            peak = jnp.broadcast_to(peak * (1.0 / code_limit), (rows.shape[0], lanes))
+            unit_ref[place] = spread(peak, own)
+            source_ref[place] = spread((codes[:, :half] << 16) | (codes[:, half:] & 0xFFFF), own)
 
         together = len(distances) if len(distances) <= 4 else math.gcd(len(distances), 4)
 
-        @pl.loop(0, tiles, unroll=math.gcd(tiles, 20))
-        def _(tile):
-            here = pl.ds(pl.multiple_of(tile * lanes, lanes), lanes)
+        for tile in range(tiles):
+            here = slice(tile * lanes, (tile + 1) * lanes)
             for group in range(groups):
                 rows = slice(group * sublanes, (group + 1) * sublanes)
                 index = transfer_ref[rows, here]
@@ -256,6 +277,13 @@
                         0, len(distances) // together, lambda i, t: add_walkers(i * together, t), total
                     )
                 new_ref[own, rows, here] = total
+
+            if last and (tile + 1) % (tiles // 2) == 0:
+                out_copy(own, (tile + 1) // (tiles // 2) - 1).start()
+    if last:
+        for own in range(rows_own):
+            for part in range(2):
+                out_copy(own, part).wait()
 
 
 def exchange(pieces, axes, counts):
@@ -326,17 +354,23 @@
     arrived = exchange(whole * blk_count if shared else whole, ("blk",), (blk_count,))
     far = blk_count // 2
     totals = g4_old
-    for places in ([0, *range(far + 1, blk_count)], [*range(1, far)], [far]):
+    groups = [0, *range(far + 1, blk_count)], [*range(1, far)], [far]
+    for places in groups:
+        last = places is groups[-1]
+        scratch_shapes = [
+            pltpu.VMEM((len(places), transfers, columns // 2), jnp.int32),
+            pltpu.VMEM((len(places), 1, columns), jnp.float32),
+            pltpu.VMEM((len(places), transfers, lanes), jnp.float32),
+        ]
+        if last:
+            scratch_shapes.append(pltpu.VMEM(g4_old.shape, jnp.float32))
+            scratch_shapes.append(pltpu.SemaphoreType.DMA((rows_own, 2)))
         totals = pl.pallas_call(
-            functools.partial(accumulate_kernel, sizes, places),
+            functools.partial(accumulate_kernel, sizes, places, last),
             out_shape=jax.ShapeDtypeStruct(g4_old.shape, jnp.float32),
             in_specs=[vmem] * (3 + len(places)),
-            out_specs=vmem,
-            scratch_shapes=[
-                pltpu.VMEM((len(places), transfers, columns // 2), jnp.int32),
-                pltpu.VMEM((len(places), 1, columns), jnp.float32),
-                pltpu.VMEM((len(places), transfers, lanes), jnp.float32),
-            ],
+            out_specs=pl.BlockSpec(memory_space=pl.ANY) if last else vmem,
+            scratch_shapes=scratch_shapes,
             compiler_params=pltpu.CompilerParams(vmem_limit_bytes=24 * 2**20),
             cost_estimate=pl.CostEstimate(
                 flops=1000 * len(places) * transfers * columns,

time: 21 us -> 20.8 us (level)
  Pallas kernels: 7.46 us -> 7.06 us
    pallas_call x3, Pallas kernels: 3.79 us -> 3.39 us  [local(): pl.pallas_call(functools.partial(accumulate_kernel, sizes, places, last),...]
  transfers between devices with their start and end apart: 6 -> 6, of which waited for: 4 -> 5; matrix products, arithmetic and copies ran while one was open for 0% -> 0% of each run, Pallas kernels for 11% -> 10%
where the time goes in v2:
time: 20.8 us; the launch traced here: 20.6 us
  starting transfers between devices  7.59 us (36%)
  Pallas kernels  7.06 us (34%)
  waiting for transfers between devices  5 us (24%)
  local copies, waits for them, and re-layouts  0.89 us (4%)
    ppermute x6, starting transfers between devices, exchange(): arrived[i] = lax.ppermute(pieces[i], axes, route)  7.59 us
    ppermute x6, waiting for transfers between devices, exchange(): arrived[i] = lax.ppermute(pieces[i], axes, route)  5 us
    pallas_call x3, Pallas kernels, local(): pl.pallas_call(functools.partial(accumulate_kernel, sizes, places, last),...  3.39 us
    pallas_call x1, Pallas kernels, local(): pl.pallas_call(functools.partial(product_kernel, sizes), out_shape=[jax.S...  2.37 us
    pallas_call x1, Pallas kernels, local(): pl.pallas_call(functools.partial(table_kernel, sizes), out_shape=[jax.Sha...  1.29 us
    unnamed x10, local copies, waits for them, and re-layouts  0.89 us
  transfers between devices with their start and end apart: 6, of which 5 were waited for; matrix products, arithmetic and copies ran while one was open for 0% of the time, Pallas kernels for 10%

profile of v2, /device:TPU:0, one launch (start us, length us, event | category | flops | bytes accessed | tf_op | source)
XLA Modules:
  0.0 20.6 jit_solution(15382728541211835610)
XLA Ops:
  0.0 0.8 %copy-done.3 = s32[1,2048]{1,0:T(1,128)S(1)} copy-done((s32[1,2048]{1,0:T(1,128)S(1)}, s32[1,2048]{1,0:T(1,128)}, u32[]{:S(2)}) %copy-start.3) | copy-done | bytes 8216
  0.8 1.3 %table.1 = (bf16[1280,1280]{1,0:T(8,128)(2,1)S(1)}, bf16[16,1024]{1,0:T(8,128)(2,1)S(1)}) custom-call(s32[1,2048]{1,0:T(1,128)S(1)} %copy-done.3), custom_call_target="tpu_custom_call" | custom-call | flops 5242880000 | bytes 15728640 | tf_op jit(solution)/shard_map/table/pallas_call | solution.py:313
  2.1 0.0 copy-start.1
  2.2 0.0 copy-start.2
  2.2 0.0 copy-start.4
  2.2 0.0 copy-done
  2.2 2.4 %product.1 = (f32[4,1280]{1,0:T(4,128)S(1)}, f32[4,1280]{1,0:T(4,128)S(1)}, f32[4,1280]{1,0:T(4,128)S(1)}, f32[4,1280]{1,0:T(4,128)S(1)}) custom-call(bf16[1,1024,2048]{2,1,0:T(8,128)(2,1)S(1)} %copy-done, s32[1,2048]{1,0:T(1,128)S(1)} %copy-done.3, bf16[1280,1280]{1,0:T(8,128)(2,1)S(1)} %get-tuple-element.11.early_ref, ...), custom_call_target="tpu_custom_call" | custom-call | tf_op jit(solution)/shard_map/product/pallas_call | solution.py:329
  4.6 0.5 %collective-permute-start = (f32[4,1280]{1,0:T(4,128)S(1)}, f32[4,1280]{1,0:T(4,128)S(1)}, u32[]{:S(2)}, u32[]{:S(2)}) collective-permute-start(f32[4,1280]{1,0:T(4,128)S(1)} %get-tuple-element.14), channel_id=1, source_target_pairs={{0,1},{1,0},{2,3},{3,2},{4,5},{5,4},{6,7},{7,6},{8,9},{9,8},{10,11... | collective-permute-start | bytes 61448 | tf_op jit(solution)/shard_map/ppermute | solution.py:298
  5.1 2.5 %collective-permute-start.1 = (f32[4,1280]{1,0:T(4,128)S(1)}, f32[4,1280]{1,0:T(4,128)S(1)}, u32[]{:S(2)}, u32[]{:S(2)}) collective-permute-start(f32[4,1280]{1,0:T(4,128)S(1)} %get-tuple-element.15), channel_id=1, source_target_pairs={{0,2},{1,3},{2,0},{3,1},{4,6},{5,7},{6,4},{7,5},{8,10},{9,11},{10,... | collective-permute-start | bytes 61448 | tf_op jit(solution)/shard_map/ppermute | solution.py:298
  7.6 0.1 collective-permute-start.2
  7.7 0.0 collective-permute-done.refs_1_
  7.7 1.6 %collective-permute-done.1.refs_2_ = f32[4,1280]{1,0:T(4,128)S(1)} collective-permute-done((f32[4,1280]{1,0:T(4,128)S(1)}, f32[4,1280]{1,0:T(4,128)S(1)}, u32[]{:S(2)}, u32[]{:S(2)}) %collective-permute-start.1) | collective-permute-done | bytes 20512 | tf_op jit(solution)/shard_map/ppermute | solution.py:298
  9.4 1.4 %collective-permute-done.2.refs_3_ = f32[4,1280]{1,0:T(4,128)S(1)} collective-permute-done((f32[4,1280]{1,0:T(4,128)S(1)}, f32[4,1280]{1,0:T(4,128)S(1)}, u32[]{:S(2)}, u32[]{:S(2)}) %collective-permute-start.2) | collective-permute-done | bytes 20512 | tf_op jit(solution)/shard_map/ppermute | solution.py:298
  10.8 3.7 %collective-permute-start.3 = (bf16[4,2560]{1,0:T(4,128)(2,1)S(1)}, bf16[4,2560]{1,0:T(4,128)(2,1)S(1)}, u32[]{:S(2)}, u32[]{:S(2)}) collective-permute-start(bf16[4,2560]{1,0:T(4,128)(2,1)S(1)} %combine.1.rest_0_), channel_id=1, source_target_pairs={{0,12},{4,8},{8,4},{12,0},{1,13},{5,9},{9,5},{13,1},{2,14},{6,10},... | collective-permute-start | bytes 61448 | tf_op jit(solution)/shard_map/ppermute | solution.py:298
  14.5 0.0 collective-permute-start.4
  14.5 0.8 %collective-permute-start.5 = (bf16[4,2560]{1,0:T(4,128)(2,1)S(1)}, bf16[4,2560]{1,0:T(4,128)(2,1)S(1)}, u32[]{:S(2)}, u32[]{:S(2)}) collective-permute-start(bf16[4,2560]{1,0:T(4,128)(2,1)S(1)} %combine.1.rest_0_), channel_id=1, source_target_pairs={{0,8},{4,12},{8,0},{12,4},{1,9},{5,13},{9,1},{13,5},{2,10},{6,14},... | collective-permute-start | bytes 61448 | tf_op jit(solution)/shard_map/ppermute | solution.py:298
  15.3 1.2 %collective-permute-done.3.rest_1_ = bf16[4,2560]{1,0:T(4,128)(2,1)S(1)} collective-permute-done((bf16[4,2560]{1,0:T(4,128)(2,1)S(1)}, bf16[4,2560]{1,0:T(4,128)(2,1)S(1)}, u32[]{:S(2)}, u32[]{:S(2)}) %collective-permute-start.3) | collective-permute-done | bytes 20512 | tf_op jit(solution)/shard_map/ppermute | solution.py:298
  16.4 0.0 copy-done.1
  16.5 0.0 copy-done.4
  16.5 1.2 %accumulate.3.old_ref = f32[1,16,2560]{2,1,0:T(8,128)S(1)} custom-call(f32[1,4]{1,0:T(1,128)S(1)} %bitcast.1, s32[16,2560]{1,0:T(8,128)S(1)} %copy-done.1, f32[1,16,2560]{2,1,0:T(8,128)S(1)} %copy-done.2, bf16[4,2560]{1,0:T(4,128)(2,1)S(1)} %combine.1.rest_0_, bf16[4,2560]{1,0:T(4,128)(2,1)S(1)} %collective-permute-done.3.rest_1_), custom_call_target="tpu_custom_call" | custom-call | flops 81920000 | bytes 491520 | tf_op jit(solution)/shard_map/accumulate/pallas_call | solution.py:368
  17.7 0.7 %collective-permute-done.4.rest_0_ = bf16[4,2560]{1,0:T(4,128)(2,1)S(1)} collective-permute-done((bf16[4,2560]{1,0:T(4,128)(2,1)S(1)}, bf16[4,2560]{1,0:T(4,128)(2,1)S(1)}, u32[]{:S(2)}, u32[]{:S(2)}) %collective-permute-start.4) | collective-permute-done | bytes 20512 | tf_op jit(solution)/shard_map/ppermute | solution.py:298
  18.3 0.8 %accumulate.4.old_ref = f32[1,16,2560]{2,1,0:T(8,128)S(1)} custom-call(f32[1,4]{1,0:T(1,128)S(1)} %bitcast.2, s32[16,2560]{1,0:T(8,128)S(1)} %copy-done.1, f32[1,16,2560]{2,1,0:T(8,128)S(1)} %accumulate.3.old_ref, bf16[4,2560]{1,0:T(4,128)(2,1)S(1)} %collective-permute-done.4.rest_0_), custom_call_target="tpu_custom_call" | custom-call | flops 40960000 | bytes 491520 | tf_op jit(solution)/shard_map/accumulate/pallas_call | solution.py:368
  19.1 0.1 collective-permute-done.5.rest_0_
  19.2 1.4 %accumulate.5 = f32[1,16,2560]{2,1,0:T(8,128)} custom-call(f32[1,4]{1,0:T(1,128)S(1)} %bitcast.3, s32[16,2560]{1,0:T(8,128)S(1)} %copy-done.1, f32[1,16,2560]{2,1,0:T(8,128)S(1)} %accumulate.4.old_ref, bf16[4,2560]{1,0:T(4,128)(2,1)S(1)} %collective-permute-done.5.rest_0_), custom_call_target="tpu_custom_call" | custom-call | flops 40960000 | bytes 491520 | tf_op jit(solution)/shard_map/accumulate/pallas_call | solution.py:368
  (4 shorter events, 0.0 us)
Async XLA Ops:
  0.0 2.2 %copy-start = (bf16[1,1024,2048]{2,1,0:T(8,128)(2,1)S(1)}, bf16[1,1024,2048]{2,1,0:T(8,128)(2,1)}, u32[]{:S(2)}) copy-start(bf16[1,1024,2048]{2,1,0:T(8,128)(2,1)} %matrix_ref.1) | copy-start | bytes 12582916
  0.0 0.8 %copy-start.3 = (s32[1,2048]{1,0:T(1,128)S(1)}, s32[1,2048]{1,0:T(1,128)}, u32[]{:S(2)}) copy-start(s32[1,2048]{1,0:T(1,128)} %vertex_ref.3) | copy-start | bytes 24580
  2.1 14.3 %copy-start.1 = (s32[16,2560]{1,0:T(8,128)S(1)}, s32[16,2560]{1,0:T(8,128)}, u32[]{:S(2)}) copy-start(s32[16,2560]{1,0:T(8,128)} %transfer_ref.5) | copy-start | bytes 491524
  2.2 14.3 %copy-start.2 = (f32[1,16,2560]{2,1,0:T(8,128)S(1)}, f32[1,16,2560]{2,1,0:T(8,128)}, u32[]{:S(2)}) copy-start(f32[1,16,2560]{2,1,0:T(8,128)} %old_ref.1) | copy-start | bytes 491524
  2.2 14.3 %copy-start.4 = (f32[4]{0:T(128)S(1)}, f32[4]{0:T(128)}, u32[]{:S(2)}) copy-start(f32[4]{0:T(128)} %param.7) | copy-start | bytes 52
  4.6 3.1 %collective-permute-start = (f32[4,1280]{1,0:T(4,128)S(1)}, f32[4,1280]{1,0:T(4,128)S(1)}, u32[]{:S(2)}, u32[]{:S(2)}) collective-permute-start(f32[4,1280]{1,0:T(4,128)S(1)} %get-tuple-element.14), channel_id=1, source_target_pairs={{0,1},{1,0},{2,3},{3,2},{4,5},{5,4},{6,7},{7,6},{8,9},{9,8},{10,11... | collective-permute-start | bytes 61448 | tf_op jit(solution)/shard_map/ppermute | solution.py:298
  5.1 4.3 %collective-permute-start.1 = (f32[4,1280]{1,0:T(4,128)S(1)}, f32[4,1280]{1,0:T(4,128)S(1)}, u32[]{:S(2)}, u32[]{:S(2)}) collective-permute-start(f32[4,1280]{1,0:T(4,128)S(1)} %get-tuple-element.15), channel_id=1, source_target_pairs={{0,2},{1,3},{2,0},{3,1},{4,6},{5,7},{6,4},{7,5},{8,10},{9,11},{10,... | collective-permute-start | bytes 61448 | tf_op jit(solution)/shard_map/ppermute | solution.py:298
  7.6 3.2 %collective-permute-start.2 = (f32[4,1280]{1,0:T(4,128)S(1)}, f32[4,1280]{1,0:T(4,128)S(1)}, u32[]{:S(2)}, u32[]{:S(2)}) collective-permute-start(f32[4,1280]{1,0:T(4,128)S(1)} %get-tuple-element.16), channel_id=1, source_target_pairs={{0,3},{1,2},{2,1},{3,0},{4,7},{5,6},{6,5},{7,4},{8,11},{9,10},{10,... | collective-permute-start | bytes 61448 | tf_op jit(solution)/shard_map/ppermute | solution.py:298
  10.8 5.6 %collective-permute-start.3 = (bf16[4,2560]{1,0:T(4,128)(2,1)S(1)}, bf16[4,2560]{1,0:T(4,128)(2,1)S(1)}, u32[]{:S(2)}, u32[]{:S(2)}) collective-permute-start(bf16[4,2560]{1,0:T(4,128)(2,1)S(1)} %combine.1.rest_0_), channel_id=1, source_target_pairs={{0,12},{4,8},{8,4},{12,0},{1,13},{5,9},{9,5},{13,1},{2,14},{6,10},... | collective-permute-start | bytes 61448 | tf_op jit(solution)/shard_map/ppermute | solution.py:298
  14.5 3.9 %collective-permute-start.4 = (bf16[4,2560]{1,0:T(4,128)(2,1)S(1)}, bf16[4,2560]{1,0:T(4,128)(2,1)S(1)}, u32[]{:S(2)}, u32[]{:S(2)}) collective-permute-start(bf16[4,2560]{1,0:T(4,128)(2,1)S(1)} %combine.1.rest_0_), channel_id=1, source_target_pairs={{0,4},{4,0},{8,12},{12,8},{1,5},{5,1},{9,13},{13,9},{2,6},{6,2},{1... | collective-permute-start | bytes 61448 | tf_op jit(solution)/shard_map/ppermute | solution.py:298
  14.5 4.7 %collective-permute-start.5 = (bf16[4,2560]{1,0:T(4,128)(2,1)S(1)}, bf16[4,2560]{1,0:T(4,128)(2,1)S(1)}, u32[]{:S(2)}, u32[]{:S(2)}) collective-permute-start(bf16[4,2560]{1,0:T(4,128)(2,1)S(1)} %combine.1.rest_0_), channel_id=1, source_target_pairs={{0,8},{4,12},{8,0},{12,4},{1,9},{5,13},{9,1},{13,5},{2,10},{6,14},... | collective-permute-start | bytes 61448 | tf_op jit(solution)/shard_map/ppermute | solution.py:298

commit v3 on v2

--- a/solution.py
+++ b/solution.py
@@ -102,11 +102,29 @@
             table_ref[row : row + 2 * sublanes, here] = cas.astype(jnp.bfloat16)
 
 
-def table_kernel(sizes, vertex_ref, table_ref, left_ref):
+def transform_kernel(sizes, matrix_hbm, vertex_hbm, *rest):
+    *sent_refs, matrix_ref, vertex_ref, left_ref, early_ref, late_ref, weight_ref, matrix_sems, vertex_sem = rest
     blk_count, walk_count, sub_count, rows_own = sizes
     walk_index = lax.axis_index("walk")
     sub_index = lax.axis_index("sub")
-    window_rows, rows_local = left_ref.shape
+    rows_local, vertices = matrix_ref.shape
+    window_rows = left_ref.shape[0]
+    early = early_ref.shape[1]
+
+    vertex_copy = pltpu.make_async_copy(vertex_hbm, vertex_ref, vertex_sem)
+    vertex_copy.start()
+    parts = matrix_sems.shape[0]
+    part = vertices // parts
+    matrix_copies = [
+        pltpu.make_async_copy(
+            matrix_hbm.at[0, :, i * part : (i + 1) * part],
+            matrix_ref.at[:, i * part : (i + 1) * part],
+            matrix_sems.at[i],
+        )
+        for i in range(parts)
+    ]
+    for copy in matrix_copies:
+        copy.start()
 
     ids, inner = split_by(row_ids(window_rows), rows_own)
     ids, blk_part = split_by(ids, blk_count)
@@ -114,31 +132,26 @@
     sub_part = toward(sub_index, sub_part, sub_count)
     walk_part = toward(walk_index, walk_part, walk_count)
     window = ((blk_part * walk_count + walk_part) * sub_count + sub_part) * rows_own + inner
+
+    vertex_copy.wait()
     own_start = pl.multiple_of(walk_index * rows_local, lanes)
     for start in range(0, rows_local, lanes):
         own_vertex = vertex_ref[:, pl.ds(own_start + start, lanes)]
         cosine, sine = cos_sin(own_vertex * window)
         left_ref[:, start : start + lanes] = (cosine + sine).astype(jnp.bfloat16)
 
-    @pl.loop(0, table_ref.shape[1] // lanes)
+    @pl.loop(0, early // lanes)
     def _(step):
-        make_table(vertex_ref, table_ref, step * lanes, step * lanes, sub_index)
-
-
-def product_kernel(sizes, matrix_ref, vertex_ref, early_ref, left_ref, *rest):
-    *sent_refs, late_ref, weight_ref = rest
-    blk_count, _, _, rows_own = sizes
-    sub_index = lax.axis_index("sub")
-    vertices = matrix_ref.shape[2]
-    window_rows = left_ref.shape[0]
-    early = early_ref.shape[1]
+        make_table(vertex_ref, early_ref, step * lanes, step * lanes, sub_index)
 
     chunk = 4 * lanes
     tiles = list(range(0, vertices - early, lanes))
     chunks = list(range(0, vertices, chunk))
     for i, start in enumerate(chunks):
+        if start % part == 0:
+            matrix_copies[start // part].wait()
         left_product = jnp.dot(
-            left_ref[...], matrix_ref[0, :, start : start + chunk], preferred_element_type=jnp.float32
+            left_ref[...], matrix_ref[:, start : start + chunk], preferred_element_type=jnp.float32
         )
         for tile in tiles[i * len(tiles) // len(chunks) : (i + 1) * len(tiles) // len(chunks)]:
             make_table(vertex_ref, late_ref, early + tile, tile, sub_index)
@@ -309,36 +322,26 @@
     devices = blk_count * walk_count * sub_count
     sizes = (blk_count, walk_count, sub_count, rows_own)
     vmem = pl.BlockSpec(memory_space=pltpu.VMEM)
-    early = 5 * vertices // (8 * 2 * lanes) * 2 * lanes
-    table, left = pl.pallas_call(
-        functools.partial(table_kernel, sizes),
-        out_shape=[
-            jax.ShapeDtypeStruct((columns_local, early), jnp.bfloat16),
-            jax.ShapeDtypeStruct((devices * rows_own, rows_local), jnp.bfloat16),
-        ],
-        in_specs=[vmem],
-        out_specs=[vmem] * 2,
-        compiler_params=pltpu.CompilerParams(vmem_limit_bytes=24 * 2**20),
-        cost_estimate=pl.CostEstimate(
-            flops=2000 * columns_local * vertices,
-            bytes_accessed=6 * columns_local * vertices,
-            transcendentals=0,
-        ),
-        name="table",
-    )(vertex)
+    early = 3 * vertices // (8 * 2 * lanes) * 2 * lanes
     sent = pl.pallas_call(
-        functools.partial(product_kernel, sizes),
+        functools.partial(transform_kernel, sizes),
         out_shape=[jax.ShapeDtypeStruct((blk_count * rows_own, columns_local), jnp.float32)]
         * (walk_count * sub_count),
-        in_specs=[vmem] * 4,
+        in_specs=[pl.BlockSpec(memory_space=pltpu.HBM)] * 2,
         out_specs=[vmem] * (walk_count * sub_count),
         scratch_shapes=[
+            pltpu.VMEM((rows_local, vertices), jnp.bfloat16),
+            pltpu.VMEM((1, vertices), jnp.int32),
+            pltpu.VMEM((devices * rows_own, rows_local), jnp.bfloat16),
+            pltpu.VMEM((columns_local, early), jnp.bfloat16),
             pltpu.VMEM((columns_local, vertices - early), jnp.bfloat16),
             pltpu.VMEM((2 * devices * rows_own, vertices), jnp.bfloat16),
+            pltpu.SemaphoreType.DMA((2,)),
+            pltpu.SemaphoreType.DMA,
         ],
         compiler_params=pltpu.CompilerParams(vmem_limit_bytes=24 * 2**20),
-        name="product",
-    )(walker_mats, vertex, table, left)
+        name="transform",
+    )(*[pltpu.with_memory_space_constraint(x, pltpu.HBM) for x in (walker_mats, vertex)])
     parts = exchange(sent, ("walk", "sub"), (walk_count, sub_count))
     shared = blk_count <= RSTEPS
     rows_each = (blk_count if shared else RSTEPS) * rows_own

time: 20.8 us -> 21.4 us (1.029)
  Pallas kernels: 7.06 us -> 8.37 us
  local copies, waits for them, and re-layouts: 0.89 us -> 0.01 us
  waiting for transfers between devices: 5 us -> 5.27 us
    pallas_call x2 -> x1, Pallas kernels: 3.66 us -> 4.97 us  [local(): pl.pallas_call(functools.partial(transform_kernel, sizes), out_shape=[jax...]
    unnamed x10 -> x6, local copies, waits for them, and re-layouts: 0.89 us -> 0.01 us
    ppermute x6, waiting for transfers between devices: 5 us -> 5.27 us  [exchange(): arrived[i] = lax.ppermute(pieces[i], axes, route)]
  transfers between devices with their start and end apart: 6 -> 6, of which waited for: 5 -> 5; matrix products, arithmetic and copies ran while one was open for 0% -> 0% of each run, Pallas kernels for 10% -> 9%
where the time goes in v3:
time: 21.4 us; the launch traced here: 21.3 us
  Pallas kernels  8.37 us (39%)
  starting transfers between devices  7.61 us (36%)
  waiting for transfers between devices  5.27 us (25%)
    ppermute x6, starting transfers between devices, exchange(): arrived[i] = lax.ppermute(pieces[i], axes, route)  7.61 us
    ppermute x6, waiting for transfers between devices, exchange(): arrived[i] = lax.ppermute(pieces[i], axes, route)  5.27 us
    pallas_call x1, Pallas kernels, local(): pl.pallas_call(functools.partial(transform_kernel, sizes), out_shape=[jax...  4.97 us
    pallas_call x3, Pallas kernels, local(): pl.pallas_call(functools.partial(accumulate_kernel, sizes, places, last),...  3.38 us
  transfers between devices with their start and end apart: 6, of which 5 were waited for; matrix products, arithmetic and copies ran while one was open for 0% of the time, Pallas kernels for 9%

profile of v3, /device:TPU:0, one launch (start us, length us, event | category | flops | bytes accessed | tf_op | source)
XLA Modules:
  0.0 21.3 jit_solution(4492189587626147047)
XLA Ops:
  0.0 0.0 copy-start
  0.0 0.0 copy-start.1
  0.0 0.0 copy-start.2
  0.0 5.0 %transform.1 = (f32[4,1280]{1,0:T(4,128)S(1)}, f32[4,1280]{1,0:T(4,128)S(1)}, f32[4,1280]{1,0:T(4,128)S(1)}, f32[4,1280]{1,0:T(4,128)S(1)}) custom-call(bf16[1,1024,2048]{2,1,0:T(8,128)(2,1)} %matrix_hbm.1, s32[1,2048]{1,0:T(1,128)} %vertex_hbm.1), custom_call_target="tpu_custom_call" | custom-call | tf_op jit(solution)/shard_map/transform/pallas_call | solution.py:326
  5.0 0.5 %collective-permute-start = (f32[4,1280]{1,0:T(4,128)S(1)}, f32[4,1280]{1,0:T(4,128)S(1)}, u32[]{:S(2)}, u32[]{:S(2)}) collective-permute-start(f32[4,1280]{1,0:T(4,128)S(1)} %get-tuple-element.10), channel_id=1, source_target_pairs={{0,1},{1,0},{2,3},{3,2},{4,5},{5,4},{6,7},{7,6},{8,9},{9,8},{10,11... | collective-permute-start | bytes 61448 | tf_op jit(solution)/shard_map/ppermute | solution.py:311
  5.5 2.6 %collective-permute-start.1 = (f32[4,1280]{1,0:T(4,128)S(1)}, f32[4,1280]{1,0:T(4,128)S(1)}, u32[]{:S(2)}, u32[]{:S(2)}) collective-permute-start(f32[4,1280]{1,0:T(4,128)S(1)} %get-tuple-element.11), channel_id=1, source_target_pairs={{0,2},{1,3},{2,0},{3,1},{4,6},{5,7},{6,4},{7,5},{8,10},{9,11},{10,... | collective-permute-start | bytes 61448 | tf_op jit(solution)/shard_map/ppermute | solution.py:311
  8.1 0.1 collective-permute-start.2
  8.1 0.0 collective-permute-done.refs_1_
  8.1 1.7 %collective-permute-done.1.refs_2_ = f32[4,1280]{1,0:T(4,128)S(1)} collective-permute-done((f32[4,1280]{1,0:T(4,128)S(1)}, f32[4,1280]{1,0:T(4,128)S(1)}, u32[]{:S(2)}, u32[]{:S(2)}) %collective-permute-start.1) | collective-permute-done | bytes 20512 | tf_op jit(solution)/shard_map/ppermute | solution.py:311
  9.8 1.4 %collective-permute-done.2.refs_3_ = f32[4,1280]{1,0:T(4,128)S(1)} collective-permute-done((f32[4,1280]{1,0:T(4,128)S(1)}, f32[4,1280]{1,0:T(4,128)S(1)}, u32[]{:S(2)}, u32[]{:S(2)}) %collective-permute-start.2) | collective-permute-done | bytes 20512 | tf_op jit(solution)/shard_map/ppermute | solution.py:311
  11.3 3.7 %collective-permute-start.3 = (bf16[4,2560]{1,0:T(4,128)(2,1)S(1)}, bf16[4,2560]{1,0:T(4,128)(2,1)S(1)}, u32[]{:S(2)}, u32[]{:S(2)}) collective-permute-start(bf16[4,2560]{1,0:T(4,128)(2,1)S(1)} %combine.1.rest_0_), channel_id=1, source_target_pairs={{0,12},{4,8},{8,4},{12,0},{1,13},{5,9},{9,5},{13,1},{2,14},{6,10},... | collective-permute-start | bytes 61448 | tf_op jit(solution)/shard_map/ppermute | solution.py:311
  15.0 0.0 collective-permute-start.4
  15.0 0.8 %collective-permute-start.5 = (bf16[4,2560]{1,0:T(4,128)(2,1)S(1)}, bf16[4,2560]{1,0:T(4,128)(2,1)S(1)}, u32[]{:S(2)}, u32[]{:S(2)}) collective-permute-start(bf16[4,2560]{1,0:T(4,128)(2,1)S(1)} %combine.1.rest_0_), channel_id=1, source_target_pairs={{0,8},{4,12},{8,0},{12,4},{1,9},{5,13},{9,1},{13,5},{2,10},{6,14},... | collective-permute-start | bytes 61448 | tf_op jit(solution)/shard_map/ppermute | solution.py:311
  15.7 1.2 %collective-permute-done.3.rest_1_ = bf16[4,2560]{1,0:T(4,128)(2,1)S(1)} collective-permute-done((bf16[4,2560]{1,0:T(4,128)(2,1)S(1)}, bf16[4,2560]{1,0:T(4,128)(2,1)S(1)}, u32[]{:S(2)}, u32[]{:S(2)}) %collective-permute-start.3) | collective-permute-done | bytes 20512 | tf_op jit(solution)/shard_map/ppermute | solution.py:311
  16.9 0.0 copy-done
  16.9 0.0 copy-done.1
  16.9 0.0 copy-done.2
  16.9 1.2 %accumulate.3.old_ref = f32[1,16,2560]{2,1,0:T(8,128)S(1)} custom-call(f32[1,4]{1,0:T(1,128)S(1)} %bitcast.1, s32[16,2560]{1,0:T(8,128)S(1)} %copy-done, f32[1,16,2560]{2,1,0:T(8,128)S(1)} %copy-done.1, bf16[4,2560]{1,0:T(4,128)(2,1)S(1)} %combine.1.rest_0_, bf16[4,2560]{1,0:T(4,128)(2,1)S(1)} %collective-permute-done.3.rest_1_), custom_call_target="tpu_custom_call" | custom-call | flops 81920000 | bytes 491520 | tf_op jit(solution)/shard_map/accumulate/pallas_call | solution.py:371
  18.2 0.6 %collective-permute-done.4.rest_0_ = bf16[4,2560]{1,0:T(4,128)(2,1)S(1)} collective-permute-done((bf16[4,2560]{1,0:T(4,128)(2,1)S(1)}, bf16[4,2560]{1,0:T(4,128)(2,1)S(1)}, u32[]{:S(2)}, u32[]{:S(2)}) %collective-permute-start.4) | collective-permute-done | bytes 20512 | tf_op jit(solution)/shard_map/ppermute | solution.py:311
  18.8 0.8 %accumulate.4.old_ref = f32[1,16,2560]{2,1,0:T(8,128)S(1)} custom-call(f32[1,4]{1,0:T(1,128)S(1)} %bitcast.2, s32[16,2560]{1,0:T(8,128)S(1)} %copy-done, f32[1,16,2560]{2,1,0:T(8,128)S(1)} %accumulate.3.old_ref, bf16[4,2560]{1,0:T(4,128)(2,1)S(1)} %collective-permute-done.4.rest_0_), custom_call_target="tpu_custom_call" | custom-call | flops 40960000 | bytes 491520 | tf_op jit(solution)/shard_map/accumulate/pallas_call | solution.py:371
  19.5 0.3 %collective-permute-done.5.rest_0_ = bf16[4,2560]{1,0:T(4,128)(2,1)S(1)} collective-permute-done((bf16[4,2560]{1,0:T(4,128)(2,1)S(1)}, bf16[4,2560]{1,0:T(4,128)(2,1)S(1)}, u32[]{:S(2)}, u32[]{:S(2)}) %collective-permute-start.5) | collective-permute-done | bytes 20512 | tf_op jit(solution)/shard_map/ppermute | solution.py:311
  19.9 1.4 %accumulate.5 = f32[1,16,2560]{2,1,0:T(8,128)} custom-call(f32[1,4]{1,0:T(1,128)S(1)} %bitcast.3, s32[16,2560]{1,0:T(8,128)S(1)} %copy-done, f32[1,16,2560]{2,1,0:T(8,128)S(1)} %accumulate.4.old_ref, bf16[4,2560]{1,0:T(4,128)(2,1)S(1)} %collective-permute-done.5.rest_0_), custom_call_target="tpu_custom_call" | custom-call | flops 40960000 | bytes 491520 | tf_op jit(solution)/shard_map/accumulate/pallas_call | solution.py:371
  (1 shorter events, 0.0 us)
Async XLA Ops:
  0.0 16.9 %copy-start = (s32[16,2560]{1,0:T(8,128)S(1)}, s32[16,2560]{1,0:T(8,128)}, u32[]{:S(2)}) copy-start(s32[16,2560]{1,0:T(8,128)} %transfer_ref.5) | copy-start | bytes 491524
  0.0 16.9 %copy-start.1 = (f32[1,16,2560]{2,1,0:T(8,128)S(1)}, f32[1,16,2560]{2,1,0:T(8,128)}, u32[]{:S(2)}) copy-start(f32[1,16,2560]{2,1,0:T(8,128)} %old_ref.1) | copy-start | bytes 491524
  0.0 16.9 %copy-start.2 = (f32[4]{0:T(128)S(1)}, f32[4]{0:T(128)}, u32[]{:S(2)}) copy-start(f32[4]{0:T(128)} %param.7) | copy-start | bytes 52
  5.0 3.2 %collective-permute-start = (f32[4,1280]{1,0:T(4,128)S(1)}, f32[4,1280]{1,0:T(4,128)S(1)}, u32[]{:S(2)}, u32[]{:S(2)}) collective-permute-start(f32[4,1280]{1,0:T(4,128)S(1)} %get-tuple-element.10), channel_id=1, source_target_pairs={{0,1},{1,0},{2,3},{3,2},{4,5},{5,4},{6,7},{7,6},{8,9},{9,8},{10,11... | collective-permute-start | bytes 61448 | tf_op jit(solution)/shard_map/ppermute | solution.py:311
  5.5 4.3 %collective-permute-start.1 = (f32[4,1280]{1,0:T(4,128)S(1)}, f32[4,1280]{1,0:T(4,128)S(1)}, u32[]{:S(2)}, u32[]{:S(2)}) collective-permute-start(f32[4,1280]{1,0:T(4,128)S(1)} %get-tuple-element.11), channel_id=1, source_target_pairs={{0,2},{1,3},{2,0},{3,1},{4,6},{5,7},{6,4},{7,5},{8,10},{9,11},{10,... | collective-permute-start | bytes 61448 | tf_op jit(solution)/shard_map/ppermute | solution.py:311
  8.1 3.2 %collective-permute-start.2 = (f32[4,1280]{1,0:T(4,128)S(1)}, f32[4,1280]{1,0:T(4,128)S(1)}, u32[]{:S(2)}, u32[]{:S(2)}) collective-permute-start(f32[4,1280]{1,0:T(4,128)S(1)} %get-tuple-element.12), channel_id=1, source_target_pairs={{0,3},{1,2},{2,1},{3,0},{4,7},{5,6},{6,5},{7,4},{8,11},{9,10},{10,... | collective-permute-start | bytes 61448 | tf_op jit(solution)/shard_map/ppermute | solution.py:311
  11.3 5.6 %collective-permute-start.3 = (bf16[4,2560]{1,0:T(4,128)(2,1)S(1)}, bf16[4,2560]{1,0:T(4,128)(2,1)S(1)}, u32[]{:S(2)}, u32[]{:S(2)}) collective-permute-start(bf16[4,2560]{1,0:T(4,128)(2,1)S(1)} %combine.1.rest_0_), channel_id=1, source_target_pairs={{0,12},{4,8},{8,4},{12,0},{1,13},{5,9},{9,5},{13,1},{2,14},{6,10},... | collective-permute-start | bytes 61448 | tf_op jit(solution)/shard_map/ppermute | solution.py:311
  15.0 3.8 %collective-permute-start.4 = (bf16[4,2560]{1,0:T(4,128)(2,1)S(1)}, bf16[4,2560]{1,0:T(4,128)(2,1)S(1)}, u32[]{:S(2)}, u32[]{:S(2)}) collective-permute-start(bf16[4,2560]{1,0:T(4,128)(2,1)S(1)} %combine.1.rest_0_), channel_id=1, source_target_pairs={{0,4},{4,0},{8,12},{12,8},{1,5},{5,1},{9,13},{13,9},{2,6},{6,2},{1... | collective-permute-start | bytes 61448 | tf_op jit(solution)/shard_map/ppermute | solution.py:311
  15.0 4.9 %collective-permute-start.5 = (bf16[4,2560]{1,0:T(4,128)(2,1)S(1)}, bf16[4,2560]{1,0:T(4,128)(2,1)S(1)}, u32[]{:S(2)}, u32[]{:S(2)}) collective-permute-start(bf16[4,2560]{1,0:T(4,128)(2,1)S(1)} %combine.1.rest_0_), channel_id=1, source_target_pairs={{0,8},{4,12},{8,0},{12,4},{1,9},{5,13},{9,1},{13,5},{2,10},{6,14},... | collective-permute-start | bytes 61448 | tf_op jit(solution)/shard_map/ppermute | solution.py:311

commit v4 on v3

--- a/solution.py
+++ b/solution.py
@@ -20,6 +20,7 @@
 sublanes = 8
 code_limit = 32767.0
 smallest_peak = 1e-30
+exponent_margin = 1e-3
 
 
 def toward(index, distance, count):
@@ -67,13 +68,13 @@
     return pl.ds(start if isinstance(start, int) else pl.multiple_of(start, lanes), lanes)
 
 
-def make_table(vertex_ref, table_ref, first, place, sub_index):
+def make_table(vertex_ref, table_ref, first, place):
     columns = table_ref.shape[0]
     blocks = columns // lanes
     half_blocks = blocks // 2
     coarse_rows = -(-max(half_blocks, 1) // sublanes) * sublanes
     middle_count = lanes // sublanes
-    center = sub_index * columns + (blocks - 1) * (lanes // 2)
+    center = (blocks - 1) * (lanes // 2)
     here = tile_of(place)
     vertex = vertex_ref[:, tile_of(first)]
     cosine, sine = cos_sin(vertex * (row_ids(sublanes) + center))
@@ -102,29 +103,42 @@
             table_ref[row : row + 2 * sublanes, here] = cas.astype(jnp.bfloat16)
 
 
+def encode(rows):
+    half = rows.shape[1] // 2
+    peak = jnp.maximum(jnp.max(jnp.abs(rows), axis=1, keepdims=True), smallest_peak)
+    exponent = jnp.ceil(jnp.log2(peak * (1.0 / code_limit)) + exponent_margin)
+    codes = jnp.floor(rows * (1.0 / jnp.exp2(exponent)) + 0.5).astype(jnp.int32)
+    words = (codes[:, :half] << 16) | (codes[:, half:] & 0xFFFF)
+    tail = jnp.broadcast_to(exponent.astype(jnp.int32), (rows.shape[0], lanes))
+    return jnp.concatenate([words, tail], axis=1)
+
+
+def units(coded):
+    return jnp.exp2(coded[:, coded.shape[1] - lanes :].astype(jnp.float32))
+
+
+def decode(coded):
+    words = coded[:, : coded.shape[1] - lanes]
+    codes = jnp.concatenate([words >> 16, (words << 16) >> 16], axis=1)
+    return codes.astype(jnp.float32) * units(coded)[:, :1]
+
+
 def transform_kernel(sizes, matrix_hbm, vertex_hbm, *rest):
-    *sent_refs, matrix_ref, vertex_ref, left_ref, early_ref, late_ref, weight_ref, matrix_sems, vertex_sem = rest
+    *sent_refs, matrix_ref, vertex_ref, left_ref, early_ref, late_ref, weight_ref, matrix_sem, vertex_sem = rest
     blk_count, walk_count, sub_count, rows_own = sizes
     walk_index = lax.axis_index("walk")
     sub_index = lax.axis_index("sub")
-    rows_local, vertices = matrix_ref.shape
+    rows_local, vertices_local = matrix_ref.shape
     window_rows = left_ref.shape[0]
     early = early_ref.shape[1]
 
     vertex_copy = pltpu.make_async_copy(vertex_hbm, vertex_ref, vertex_sem)
     vertex_copy.start()
-    parts = matrix_sems.shape[0]
-    part = vertices // parts
-    matrix_copies = [
-        pltpu.make_async_copy(
-            matrix_hbm.at[0, :, i * part : (i + 1) * part],
-            matrix_ref.at[:, i * part : (i + 1) * part],
-            matrix_sems.at[i],
-        )
-        for i in range(parts)
-    ]
-    for copy in matrix_copies:
-        copy.start()
+    first = pl.multiple_of(sub_index * vertices_local, lanes)
+    matrix_copy = pltpu.make_async_copy(
+        matrix_hbm.at[0, :, pl.ds(first, vertices_local)], matrix_ref, matrix_sem
+    )
+    matrix_copy.start()
 
     ids, inner = split_by(row_ids(window_rows), rows_own)
     ids, blk_part = split_by(ids, blk_count)
@@ -142,65 +156,56 @@
 
     @pl.loop(0, early // lanes)
     def _(step):
-        make_table(vertex_ref, early_ref, step * lanes, step * lanes, sub_index)
-
-    chunk = 4 * lanes
-    tiles = list(range(0, vertices - early, lanes))
-    chunks = list(range(0, vertices, chunk))
-    for i, start in enumerate(chunks):
-        if start % part == 0:
-            matrix_copies[start // part].wait()
+        make_table(vertex_ref, early_ref, first + step * lanes, step * lanes)
+
+    matrix_copy.wait()
+    late = vertices_local - early
+    for start, size in ((0, early), (early, late)):
         left_product = jnp.dot(
-            left_ref[...], matrix_ref[:, start : start + chunk], preferred_element_type=jnp.float32
+            left_ref[...], matrix_ref[:, start : start + size], preferred_element_type=jnp.float32
         )
-        for tile in tiles[i * len(tiles) // len(chunks) : (i + 1) * len(tiles) // len(chunks)]:
-            make_table(vertex_ref, late_ref, early + tile, tile, sub_index)
         high = left_product.astype(jnp.bfloat16)
-        weight_ref[:window_rows, start : start + chunk] = high
-        weight_ref[window_rows:, start : start + chunk] = (
+        weight_ref[:window_rows, start : start + size] = high
+        weight_ref[window_rows:, start : start + size] = (
             left_product - high.astype(jnp.float32)
         ).astype(jnp.bfloat16)
+    for tile in range(0, late, lanes):
+        make_table(vertex_ref, late_ref, first + early + tile, tile)
     green = sum(
         lax.dot_general(
+            table_ref[...],
             weight_ref[:, start : start + table_ref.shape[1]],
-            table_ref[...],
             (((1,), (1,)), ((), ())),
             preferred_element_type=jnp.float32,
         )
         for start, table_ref in ((0, early_ref), (early, late_ref))
-    )
+    ).T
     green = green[:window_rows] + green[window_rows:]
     rows_each = blk_count * rows_own
     for place, sent_ref in enumerate(sent_refs):
-        sent_ref[...] = green[place * rows_each : (place + 1) * rows_each]
-
-
-def pick_rows(rows, wanted):
-    ids = lax.broadcasted_iota(jnp.int32, (wanted.shape[0], rows.shape[0]), 1)
-    chosen = jnp.where(ids == wanted, 1.0, 0.0).astype(jnp.bfloat16)
-    return jnp.dot(chosen, rows, preferred_element_type=jnp.float32)
+        rows = green[place * rows_each : (place + 1) * rows_each]
+        sent_ref[...] = rows if place == 0 else encode(rows)
 
 
 def combine_kernel(sizes, *refs):
     blk_count, walk_count, sub_count, rows_own = sizes
     blk_index = lax.axis_index("blk")
-    sub_index = lax.axis_index("sub")
-    part_refs, whole_refs = refs[: walk_count * sub_count], refs[walk_count * sub_count :]
-    columns_part = part_refs[0].shape[1]
-    for distance in range(sub_count):
-        sub_part = back(sub_index, distance, sub_count)
-        here = pl.ds(pl.multiple_of(sub_part * columns_part, lanes), columns_part)
-        total = sum(
-            part_refs[walk_part * sub_count + distance][...] for walk_part in range(walk_count)
-        ).astype(jnp.bfloat16)
-        if len(whole_refs) == 1:
-            whole_refs[0][:, here] = total
-            continue
-        for place, whole_ref in enumerate(whole_refs):
-            ids = lax.broadcasted_iota(jnp.int32, (whole_ref.shape[0], 1), 0)
-            step, inner = split_by(ids, rows_own)
-            _, blk_part = split_by(toward(blk_index, place, blk_count) + RSTEPS * blk_count - step, blk_count)
-            whole_ref[:, here] = pick_rows(total, blk_part * rows_own + inner).astype(whole_ref.dtype)
+    parts = walk_count * sub_count
+    part_refs, whole_refs, row_ref = refs[:parts], refs[parts:-1], refs[-1]
+    total = part_refs[0][...] + sum(decode(part_ref[...]) for part_ref in part_refs[1:])
+    coded = encode(total)
+    if len(whole_refs) == 1:
+        whole_refs[0][...] = coded
+        return
+    for row in range(blk_count * rows_own):
+        row_ref[row] = coded[row : row + 1]
+    for place, whole_ref in enumerate(whole_refs):
+        for step in range(RSTEPS):
+            blk_part = toward(blk_index, place, blk_count) + RSTEPS * blk_count - step
+            _, blk_part = split_by(blk_part, blk_count)
+            for inner in range(rows_own):
+                row = step * rows_own + inner
+                whole_ref[row : row + 1] = row_ref[blk_part * rows_own + inner]
 
 
 def accumulate_kernel(sizes, distances, last, weights_ref, transfer_ref, old_ref, *rest):
@@ -238,19 +243,16 @@
 
     for own in range(rows_own):
         for place, distance in enumerate(distances):
-            rows = arrived_refs[place][...].astype(jnp.float32)
+            coded = arrived_refs[place][...]
             walker = back(blk_index, distance, blk_count)
             weight = jnp.sum(jnp.where(walker_ids == walker, weights, 0.0), axis=1, keepdims=True)
-            left = rows[own : own + 1]
-            for blk_part in range(1, rows.shape[0] // rows_own):
+            left = coded[own : own + 1]
+            for blk_part in range(1, coded.shape[0] // rows_own):
                 row = blk_part * rows_own + own
-                left = jnp.where(step[:1] == blk_part, rows[row : row + 1], left)
-            left_ref[place] = left * weight
-            peak = jnp.maximum(jnp.max(jnp.abs(rows), axis=1, keepdims=True), smallest_peak)
-            codes = jnp.floor(rows * (code_limit / peak) + 0.5).astype(jnp.int32)
-            peak = jnp.broadcast_to(peak * (1.0 / code_limit), (rows.shape[0], lanes))
-            unit_ref[place] = spread(peak, own)
-            source_ref[place] = spread((codes[:, :half] << 16) | (codes[:, half:] & 0xFFFF), own)
+                left = jnp.where(step[:1] == blk_part, coded[row : row + 1], left)
+            left_ref[place] = decode(left) * weight
+            unit_ref[place] = spread(units(coded), own)
+            source_ref[place] = spread(coded[:, :half], own)
 
         together = len(distances) if len(distances) <= 4 else math.gcd(len(distances), 4)
 
@@ -318,25 +320,28 @@
     sub_count = lax.axis_size("sub")
     rows_local, vertices = walker_mats.shape[1:]
     rows_own, transfers, columns = g4_old.shape
-    columns_local = columns // sub_count
     devices = blk_count * walk_count * sub_count
     sizes = (blk_count, walk_count, sub_count, rows_own)
     vmem = pl.BlockSpec(memory_space=pltpu.VMEM)
-    early = 3 * vertices // (8 * 2 * lanes) * 2 * lanes
+    vertices_local = vertices // sub_count
+    early = vertices_local // (4 * lanes) * 2 * lanes
+    coded = columns // 2 + lanes
     sent = pl.pallas_call(
         functools.partial(transform_kernel, sizes),
-        out_shape=[jax.ShapeDtypeStruct((blk_count * rows_own, columns_local), jnp.float32)]
-        * (walk_count * sub_count),
-        in_specs=[pl.BlockSpec(memory_space=pltpu.HBM)] * 2,
+        out_shape=[
+            jax.ShapeDtypeStruct((blk_count * rows_own, coded if place else columns), jnp.int32 if place else jnp.float32)
+            for place in range(walk_count * sub_count)
+        ],
+        in_specs=[pl.BlockSpec(memory_space=pl.ANY)] * 2,
         out_specs=[vmem] * (walk_count * sub_count),
         scratch_shapes=[
-            pltpu.VMEM((rows_local, vertices), jnp.bfloat16),
+            pltpu.VMEM((rows_local, vertices_local), jnp.bfloat16),
             pltpu.VMEM((1, vertices), jnp.int32),
             pltpu.VMEM((devices * rows_own, rows_local), jnp.bfloat16),
-            pltpu.VMEM((columns_local, early), jnp.bfloat16),
-            pltpu.VMEM((columns_local, vertices - early), jnp.bfloat16),
-            pltpu.VMEM((2 * devices * rows_own, vertices), jnp.bfloat16),
-            pltpu.SemaphoreType.DMA((2,)),
+            pltpu.VMEM((columns, early), jnp.bfloat16),
+            pltpu.VMEM((columns, vertices_local - early), jnp.bfloat16),
+            pltpu.VMEM((2 * devices * rows_own, vertices_local), jnp.bfloat16),
+            pltpu.SemaphoreType.DMA,
             pltpu.SemaphoreType.DMA,
         ],
         compiler_params=pltpu.CompilerParams(vmem_limit_bytes=24 * 2**20),
@@ -348,9 +353,10 @@
     whole_count = 1 if shared else blk_count
     whole = pl.pallas_call(
         functools.partial(combine_kernel, sizes),
-        out_shape=[jax.ShapeDtypeStruct((rows_each, columns), jnp.bfloat16)] * whole_count,
+        out_shape=[jax.ShapeDtypeStruct((rows_each, coded), jnp.int32)] * whole_count,
         in_specs=[vmem] * len(parts),
         out_specs=[vmem] * whole_count,
+        scratch_shapes=[pltpu.VMEM((blk_count * rows_own, 1, coded), jnp.int32)],
         compiler_params=pltpu.CompilerParams(vmem_limit_bytes=24 * 2**20),
         name="combine",
     )(*parts)

time: 21.4 us -> 20.5 us (0.958)
  Pallas kernels: 8.37 us -> 7.12 us
  waiting for transfers between devices: 5.27 us -> 5.55 us
    pallas_call x1, Pallas kernels: 4.97 us -> 3.83 us  [local(): pl.pallas_call(functools.partial(transform_kernel, sizes), out_shape=[jax...]
    pallas_call x3, Pallas kernels: 3.38 us -> 3.07 us  [local(): pl.pallas_call(functools.partial(accumulate_kernel, sizes, places, last),...]
    ppermute x6, waiting for transfers between devices: 5.27 us -> 5.55 us  [exchange(): arrived[i] = lax.ppermute(pieces[i], axes, route)]
where the time goes in v4:
time: 20.5 us; the launch traced here: 20.3 us
  starting transfers between devices  7.61 us (37%)
  Pallas kernels  7.12 us (35%)
  waiting for transfers between devices  5.55 us (27%)
    ppermute x6, starting transfers between devices, exchange(): arrived[i] = lax.ppermute(pieces[i], axes, route)  7.61 us
    ppermute x6, waiting for transfers between devices, exchange(): arrived[i] = lax.ppermute(pieces[i], axes, route)  5.55 us
    pallas_call x1, Pallas kernels, local(): pl.pallas_call(functools.partial(transform_kernel, sizes), out_shape=[jax...  3.83 us
    pallas_call x3, Pallas kernels, local(): pl.pallas_call(functools.partial(accumulate_kernel, sizes, places, last),...  3.07 us
  transfers between devices with their start and end apart: 6, of which 5 were waited for; matrix products, arithmetic and copies ran while one was open for 0% of the time, Pallas kernels for 9%

profile of v4, /device:TPU:0, one launch (start us, length us, event | category | flops | bytes accessed | tf_op | source)
XLA Modules:
  0.0 20.3 jit_solution(12435398494368914054)
XLA Ops:
  0.0 0.0 copy-start
  0.0 0.0 copy-start.1
  0.0 0.0 copy-start.2
  0.0 3.8 %transform.1 = (f32[4,2560]{1,0:T(4,128)S(1)}, s32[4,1408]{1,0:T(4,128)S(1)}, s32[4,1408]{1,0:T(4,128)S(1)}, s32[4,1408]{1,0:T(4,128)S(1)}) custom-call(bf16[1,1024,2048]{2,1,0:T(8,128)(2,1)} %matrix_hbm.1, s32[1,2048]{1,0:T(1,128)} %vertex_hbm.1), custom_call_target="tpu_custom_call" | custom-call | tf_op jit(solution)/shard_map/transform/pallas_call | solution.py:329
  3.8 0.5 %collective-permute-start = (s32[4,1408]{1,0:T(4,128)S(1)}, s32[4,1408]{1,0:T(4,128)S(1)}, u32[]{:S(2)}, u32[]{:S(2)}) collective-permute-start(s32[4,1408]{1,0:T(4,128)S(1)} %get-tuple-element.10), channel_id=1, source_target_pairs={{0,1},{1,0},{2,3},{3,2},{4,5},{5,4},{6,7},{7,6},{8,9},{9,8},{10,11... | collective-permute-start | bytes 67592 | tf_op jit(solution)/shard_map/ppermute | solution.py:313
  4.4 2.6 %collective-permute-start.1 = (s32[4,1408]{1,0:T(4,128)S(1)}, s32[4,1408]{1,0:T(4,128)S(1)}, u32[]{:S(2)}, u32[]{:S(2)}) collective-permute-start(s32[4,1408]{1,0:T(4,128)S(1)} %get-tuple-element.11), channel_id=1, source_target_pairs={{0,2},{1,3},{2,0},{3,1},{4,6},{5,7},{6,4},{7,5},{8,10},{9,11},{10,... | collective-permute-start | bytes 67592 | tf_op jit(solution)/shard_map/ppermute | solution.py:313
  6.9 0.1 collective-permute-start.2
  7.0 0.0 collective-permute-done.refs_1_
  7.0 1.7 %collective-permute-done.1.refs_2_ = s32[4,1408]{1,0:T(4,128)S(1)} collective-permute-done((s32[4,1408]{1,0:T(4,128)S(1)}, s32[4,1408]{1,0:T(4,128)S(1)}, u32[]{:S(2)}, u32[]{:S(2)}) %collective-permute-start.1) | collective-permute-done | bytes 22560 | tf_op jit(solution)/shard_map/ppermute | solution.py:313
  8.7 1.4 %collective-permute-done.2.refs_3_ = s32[4,1408]{1,0:T(4,128)S(1)} collective-permute-done((s32[4,1408]{1,0:T(4,128)S(1)}, s32[4,1408]{1,0:T(4,128)S(1)}, u32[]{:S(2)}, u32[]{:S(2)}) %collective-permute-start.2) | collective-permute-done | bytes 22560 | tf_op jit(solution)/shard_map/ppermute | solution.py:313
  10.2 0.2 %combine.1.rest_0_ = s32[4,1408]{1,0:T(4,128)S(1)} custom-call(f32[4,2560]{1,0:T(4,128)S(1)} %get-tuple-element.9.refs_0_, s32[4,1408]{1,0:T(4,128)S(1)} %collective-permute-done.refs_1_, s32[4,1408]{1,0:T(4,128)S(1)} %collective-permute-done.1.refs_2_, s32[4,1408]{1,0:T(4,128)S(1)} %collective-permute-done.2.refs_3_), custom_call_target="tpu_custom_call" | custom-call | tf_op jit(solution)/shard_map/combine/pallas_call | solution.py:354
  10.4 3.7 %collective-permute-start.3 = (s32[4,1408]{1,0:T(4,128)S(1)}, s32[4,1408]{1,0:T(4,128)S(1)}, u32[]{:S(2)}, u32[]{:S(2)}) collective-permute-start(s32[4,1408]{1,0:T(4,128)S(1)} %combine.1.rest_0_), channel_id=1, source_target_pairs={{0,12},{4,8},{8,4},{12,0},{1,13},{5,9},{9,5},{13,1},{2,14},{6,10},... | collective-permute-start | bytes 67592 | tf_op jit(solution)/shard_map/ppermute | solution.py:313
  14.1 0.0 collective-permute-start.4
  14.1 0.8 %collective-permute-start.5 = (s32[4,1408]{1,0:T(4,128)S(1)}, s32[4,1408]{1,0:T(4,128)S(1)}, u32[]{:S(2)}, u32[]{:S(2)}) collective-permute-start(s32[4,1408]{1,0:T(4,128)S(1)} %combine.1.rest_0_), channel_id=1, source_target_pairs={{0,8},{4,12},{8,0},{12,4},{1,9},{5,13},{9,1},{13,5},{2,10},{6,14},... | collective-permute-start | bytes 67592 | tf_op jit(solution)/shard_map/ppermute | solution.py:313
  14.8 1.2 %collective-permute-done.3.rest_1_ = s32[4,1408]{1,0:T(4,128)S(1)} collective-permute-done((s32[4,1408]{1,0:T(4,128)S(1)}, s32[4,1408]{1,0:T(4,128)S(1)}, u32[]{:S(2)}, u32[]{:S(2)}) %collective-permute-start.3) | collective-permute-done | bytes 22560 | tf_op jit(solution)/shard_map/ppermute | solution.py:313
  16.1 0.0 copy-done
  16.1 0.0 copy-done.1
  16.1 0.0 copy-done.2
  16.1 1.1 %accumulate.3.old_ref = f32[1,16,2560]{2,1,0:T(8,128)S(1)} custom-call(f32[1,4]{1,0:T(1,128)S(1)} %bitcast.1, s32[16,2560]{1,0:T(8,128)S(1)} %copy-done, f32[1,16,2560]{2,1,0:T(8,128)S(1)} %copy-done.1, s32[4,1408]{1,0:T(4,128)S(1)} %combine.1.rest_0_, s32[4,1408]{1,0:T(4,128)S(1)} %collective-permute-done.3.rest_1_), custom_call_target="tpu_custom_call" | custom-call | flops 81920000 | bytes 491520 | tf_op jit(solution)/shard_map/accumulate/pallas_call | solution.py:377
  17.2 0.8 %collective-permute-done.4.rest_0_ = s32[4,1408]{1,0:T(4,128)S(1)} collective-permute-done((s32[4,1408]{1,0:T(4,128)S(1)}, s32[4,1408]{1,0:T(4,128)S(1)}, u32[]{:S(2)}, u32[]{:S(2)}) %collective-permute-start.4) | collective-permute-done | bytes 22560 | tf_op jit(solution)/shard_map/ppermute | solution.py:313
  17.9 0.7 %accumulate.4.old_ref = f32[1,16,2560]{2,1,0:T(8,128)S(1)} custom-call(f32[1,4]{1,0:T(1,128)S(1)} %bitcast.2, s32[16,2560]{1,0:T(8,128)S(1)} %copy-done, f32[1,16,2560]{2,1,0:T(8,128)S(1)} %accumulate.3.old_ref, s32[4,1408]{1,0:T(4,128)S(1)} %collective-permute-done.4.rest_0_), custom_call_target="tpu_custom_call" | custom-call | flops 40960000 | bytes 491520 | tf_op jit(solution)/shard_map/accumulate/pallas_call | solution.py:377
  18.6 0.4 %collective-permute-done.5.rest_0_ = s32[4,1408]{1,0:T(4,128)S(1)} collective-permute-done((s32[4,1408]{1,0:T(4,128)S(1)}, s32[4,1408]{1,0:T(4,128)S(1)}, u32[]{:S(2)}, u32[]{:S(2)}) %collective-permute-start.5) | collective-permute-done | bytes 22560 | tf_op jit(solution)/shard_map/ppermute | solution.py:313
  19.0 1.3 %accumulate.5 = f32[1,16,2560]{2,1,0:T(8,128)} custom-call(f32[1,4]{1,0:T(1,128)S(1)} %bitcast.3, s32[16,2560]{1,0:T(8,128)S(1)} %copy-done, f32[1,16,2560]{2,1,0:T(8,128)S(1)} %accumulate.4.old_ref, s32[4,1408]{1,0:T(4,128)S(1)} %collective-permute-done.5.rest_0_), custom_call_target="tpu_custom_call" | custom-call | flops 40960000 | bytes 491520 | tf_op jit(solution)/shard_map/accumulate/pallas_call | solution.py:377
Async XLA Ops:
  0.0 16.1 %copy-start = (s32[16,2560]{1,0:T(8,128)S(1)}, s32[16,2560]{1,0:T(8,128)}, u32[]{:S(2)}) copy-start(s32[16,2560]{1,0:T(8,128)} %transfer_ref.5) | copy-start | bytes 491524
  0.0 16.1 %copy-start.1 = (f32[1,16,2560]{2,1,0:T(8,128)S(1)}, f32[1,16,2560]{2,1,0:T(8,128)}, u32[]{:S(2)}) copy-start(f32[1,16,2560]{2,1,0:T(8,128)} %old_ref.1) | copy-start | bytes 491524
  0.0 16.1 %copy-start.2 = (f32[4]{0:T(128)S(1)}, f32[4]{0:T(128)}, u32[]{:S(2)}) copy-start(f32[4]{0:T(128)} %param.7) | copy-start | bytes 52
  3.8 3.2 %collective-permute-start = (s32[4,1408]{1,0:T(4,128)S(1)}, s32[4,1408]{1,0:T(4,128)S(1)}, u32[]{:S(2)}, u32[]{:S(2)}) collective-permute-start(s32[4,1408]{1,0:T(4,128)S(1)} %get-tuple-element.10), channel_id=1, source_target_pairs={{0,1},{1,0},{2,3},{3,2},{4,5},{5,4},{6,7},{7,6},{8,9},{9,8},{10,11... | collective-permute-start | bytes 67592 | tf_op jit(solution)/shard_map/ppermute | solution.py:313
  4.4 4.3 %collective-permute-start.1 = (s32[4,1408]{1,0:T(4,128)S(1)}, s32[4,1408]{1,0:T(4,128)S(1)}, u32[]{:S(2)}, u32[]{:S(2)}) collective-permute-start(s32[4,1408]{1,0:T(4,128)S(1)} %get-tuple-element.11), channel_id=1, source_target_pairs={{0,2},{1,3},{2,0},{3,1},{4,6},{5,7},{6,4},{7,5},{8,10},{9,11},{10,... | collective-permute-start | bytes 67592 | tf_op jit(solution)/shard_map/ppermute | solution.py:313
  6.9 3.2 %collective-permute-start.2 = (s32[4,1408]{1,0:T(4,128)S(1)}, s32[4,1408]{1,0:T(4,128)S(1)}, u32[]{:S(2)}, u32[]{:S(2)}) collective-permute-start(s32[4,1408]{1,0:T(4,128)S(1)} %get-tuple-element.12), channel_id=1, source_target_pairs={{0,3},{1,2},{2,1},{3,0},{4,7},{5,6},{6,5},{7,4},{8,11},{9,10},{10,... | collective-permute-start | bytes 67592 | tf_op jit(solution)/shard_map/ppermute | solution.py:313
  10.4 5.7 %collective-permute-start.3 = (s32[4,1408]{1,0:T(4,128)S(1)}, s32[4,1408]{1,0:T(4,128)S(1)}, u32[]{:S(2)}, u32[]{:S(2)}) collective-permute-start(s32[4,1408]{1,0:T(4,128)S(1)} %combine.1.rest_0_), channel_id=1, source_target_pairs={{0,12},{4,8},{8,4},{12,0},{1,13},{5,9},{9,5},{13,1},{2,14},{6,10},... | collective-permute-start | bytes 67592 | tf_op jit(solution)/shard_map/ppermute | solution.py:313
  14.1 3.9 %collective-permute-start.4 = (s32[4,1408]{1,0:T(4,128)S(1)}, s32[4,1408]{1,0:T(4,128)S(1)}, u32[]{:S(2)}, u32[]{:S(2)}) collective-permute-start(s32[4,1408]{1,0:T(4,128)S(1)} %combine.1.rest_0_), channel_id=1, source_target_pairs={{0,4},{4,0},{8,12},{12,8},{1,5},{5,1},{9,13},{13,9},{2,6},{6,2},{1... | collective-permute-start | bytes 67592 | tf_op jit(solution)/shard_map/ppermute | solution.py:313
  14.1 4.9 %collective-permute-start.5 = (s32[4,1408]{1,0:T(4,128)S(1)}, s32[4,1408]{1,0:T(4,128)S(1)}, u32[]{:S(2)}, u32[]{:S(2)}) collective-permute-start(s32[4,1408]{1,0:T(4,128)S(1)} %combine.1.rest_0_), channel_id=1, source_target_pairs={{0,8},{4,12},{8,0},{12,4},{1,9},{5,13},{9,1},{13,5},{2,10},{6,14},... | collective-permute-start | bytes 67592 | tf_op jit(solution)/shard_map/ppermute | solution.py:313

commit v5 on v4

--- a/solution.py
+++ b/solution.py
@@ -124,7 +124,7 @@
 
 
 def transform_kernel(sizes, matrix_hbm, vertex_hbm, *rest):
-    *sent_refs, matrix_ref, vertex_ref, left_ref, early_ref, late_ref, weight_ref, matrix_sem, vertex_sem = rest
+    *sent_refs, matrix_ref, vertex_ref, left_ref, early_ref, middle_ref, late_ref, weight_ref, matrix_sem, vertex_sem = rest
     blk_count, walk_count, sub_count, rows_own = sizes
     walk_index = lax.axis_index("walk")
     sub_index = lax.axis_index("sub")
@@ -154,32 +154,35 @@
         cosine, sine = cos_sin(own_vertex * window)
         left_ref[:, start : start + lanes] = (cosine + sine).astype(jnp.bfloat16)
 
-    @pl.loop(0, early // lanes)
+    @pl.loop(0, early // lanes, unroll=2)
     def _(step):
         make_table(vertex_ref, early_ref, first + step * lanes, step * lanes)
 
     matrix_copy.wait()
-    late = vertices_local - early
-    for start, size in ((0, early), (early, late)):
+    chunk = 4 * lanes
+    for start in range(0, vertices_local, chunk):
         left_product = jnp.dot(
-            left_ref[...], matrix_ref[:, start : start + size], preferred_element_type=jnp.float32
+            left_ref[...], matrix_ref[:, start : start + chunk], preferred_element_type=jnp.float32
         )
         high = left_product.astype(jnp.bfloat16)
-        weight_ref[:window_rows, start : start + size] = high
-        weight_ref[window_rows:, start : start + size] = (
+        weight_ref[:window_rows, start : start + chunk] = high
+        weight_ref[window_rows:, start : start + chunk] = (
             left_product - high.astype(jnp.float32)
         ).astype(jnp.bfloat16)
-    for tile in range(0, late, lanes):
-        make_table(vertex_ref, late_ref, first + early + tile, tile)
-    green = sum(
-        lax.dot_general(
+    green, start = 0.0, 0
+    for table_ref in (early_ref, middle_ref, late_ref):
+        size = table_ref.shape[1]
+        if table_ref is not early_ref:
+            for tile in range(0, size, lanes):
+                make_table(vertex_ref, table_ref, first + start + tile, tile)
+        green += lax.dot_general(
             table_ref[...],
-            weight_ref[:, start : start + table_ref.shape[1]],
+            weight_ref[:, start : start + size],
             (((1,), (1,)), ((), ())),
             preferred_element_type=jnp.float32,
         )
-        for start, table_ref in ((0, early_ref), (early, late_ref))
-    ).T
+        start += size
+    green = green.T
     green = green[:window_rows] + green[window_rows:]
     rows_each = blk_count * rows_own
     for place, sent_ref in enumerate(sent_refs):
@@ -325,6 +328,7 @@
     vmem = pl.BlockSpec(memory_space=pltpu.VMEM)
     vertices_local = vertices // sub_count
     early = vertices_local // (4 * lanes) * 2 * lanes
+    middle = early // 2
     coded = columns // 2 + lanes
     sent = pl.pallas_call(
         functools.partial(transform_kernel, sizes),
@@ -339,7 +343,8 @@
             pltpu.VMEM((1, vertices), jnp.int32),
             pltpu.VMEM((devices * rows_own, rows_local), jnp.bfloat16),
             pltpu.VMEM((columns, early), jnp.bfloat16),
-            pltpu.VMEM((columns, vertices_local - early), jnp.bfloat16),
+            pltpu.VMEM((columns, middle), jnp.bfloat16),
+            pltpu.VMEM((columns, vertices_local - early - middle), jnp.bfloat16),
             pltpu.VMEM((2 * devices * rows_own, vertices_local), jnp.bfloat16),
             pltpu.SemaphoreType.DMA,
             pltpu.SemaphoreType.DMA,
@@ -347,6 +352,9 @@
         compiler_params=pltpu.CompilerParams(vmem_limit_bytes=24 * 2**20),
         name="transform",
     )(*[pltpu.with_memory_space_constraint(x, pltpu.HBM) for x in (walker_mats, vertex)])
+    sent, weights, transfer_table, g4_old = lax.optimization_barrier(
+        (sent, weights, transfer_table, g4_old)
+    )
     parts = exchange(sent, ("walk", "sub"), (walk_count, sub_count))
     shared = blk_count <= RSTEPS
     rows_each = (blk_count if shared else RSTEPS) * rows_own

time: 20.5 us -> 20.6 us (level)
  no operation moved by 1% of the time
where the time goes in v5:
time: 20.6 us; the launch traced here: 20.4 us
  starting transfers between devices  7.61 us (37%)
  Pallas kernels  7.21 us (35%)
  waiting for transfers between devices  5.55 us (27%)
    ppermute x6, starting transfers between devices, exchange(): arrived[i] = lax.ppermute(pieces[i], axes, route)  7.61 us
    ppermute x6, waiting for transfers between devices, exchange(): arrived[i] = lax.ppermute(pieces[i], axes, route)  5.55 us
    pallas_call x1, Pallas kernels, local(): pl.pallas_call(functools.partial(transform_kernel, sizes), out_shape=[jax...  3.93 us
    pallas_call x3, Pallas kernels, local(): pl.pallas_call(functools.partial(accumulate_kernel, sizes, places, last),...  3.07 us
  transfers between devices with their start and end apart: 6, of which 5 were waited for; matrix products, arithmetic and copies ran while one was open for 0% of the time, Pallas kernels for 9%

profile of v5, /device:TPU:0, one launch (start us, length us, event | category | flops | bytes accessed | tf_op | source)
XLA Modules:
  0.0 20.4 jit_solution(8552756146366229496)
XLA Ops:
  0.0 0.0 copy-start.1
  0.0 0.0 copy-start
  0.0 0.0 copy-start.2
  0.0 3.9 %transform.1 = (f32[4,2560]{1,0:T(4,128)S(1)}, s32[4,1408]{1,0:T(4,128)S(1)}, s32[4,1408]{1,0:T(4,128)S(1)}, s32[4,1408]{1,0:T(4,128)S(1)}) custom-call(bf16[1,1024,2048]{2,1,0:T(8,128)(2,1)} %matrix_hbm.1, s32[1,2048]{1,0:T(1,128)} %vertex_hbm.1), custom_call_target="tpu_custom_call" | custom-call | tf_op jit(solution)/shard_map/transform/pallas_call | solution.py:333
  3.9 0.5 %collective-permute-start = (s32[4,1408]{1,0:T(4,128)S(1)}, s32[4,1408]{1,0:T(4,128)S(1)}, u32[]{:S(2)}, u32[]{:S(2)}) collective-permute-start(s32[4,1408]{1,0:T(4,128)S(1)} %get-tuple-element.24), channel_id=1, source_target_pairs={{0,1},{1,0},{2,3},{3,2},{4,5},{5,4},{6,7},{7,6},{8,9},{9,8},{10,11... | collective-permute-start | bytes 67592 | tf_op jit(solution)/shard_map/ppermute | solution.py:316
  4.5 2.6 %collective-permute-start.1 = (s32[4,1408]{1,0:T(4,128)S(1)}, s32[4,1408]{1,0:T(4,128)S(1)}, u32[]{:S(2)}, u32[]{:S(2)}) collective-permute-start(s32[4,1408]{1,0:T(4,128)S(1)} %get-tuple-element.25), channel_id=1, source_target_pairs={{0,2},{1,3},{2,0},{3,1},{4,6},{5,7},{6,4},{7,5},{8,10},{9,11},{10,... | collective-permute-start | bytes 67592 | tf_op jit(solution)/shard_map/ppermute | solution.py:316
  7.0 0.1 collective-permute-start.2
  7.1 0.0 collective-permute-done.refs_1_
  7.1 1.7 %collective-permute-done.1.refs_2_ = s32[4,1408]{1,0:T(4,128)S(1)} collective-permute-done((s32[4,1408]{1,0:T(4,128)S(1)}, s32[4,1408]{1,0:T(4,128)S(1)}, u32[]{:S(2)}, u32[]{:S(2)}) %collective-permute-start.1) | collective-permute-done | bytes 22560 | tf_op jit(solution)/shard_map/ppermute | solution.py:316
  8.8 1.4 %collective-permute-done.2.refs_3_ = s32[4,1408]{1,0:T(4,128)S(1)} collective-permute-done((s32[4,1408]{1,0:T(4,128)S(1)}, s32[4,1408]{1,0:T(4,128)S(1)}, u32[]{:S(2)}, u32[]{:S(2)}) %collective-permute-start.2) | collective-permute-done | bytes 22560 | tf_op jit(solution)/shard_map/ppermute | solution.py:316
  10.3 0.2 %combine.1.rest_0_ = s32[4,1408]{1,0:T(4,128)S(1)} custom-call(f32[4,2560]{1,0:T(4,128)S(1)} %get-tuple-element.23.refs_0_, s32[4,1408]{1,0:T(4,128)S(1)} %collective-permute-done.refs_1_, s32[4,1408]{1,0:T(4,128)S(1)} %collective-permute-done.1.refs_2_, s32[4,1408]{1,0:T(4,128)S(1)} %collective-permute-done.2.refs_3_), custom_call_target="tpu_custom_call" | custom-call | tf_op jit(solution)/shard_map/combine/pallas_call | solution.py:362
  10.5 3.7 %collective-permute-start.3 = (s32[4,1408]{1,0:T(4,128)S(1)}, s32[4,1408]{1,0:T(4,128)S(1)}, u32[]{:S(2)}, u32[]{:S(2)}) collective-permute-start(s32[4,1408]{1,0:T(4,128)S(1)} %combine.1.rest_0_), channel_id=1, source_target_pairs={{0,12},{4,8},{8,4},{12,0},{1,13},{5,9},{9,5},{13,1},{2,14},{6,10},... | collective-permute-start | bytes 67592 | tf_op jit(solution)/shard_map/ppermute | solution.py:316
  14.1 0.0 collective-permute-start.4
  14.1 0.8 %collective-permute-start.5 = (s32[4,1408]{1,0:T(4,128)S(1)}, s32[4,1408]{1,0:T(4,128)S(1)}, u32[]{:S(2)}, u32[]{:S(2)}) collective-permute-start(s32[4,1408]{1,0:T(4,128)S(1)} %combine.1.rest_0_), channel_id=1, source_target_pairs={{0,8},{4,12},{8,0},{12,4},{1,9},{5,13},{9,1},{13,5},{2,10},{6,14},... | collective-permute-start | bytes 67592 | tf_op jit(solution)/shard_map/ppermute | solution.py:316
  14.9 1.2 %collective-permute-done.3.rest_1_ = s32[4,1408]{1,0:T(4,128)S(1)} collective-permute-done((s32[4,1408]{1,0:T(4,128)S(1)}, s32[4,1408]{1,0:T(4,128)S(1)}, u32[]{:S(2)}, u32[]{:S(2)}) %collective-permute-start.3) | collective-permute-done | bytes 22560 | tf_op jit(solution)/shard_map/ppermute | solution.py:316
  16.1 0.0 copy-done.1
  16.1 0.0 copy-done
  16.2 0.0 copy-done.2
  16.2 1.1 %accumulate.3.old_ref = f32[1,16,2560]{2,1,0:T(8,128)S(1)} custom-call(f32[1,4]{1,0:T(1,128)S(1)} %bitcast.1, s32[16,2560]{1,0:T(8,128)S(1)} %copy-done, f32[1,16,2560]{2,1,0:T(8,128)S(1)} %copy-done.1, s32[4,1408]{1,0:T(4,128)S(1)} %combine.1.rest_0_, s32[4,1408]{1,0:T(4,128)S(1)} %collective-permute-done.3.rest_1_), custom_call_target="tpu_custom_call" | custom-call | flops 81920000 | bytes 491520 | tf_op jit(solution)/shard_map/accumulate/pallas_call | solution.py:385
  17.3 0.8 %collective-permute-done.4.rest_0_ = s32[4,1408]{1,0:T(4,128)S(1)} collective-permute-done((s32[4,1408]{1,0:T(4,128)S(1)}, s32[4,1408]{1,0:T(4,128)S(1)}, u32[]{:S(2)}, u32[]{:S(2)}) %collective-permute-start.4) | collective-permute-done | bytes 22560 | tf_op jit(solution)/shard_map/ppermute | solution.py:316
  18.0 0.7 %accumulate.4.old_ref = f32[1,16,2560]{2,1,0:T(8,128)S(1)} custom-call(f32[1,4]{1,0:T(1,128)S(1)} %bitcast.2, s32[16,2560]{1,0:T(8,128)S(1)} %copy-done, f32[1,16,2560]{2,1,0:T(8,128)S(1)} %accumulate.3.old_ref, s32[4,1408]{1,0:T(4,128)S(1)} %collective-permute-done.4.rest_0_), custom_call_target="tpu_custom_call" | custom-call | flops 40960000 | bytes 491520 | tf_op jit(solution)/shard_map/accumulate/pallas_call | solution.py:385
  18.7 0.4 %collective-permute-done.5.rest_0_ = s32[4,1408]{1,0:T(4,128)S(1)} collective-permute-done((s32[4,1408]{1,0:T(4,128)S(1)}, s32[4,1408]{1,0:T(4,128)S(1)}, u32[]{:S(2)}, u32[]{:S(2)}) %collective-permute-start.5) | collective-permute-done | bytes 22560 | tf_op jit(solution)/shard_map/ppermute | solution.py:316
  19.1 1.3 %accumulate.5 = f32[1,16,2560]{2,1,0:T(8,128)} custom-call(f32[1,4]{1,0:T(1,128)S(1)} %bitcast.3, s32[16,2560]{1,0:T(8,128)S(1)} %copy-done, f32[1,16,2560]{2,1,0:T(8,128)S(1)} %accumulate.4.old_ref, s32[4,1408]{1,0:T(4,128)S(1)} %collective-permute-done.5.rest_0_), custom_call_target="tpu_custom_call" | custom-call | flops 40960000 | bytes 491520 | tf_op jit(solution)/shard_map/accumulate/pallas_call | solution.py:385
Async XLA Ops:
  0.0 16.1 %copy-start.1 = (f32[1,16,2560]{2,1,0:T(8,128)S(1)}, f32[1,16,2560]{2,1,0:T(8,128)}, u32[]{:S(2)}) copy-start(f32[1,16,2560]{2,1,0:T(8,128)} %old_ref) | copy-start | bytes 491524
  0.0 16.1 %copy-start = (s32[16,2560]{1,0:T(8,128)S(1)}, s32[16,2560]{1,0:T(8,128)}, u32[]{:S(2)}) copy-start(s32[16,2560]{1,0:T(8,128)} %transfer_ref.2) | copy-start | bytes 491524
  0.0 16.1 %copy-start.2 = (f32[4]{0:T(128)S(1)}, f32[4]{0:T(128)}, u32[]{:S(2)}) copy-start(f32[4]{0:T(128)} %param.7) | copy-start | bytes 52
  3.9 3.2 %collective-permute-start = (s32[4,1408]{1,0:T(4,128)S(1)}, s32[4,1408]{1,0:T(4,128)S(1)}, u32[]{:S(2)}, u32[]{:S(2)}) collective-permute-start(s32[4,1408]{1,0:T(4,128)S(1)} %get-tuple-element.24), channel_id=1, source_target_pairs={{0,1},{1,0},{2,3},{3,2},{4,5},{5,4},{6,7},{7,6},{8,9},{9,8},{10,11... | collective-permute-start | bytes 67592 | tf_op jit(solution)/shard_map/ppermute | solution.py:316
  4.5 4.3 %collective-permute-start.1 = (s32[4,1408]{1,0:T(4,128)S(1)}, s32[4,1408]{1,0:T(4,128)S(1)}, u32[]{:S(2)}, u32[]{:S(2)}) collective-permute-start(s32[4,1408]{1,0:T(4,128)S(1)} %get-tuple-element.25), channel_id=1, source_target_pairs={{0,2},{1,3},{2,0},{3,1},{4,6},{5,7},{6,4},{7,5},{8,10},{9,11},{10,... | collective-permute-start | bytes 67592 | tf_op jit(solution)/shard_map/ppermute | solution.py:316
  7.0 3.2 %collective-permute-start.2 = (s32[4,1408]{1,0:T(4,128)S(1)}, s32[4,1408]{1,0:T(4,128)S(1)}, u32[]{:S(2)}, u32[]{:S(2)}) collective-permute-start(s32[4,1408]{1,0:T(4,128)S(1)} %get-tuple-element.26), channel_id=1, source_target_pairs={{0,3},{1,2},{2,1},{3,0},{4,7},{5,6},{6,5},{7,4},{8,11},{9,10},{10,... | collective-permute-start | bytes 67592 | tf_op jit(solution)/shard_map/ppermute | solution.py:316
  10.5 5.7 %collective-permute-start.3 = (s32[4,1408]{1,0:T(4,128)S(1)}, s32[4,1408]{1,0:T(4,128)S(1)}, u32[]{:S(2)}, u32[]{:S(2)}) collective-permute-start(s32[4,1408]{1,0:T(4,128)S(1)} %combine.1.rest_0_), channel_id=1, source_target_pairs={{0,12},{4,8},{8,4},{12,0},{1,13},{5,9},{9,5},{13,1},{2,14},{6,10},... | collective-permute-start | bytes 67592 | tf_op jit(solution)/shard_map/ppermute | solution.py:316
  14.1 3.9 %collective-permute-start.4 = (s32[4,1408]{1,0:T(4,128)S(1)}, s32[4,1408]{1,0:T(4,128)S(1)}, u32[]{:S(2)}, u32[]{:S(2)}) collective-permute-start(s32[4,1408]{1,0:T(4,128)S(1)} %combine.1.rest_0_), channel_id=1, source_target_pairs={{0,4},{4,0},{8,12},{12,8},{1,5},{5,1},{9,13},{13,9},{2,6},{6,2},{1... | collective-permute-start | bytes 67592 | tf_op jit(solution)/shard_map/ppermute | solution.py:316
  14.1 4.9 %collective-permute-start.5 = (s32[4,1408]{1,0:T(4,128)S(1)}, s32[4,1408]{1,0:T(4,128)S(1)}, u32[]{:S(2)}, u32[]{:S(2)}) collective-permute-start(s32[4,1408]{1,0:T(4,128)S(1)} %combine.1.rest_0_), channel_id=1, source_target_pairs={{0,8},{4,12},{8,0},{12,4},{1,9},{5,13},{9,1},{13,5},{2,10},{6,14},... | collective-permute-start | bytes 67592 | tf_op jit(solution)/shard_map/ppermute | solution.py:316

commit v6 on v5

--- a/solution.py
+++ b/solution.py
@@ -154,7 +154,7 @@
         cosine, sine = cos_sin(own_vertex * window)
         left_ref[:, start : start + lanes] = (cosine + sine).astype(jnp.bfloat16)
 
-    @pl.loop(0, early // lanes, unroll=2)
+    @pl.loop(0, early // lanes)
     def _(step):
         make_table(vertex_ref, early_ref, first + step * lanes, step * lanes)
 
@@ -185,9 +185,10 @@
     green = green.T
     green = green[:window_rows] + green[window_rows:]
     rows_each = blk_count * rows_own
+    coded = encode(green)
     for place, sent_ref in enumerate(sent_refs):
-        rows = green[place * rows_each : (place + 1) * rows_each]
-        sent_ref[...] = rows if place == 0 else encode(rows)
+        rows = coded if place else green
+        sent_ref[...] = rows[place * rows_each : (place + 1) * rows_each]
 
 
 def combine_kernel(sizes, *refs):
@@ -352,9 +353,6 @@
         compiler_params=pltpu.CompilerParams(vmem_limit_bytes=24 * 2**20),
         name="transform",
     )(*[pltpu.with_memory_space_constraint(x, pltpu.HBM) for x in (walker_mats, vertex)])
-    sent, weights, transfer_table, g4_old = lax.optimization_barrier(
-        (sent, weights, transfer_table, g4_old)
-    )
     parts = exchange(sent, ("walk", "sub"), (walk_count, sub_count))
     shared = blk_count <= RSTEPS
     rows_each = (blk_count if shared else RSTEPS) * rows_own

time: 20.6 us -> 20.5 us (level)
  no operation moved by 1% of the time
where the time goes in v6:
time: 20.5 us; the launch traced here: 20.3 us
  starting transfers between devices  7.61 us (37%)
  Pallas kernels  7.13 us (35%)
  waiting for transfers between devices  5.55 us (27%)
    ppermute x6, starting transfers between devices, exchange(): arrived[i] = lax.ppermute(pieces[i], axes, route)  7.61 us
    ppermute x6, waiting for transfers between devices, exchange(): arrived[i] = lax.ppermute(pieces[i], axes, route)  5.55 us
    pallas_call x1, Pallas kernels, local(): pl.pallas_call(functools.partial(transform_kernel, sizes), out_shape=[jax...  3.84 us
    pallas_call x3, Pallas kernels, local(): pl.pallas_call(functools.partial(accumulate_kernel, sizes, places, last),...  3.07 us
  transfers between devices with their start and end apart: 6, of which 5 were waited for; matrix products, arithmetic and copies ran while one was open for 0% of the time, Pallas kernels for 9%

profile of v6, /device:TPU:0, one launch (start us, length us, event | category | flops | bytes accessed | tf_op | source)
XLA Modules:
  0.0 20.3 jit_solution(5066779347090159913)
XLA Ops:
  0.0 0.0 copy-start
  0.0 0.0 copy-start.1
  0.0 0.0 copy-start.2
  0.0 3.8 %transform.1 = (f32[4,2560]{1,0:T(4,128)S(1)}, s32[4,1408]{1,0:T(4,128)S(1)}, s32[4,1408]{1,0:T(4,128)S(1)}, s32[4,1408]{1,0:T(4,128)S(1)}) custom-call(bf16[1,1024,2048]{2,1,0:T(8,128)(2,1)} %matrix_hbm.1, s32[1,2048]{1,0:T(1,128)} %vertex_hbm.1), custom_call_target="tpu_custom_call" | custom-call | tf_op jit(solution)/shard_map/transform/pallas_call | solution.py:334
  3.9 0.5 %collective-permute-start = (s32[4,1408]{1,0:T(4,128)S(1)}, s32[4,1408]{1,0:T(4,128)S(1)}, u32[]{:S(2)}, u32[]{:S(2)}) collective-permute-start(s32[4,1408]{1,0:T(4,128)S(1)} %get-tuple-element.10), channel_id=1, source_target_pairs={{0,1},{1,0},{2,3},{3,2},{4,5},{5,4},{6,7},{7,6},{8,9},{9,8},{10,11... | collective-permute-start | bytes 67592 | tf_op jit(solution)/shard_map/ppermute | solution.py:317
  4.4 2.6 %collective-permute-start.1 = (s32[4,1408]{1,0:T(4,128)S(1)}, s32[4,1408]{1,0:T(4,128)S(1)}, u32[]{:S(2)}, u32[]{:S(2)}) collective-permute-start(s32[4,1408]{1,0:T(4,128)S(1)} %get-tuple-element.11), channel_id=1, source_target_pairs={{0,2},{1,3},{2,0},{3,1},{4,6},{5,7},{6,4},{7,5},{8,10},{9,11},{10,... | collective-permute-start | bytes 67592 | tf_op jit(solution)/shard_map/ppermute | solution.py:317
  6.9 0.1 collective-permute-start.2
  7.0 0.0 collective-permute-done.refs_1_
  7.0 1.7 %collective-permute-done.1.refs_2_ = s32[4,1408]{1,0:T(4,128)S(1)} collective-permute-done((s32[4,1408]{1,0:T(4,128)S(1)}, s32[4,1408]{1,0:T(4,128)S(1)}, u32[]{:S(2)}, u32[]{:S(2)}) %collective-permute-start.1) | collective-permute-done | bytes 22560 | tf_op jit(solution)/shard_map/ppermute | solution.py:317
  8.7 1.4 %collective-permute-done.2.refs_3_ = s32[4,1408]{1,0:T(4,128)S(1)} collective-permute-done((s32[4,1408]{1,0:T(4,128)S(1)}, s32[4,1408]{1,0:T(4,128)S(1)}, u32[]{:S(2)}, u32[]{:S(2)}) %collective-permute-start.2) | collective-permute-done | bytes 22560 | tf_op jit(solution)/shard_map/ppermute | solution.py:317
  10.2 0.2 %combine.1.rest_0_ = s32[4,1408]{1,0:T(4,128)S(1)} custom-call(f32[4,2560]{1,0:T(4,128)S(1)} %get-tuple-element.9.refs_0_, s32[4,1408]{1,0:T(4,128)S(1)} %collective-permute-done.refs_1_, s32[4,1408]{1,0:T(4,128)S(1)} %collective-permute-done.1.refs_2_, s32[4,1408]{1,0:T(4,128)S(1)} %collective-permute-done.2.refs_3_), custom_call_target="tpu_custom_call" | custom-call | tf_op jit(solution)/shard_map/combine/pallas_call | solution.py:360
  10.4 3.7 %collective-permute-start.3 = (s32[4,1408]{1,0:T(4,128)S(1)}, s32[4,1408]{1,0:T(4,128)S(1)}, u32[]{:S(2)}, u32[]{:S(2)}) collective-permute-start(s32[4,1408]{1,0:T(4,128)S(1)} %combine.1.rest_0_), channel_id=1, source_target_pairs={{0,12},{4,8},{8,4},{12,0},{1,13},{5,9},{9,5},{13,1},{2,14},{6,10},... | collective-permute-start | bytes 67592 | tf_op jit(solution)/shard_map/ppermute | solution.py:317
  14.1 0.0 collective-permute-start.4
  14.1 0.8 %collective-permute-start.5 = (s32[4,1408]{1,0:T(4,128)S(1)}, s32[4,1408]{1,0:T(4,128)S(1)}, u32[]{:S(2)}, u32[]{:S(2)}) collective-permute-start(s32[4,1408]{1,0:T(4,128)S(1)} %combine.1.rest_0_), channel_id=1, source_target_pairs={{0,8},{4,12},{8,0},{12,4},{1,9},{5,13},{9,1},{13,5},{2,10},{6,14},... | collective-permute-start | bytes 67592 | tf_op jit(solution)/shard_map/ppermute | solution.py:317
  14.8 1.2 %collective-permute-done.3.rest_1_ = s32[4,1408]{1,0:T(4,128)S(1)} collective-permute-done((s32[4,1408]{1,0:T(4,128)S(1)}, s32[4,1408]{1,0:T(4,128)S(1)}, u32[]{:S(2)}, u32[]{:S(2)}) %collective-permute-start.3) | collective-permute-done | bytes 22560 | tf_op jit(solution)/shard_map/ppermute | solution.py:317
  16.1 0.0 copy-done
  16.1 0.0 copy-done.1
  16.1 0.0 copy-done.2
  16.1 1.1 %accumulate.3.old_ref = f32[1,16,2560]{2,1,0:T(8,128)S(1)} custom-call(f32[1,4]{1,0:T(1,128)S(1)} %bitcast.1, s32[16,2560]{1,0:T(8,128)S(1)} %copy-done, f32[1,16,2560]{2,1,0:T(8,128)S(1)} %copy-done.1, s32[4,1408]{1,0:T(4,128)S(1)} %combine.1.rest_0_, s32[4,1408]{1,0:T(4,128)S(1)} %collective-permute-done.3.rest_1_), custom_call_target="tpu_custom_call" | custom-call | flops 81920000 | bytes 491520 | tf_op jit(solution)/shard_map/accumulate/pallas_call | solution.py:383
  17.2 0.8 %collective-permute-done.4.rest_0_ = s32[4,1408]{1,0:T(4,128)S(1)} collective-permute-done((s32[4,1408]{1,0:T(4,128)S(1)}, s32[4,1408]{1,0:T(4,128)S(1)}, u32[]{:S(2)}, u32[]{:S(2)}) %collective-permute-start.4) | collective-permute-done | bytes 22560 | tf_op jit(solution)/shard_map/ppermute | solution.py:317
  17.9 0.7 %accumulate.4.old_ref = f32[1,16,2560]{2,1,0:T(8,128)S(1)} custom-call(f32[1,4]{1,0:T(1,128)S(1)} %bitcast.2, s32[16,2560]{1,0:T(8,128)S(1)} %copy-done, f32[1,16,2560]{2,1,0:T(8,128)S(1)} %accumulate.3.old_ref, s32[4,1408]{1,0:T(4,128)S(1)} %collective-permute-done.4.rest_0_), custom_call_target="tpu_custom_call" | custom-call | flops 40960000 | bytes 491520 | tf_op jit(solution)/shard_map/accumulate/pallas_call | solution.py:383
  18.6 0.4 %collective-permute-done.5.rest_0_ = s32[4,1408]{1,0:T(4,128)S(1)} collective-permute-done((s32[4,1408]{1,0:T(4,128)S(1)}, s32[4,1408]{1,0:T(4,128)S(1)}, u32[]{:S(2)}, u32[]{:S(2)}) %collective-permute-start.5) | collective-permute-done | bytes 22560 | tf_op jit(solution)/shard_map/ppermute | solution.py:317
  19.0 1.3 %accumulate.5 = f32[1,16,2560]{2,1,0:T(8,128)} custom-call(f32[1,4]{1,0:T(1,128)S(1)} %bitcast.3, s32[16,2560]{1,0:T(8,128)S(1)} %copy-done, f32[1,16,2560]{2,1,0:T(8,128)S(1)} %accumulate.4.old_ref, s32[4,1408]{1,0:T(4,128)S(1)} %collective-permute-done.5.rest_0_), custom_call_target="tpu_custom_call" | custom-call | flops 40960000 | bytes 491520 | tf_op jit(solution)/shard_map/accumulate/pallas_call | solution.py:383
Async XLA Ops:
  0.0 16.1 %copy-start = (s32[16,2560]{1,0:T(8,128)S(1)}, s32[16,2560]{1,0:T(8,128)}, u32[]{:S(2)}) copy-start(s32[16,2560]{1,0:T(8,128)} %transfer_ref.5) | copy-start | bytes 491524
  0.0 16.1 %copy-start.1 = (f32[1,16,2560]{2,1,0:T(8,128)S(1)}, f32[1,16,2560]{2,1,0:T(8,128)}, u32[]{:S(2)}) copy-start(f32[1,16,2560]{2,1,0:T(8,128)} %old_ref.1) | copy-start | bytes 491524
  0.0 16.1 %copy-start.2 = (f32[4]{0:T(128)S(1)}, f32[4]{0:T(128)}, u32[]{:S(2)}) copy-start(f32[4]{0:T(128)} %param.7) | copy-start | bytes 52
  3.9 3.2 %collective-permute-start = (s32[4,1408]{1,0:T(4,128)S(1)}, s32[4,1408]{1,0:T(4,128)S(1)}, u32[]{:S(2)}, u32[]{:S(2)}) collective-permute-start(s32[4,1408]{1,0:T(4,128)S(1)} %get-tuple-element.10), channel_id=1, source_target_pairs={{0,1},{1,0},{2,3},{3,2},{4,5},{5,4},{6,7},{7,6},{8,9},{9,8},{10,11... | collective-permute-start | bytes 67592 | tf_op jit(solution)/shard_map/ppermute | solution.py:317
  4.4 4.3 %collective-permute-start.1 = (s32[4,1408]{1,0:T(4,128)S(1)}, s32[4,1408]{1,0:T(4,128)S(1)}, u32[]{:S(2)}, u32[]{:S(2)}) collective-permute-start(s32[4,1408]{1,0:T(4,128)S(1)} %get-tuple-element.11), channel_id=1, source_target_pairs={{0,2},{1,3},{2,0},{3,1},{4,6},{5,7},{6,4},{7,5},{8,10},{9,11},{10,... | collective-permute-start | bytes 67592 | tf_op jit(solution)/shard_map/ppermute | solution.py:317
  6.9 3.2 %collective-permute-start.2 = (s32[4,1408]{1,0:T(4,128)S(1)}, s32[4,1408]{1,0:T(4,128)S(1)}, u32[]{:S(2)}, u32[]{:S(2)}) collective-permute-start(s32[4,1408]{1,0:T(4,128)S(1)} %get-tuple-element.12), channel_id=1, source_target_pairs={{0,3},{1,2},{2,1},{3,0},{4,7},{5,6},{6,5},{7,4},{8,11},{9,10},{10,... | collective-permute-start | bytes 67592 | tf_op jit(solution)/shard_map/ppermute | solution.py:317
  10.4 5.7 %collective-permute-start.3 = (s32[4,1408]{1,0:T(4,128)S(1)}, s32[4,1408]{1,0:T(4,128)S(1)}, u32[]{:S(2)}, u32[]{:S(2)}) collective-permute-start(s32[4,1408]{1,0:T(4,128)S(1)} %combine.1.rest_0_), channel_id=1, source_target_pairs={{0,12},{4,8},{8,4},{12,0},{1,13},{5,9},{9,5},{13,1},{2,14},{6,10},... | collective-permute-start | bytes 67592 | tf_op jit(solution)/shard_map/ppermute | solution.py:317
  14.1 3.9 %collective-permute-start.4 = (s32[4,1408]{1,0:T(4,128)S(1)}, s32[4,1408]{1,0:T(4,128)S(1)}, u32[]{:S(2)}, u32[]{:S(2)}) collective-permute-start(s32[4,1408]{1,0:T(4,128)S(1)} %combine.1.rest_0_), channel_id=1, source_target_pairs={{0,4},{4,0},{8,12},{12,8},{1,5},{5,1},{9,13},{13,9},{2,6},{6,2},{1... | collective-permute-start | bytes 67592 | tf_op jit(solution)/shard_map/ppermute | solution.py:317
  14.1 4.9 %collective-permute-start.5 = (s32[4,1408]{1,0:T(4,128)S(1)}, s32[4,1408]{1,0:T(4,128)S(1)}, u32[]{:S(2)}, u32[]{:S(2)}) collective-permute-start(s32[4,1408]{1,0:T(4,128)S(1)} %combine.1.rest_0_), channel_id=1, source_target_pairs={{0,8},{4,12},{8,0},{12,4},{1,9},{5,13},{9,1},{13,5},{2,10},{6,14},... | collective-permute-start | bytes 67592 | tf_op jit(solution)/shard_map/ppermute | solution.py:317

commit v7 on v6

--- a/solution.py
+++ b/solution.py
@@ -328,8 +328,8 @@
     sizes = (blk_count, walk_count, sub_count, rows_own)
     vmem = pl.BlockSpec(memory_space=pltpu.VMEM)
     vertices_local = vertices // sub_count
-    early = vertices_local // (4 * lanes) * 2 * lanes
-    middle = early // 2
+    early = vertices_local // (8 * lanes) * 2 * lanes
+    middle = 2 * early
     coded = columns // 2 + lanes
     sent = pl.pallas_call(
         functools.partial(transform_kernel, sizes),

time: 20.5 us -> 20.8 us (1.015)
  Pallas kernels: 7.13 us -> 7.45 us
    pallas_call x1, Pallas kernels: 3.84 us -> 4.16 us  [local(): pl.pallas_call(functools.partial(transform_kernel, sizes), out_shape=[jax...]
  transfers between devices with their start and end apart: 6 -> 6, of which waited for: 5 -> 5; matrix products, arithmetic and copies ran while one was open for 0% -> 0% of each run, Pallas kernels for 9% -> 8%
where the time goes in v7:
time: 20.8 us; the launch traced here: 20.7 us
  starting transfers between devices  7.61 us (37%)
  Pallas kernels  7.45 us (36%)
  waiting for transfers between devices  5.55 us (27%)
    ppermute x6, starting transfers between devices, exchange(): arrived[i] = lax.ppermute(pieces[i], axes, route)  7.61 us
    ppermute x6, waiting for transfers between devices, exchange(): arrived[i] = lax.ppermute(pieces[i], axes, route)  5.55 us
    pallas_call x1, Pallas kernels, local(): pl.pallas_call(functools.partial(transform_kernel, sizes), out_shape=[jax...  4.16 us
    pallas_call x3, Pallas kernels, local(): pl.pallas_call(functools.partial(accumulate_kernel, sizes, places, last),...  3.07 us
  transfers between devices with their start and end apart: 6, of which 5 were waited for; matrix products, arithmetic and copies ran while one was open for 0% of the time, Pallas kernels for 8%

profile of v7, /device:TPU:0, one launch (start us, length us, event | category | flops | bytes accessed | tf_op | source)
XLA Modules:
  0.0 20.7 jit_solution(10516351049342650707)
XLA Ops:
  0.0 0.0 copy-start
  0.0 0.0 copy-start.1
  0.0 0.0 copy-start.2
  0.0 4.2 %transform.1 = (f32[4,2560]{1,0:T(4,128)S(1)}, s32[4,1408]{1,0:T(4,128)S(1)}, s32[4,1408]{1,0:T(4,128)S(1)}, s32[4,1408]{1,0:T(4,128)S(1)}) custom-call(bf16[1,1024,2048]{2,1,0:T(8,128)(2,1)} %matrix_hbm.1, s32[1,2048]{1,0:T(1,128)} %vertex_hbm.1), custom_call_target="tpu_custom_call" | custom-call | tf_op jit(solution)/shard_map/transform/pallas_call | solution.py:334
  4.2 0.5 %collective-permute-start = (s32[4,1408]{1,0:T(4,128)S(1)}, s32[4,1408]{1,0:T(4,128)S(1)}, u32[]{:S(2)}, u32[]{:S(2)}) collective-permute-start(s32[4,1408]{1,0:T(4,128)S(1)} %get-tuple-element.10), channel_id=1, source_target_pairs={{0,1},{1,0},{2,3},{3,2},{4,5},{5,4},{6,7},{7,6},{8,9},{9,8},{10,11... | collective-permute-start | bytes 67592 | tf_op jit(solution)/shard_map/ppermute | solution.py:317
  4.7 2.6 %collective-permute-start.1 = (s32[4,1408]{1,0:T(4,128)S(1)}, s32[4,1408]{1,0:T(4,128)S(1)}, u32[]{:S(2)}, u32[]{:S(2)}) collective-permute-start(s32[4,1408]{1,0:T(4,128)S(1)} %get-tuple-element.11), channel_id=1, source_target_pairs={{0,2},{1,3},{2,0},{3,1},{4,6},{5,7},{6,4},{7,5},{8,10},{9,11},{10,... | collective-permute-start | bytes 67592 | tf_op jit(solution)/shard_map/ppermute | solution.py:317
  7.3 0.1 collective-permute-start.2
  7.3 0.0 collective-permute-done.refs_1_
  7.3 1.7 %collective-permute-done.1.refs_2_ = s32[4,1408]{1,0:T(4,128)S(1)} collective-permute-done((s32[4,1408]{1,0:T(4,128)S(1)}, s32[4,1408]{1,0:T(4,128)S(1)}, u32[]{:S(2)}, u32[]{:S(2)}) %collective-permute-start.1) | collective-permute-done | bytes 22560 | tf_op jit(solution)/shard_map/ppermute | solution.py:317
  9.0 1.4 %collective-permute-done.2.refs_3_ = s32[4,1408]{1,0:T(4,128)S(1)} collective-permute-done((s32[4,1408]{1,0:T(4,128)S(1)}, s32[4,1408]{1,0:T(4,128)S(1)}, u32[]{:S(2)}, u32[]{:S(2)}) %collective-permute-start.2) | collective-permute-done | bytes 22560 | tf_op jit(solution)/shard_map/ppermute | solution.py:317
  10.5 0.2 %combine.1.rest_0_ = s32[4,1408]{1,0:T(4,128)S(1)} custom-call(f32[4,2560]{1,0:T(4,128)S(1)} %get-tuple-element.9.refs_0_, s32[4,1408]{1,0:T(4,128)S(1)} %collective-permute-done.refs_1_, s32[4,1408]{1,0:T(4,128)S(1)} %collective-permute-done.1.refs_2_, s32[4,1408]{1,0:T(4,128)S(1)} %collective-permute-done.2.refs_3_), custom_call_target="tpu_custom_call" | custom-call | tf_op jit(solution)/shard_map/combine/pallas_call | solution.py:360
  10.7 3.7 %collective-permute-start.3 = (s32[4,1408]{1,0:T(4,128)S(1)}, s32[4,1408]{1,0:T(4,128)S(1)}, u32[]{:S(2)}, u32[]{:S(2)}) collective-permute-start(s32[4,1408]{1,0:T(4,128)S(1)} %combine.1.rest_0_), channel_id=1, source_target_pairs={{0,12},{4,8},{8,4},{12,0},{1,13},{5,9},{9,5},{13,1},{2,14},{6,10},... | collective-permute-start | bytes 67592 | tf_op jit(solution)/shard_map/ppermute | solution.py:317
  14.4 0.0 collective-permute-start.4
  14.4 0.8 %collective-permute-start.5 = (s32[4,1408]{1,0:T(4,128)S(1)}, s32[4,1408]{1,0:T(4,128)S(1)}, u32[]{:S(2)}, u32[]{:S(2)}) collective-permute-start(s32[4,1408]{1,0:T(4,128)S(1)} %combine.1.rest_0_), channel_id=1, source_target_pairs={{0,8},{4,12},{8,0},{12,4},{1,9},{5,13},{9,1},{13,5},{2,10},{6,14},... | collective-permute-start | bytes 67592 | tf_op jit(solution)/shard_map/ppermute | solution.py:317
  15.2 1.2 %collective-permute-done.3.rest_1_ = s32[4,1408]{1,0:T(4,128)S(1)} collective-permute-done((s32[4,1408]{1,0:T(4,128)S(1)}, s32[4,1408]{1,0:T(4,128)S(1)}, u32[]{:S(2)}, u32[]{:S(2)}) %collective-permute-start.3) | collective-permute-done | bytes 22560 | tf_op jit(solution)/shard_map/ppermute | solution.py:317
  16.4 0.0 copy-done
  16.4 0.0 copy-done.1
  16.4 0.0 copy-done.2
  16.4 1.1 %accumulate.3.old_ref = f32[1,16,2560]{2,1,0:T(8,128)S(1)} custom-call(f32[1,4]{1,0:T(1,128)S(1)} %bitcast.1, s32[16,2560]{1,0:T(8,128)S(1)} %copy-done, f32[1,16,2560]{2,1,0:T(8,128)S(1)} %copy-done.1, s32[4,1408]{1,0:T(4,128)S(1)} %combine.1.rest_0_, s32[4,1408]{1,0:T(4,128)S(1)} %collective-permute-done.3.rest_1_), custom_call_target="tpu_custom_call" | custom-call | flops 81920000 | bytes 491520 | tf_op jit(solution)/shard_map/accumulate/pallas_call | solution.py:383
  17.5 0.8 %collective-permute-done.4.rest_0_ = s32[4,1408]{1,0:T(4,128)S(1)} collective-permute-done((s32[4,1408]{1,0:T(4,128)S(1)}, s32[4,1408]{1,0:T(4,128)S(1)}, u32[]{:S(2)}, u32[]{:S(2)}) %collective-permute-start.4) | collective-permute-done | bytes 22560 | tf_op jit(solution)/shard_map/ppermute | solution.py:317
  18.2 0.7 %accumulate.4.old_ref = f32[1,16,2560]{2,1,0:T(8,128)S(1)} custom-call(f32[1,4]{1,0:T(1,128)S(1)} %bitcast.2, s32[16,2560]{1,0:T(8,128)S(1)} %copy-done, f32[1,16,2560]{2,1,0:T(8,128)S(1)} %accumulate.3.old_ref, s32[4,1408]{1,0:T(4,128)S(1)} %collective-permute-done.4.rest_0_), custom_call_target="tpu_custom_call" | custom-call | flops 40960000 | bytes 491520 | tf_op jit(solution)/shard_map/accumulate/pallas_call | solution.py:383
  18.9 0.4 %collective-permute-done.5.rest_0_ = s32[4,1408]{1,0:T(4,128)S(1)} collective-permute-done((s32[4,1408]{1,0:T(4,128)S(1)}, s32[4,1408]{1,0:T(4,128)S(1)}, u32[]{:S(2)}, u32[]{:S(2)}) %collective-permute-start.5) | collective-permute-done | bytes 22560 | tf_op jit(solution)/shard_map/ppermute | solution.py:317
  19.3 1.3 %accumulate.5 = f32[1,16,2560]{2,1,0:T(8,128)} custom-call(f32[1,4]{1,0:T(1,128)S(1)} %bitcast.3, s32[16,2560]{1,0:T(8,128)S(1)} %copy-done, f32[1,16,2560]{2,1,0:T(8,128)S(1)} %accumulate.4.old_ref, s32[4,1408]{1,0:T(4,128)S(1)} %collective-permute-done.5.rest_0_), custom_call_target="tpu_custom_call" | custom-call | flops 40960000 | bytes 491520 | tf_op jit(solution)/shard_map/accumulate/pallas_call | solution.py:383
Async XLA Ops:
  0.0 16.4 %copy-start = (s32[16,2560]{1,0:T(8,128)S(1)}, s32[16,2560]{1,0:T(8,128)}, u32[]{:S(2)}) copy-start(s32[16,2560]{1,0:T(8,128)} %transfer_ref.5) | copy-start | bytes 491524
  0.0 16.4 %copy-start.1 = (f32[1,16,2560]{2,1,0:T(8,128)S(1)}, f32[1,16,2560]{2,1,0:T(8,128)}, u32[]{:S(2)}) copy-start(f32[1,16,2560]{2,1,0:T(8,128)} %old_ref.1) | copy-start | bytes 491524
  0.0 16.4 %copy-start.2 = (f32[4]{0:T(128)S(1)}, f32[4]{0:T(128)}, u32[]{:S(2)}) copy-start(f32[4]{0:T(128)} %param.7) | copy-start | bytes 52
  4.2 3.2 %collective-permute-start = (s32[4,1408]{1,0:T(4,128)S(1)}, s32[4,1408]{1,0:T(4,128)S(1)}, u32[]{:S(2)}, u32[]{:S(2)}) collective-permute-start(s32[4,1408]{1,0:T(4,128)S(1)} %get-tuple-element.10), channel_id=1, source_target_pairs={{0,1},{1,0},{2,3},{3,2},{4,5},{5,4},{6,7},{7,6},{8,9},{9,8},{10,11... | collective-permute-start | bytes 67592 | tf_op jit(solution)/shard_map/ppermute | solution.py:317
  4.7 4.3 %collective-permute-start.1 = (s32[4,1408]{1,0:T(4,128)S(1)}, s32[4,1408]{1,0:T(4,128)S(1)}, u32[]{:S(2)}, u32[]{:S(2)}) collective-permute-start(s32[4,1408]{1,0:T(4,128)S(1)} %get-tuple-element.11), channel_id=1, source_target_pairs={{0,2},{1,3},{2,0},{3,1},{4,6},{5,7},{6,4},{7,5},{8,10},{9,11},{10,... | collective-permute-start | bytes 67592 | tf_op jit(solution)/shard_map/ppermute | solution.py:317
  7.3 3.2 %collective-permute-start.2 = (s32[4,1408]{1,0:T(4,128)S(1)}, s32[4,1408]{1,0:T(4,128)S(1)}, u32[]{:S(2)}, u32[]{:S(2)}) collective-permute-start(s32[4,1408]{1,0:T(4,128)S(1)} %get-tuple-element.12), channel_id=1, source_target_pairs={{0,3},{1,2},{2,1},{3,0},{4,7},{5,6},{6,5},{7,4},{8,11},{9,10},{10,... | collective-permute-start | bytes 67592 | tf_op jit(solution)/shard_map/ppermute | solution.py:317
  10.7 5.7 %collective-permute-start.3 = (s32[4,1408]{1,0:T(4,128)S(1)}, s32[4,1408]{1,0:T(4,128)S(1)}, u32[]{:S(2)}, u32[]{:S(2)}) collective-permute-start(s32[4,1408]{1,0:T(4,128)S(1)} %combine.1.rest_0_), channel_id=1, source_target_pairs={{0,12},{4,8},{8,4},{12,0},{1,13},{5,9},{9,5},{13,1},{2,14},{6,10},... | collective-permute-start | bytes 67592 | tf_op jit(solution)/shard_map/ppermute | solution.py:317
  14.4 3.9 %collective-permute-start.4 = (s32[4,1408]{1,0:T(4,128)S(1)}, s32[4,1408]{1,0:T(4,128)S(1)}, u32[]{:S(2)}, u32[]{:S(2)}) collective-permute-start(s32[4,1408]{1,0:T(4,128)S(1)} %combine.1.rest_0_), channel_id=1, source_target_pairs={{0,4},{4,0},{8,12},{12,8},{1,5},{5,1},{9,13},{13,9},{2,6},{6,2},{1... | collective-permute-start | bytes 67592 | tf_op jit(solution)/shard_map/ppermute | solution.py:317
  14.4 4.9 %collective-permute-start.5 = (s32[4,1408]{1,0:T(4,128)S(1)}, s32[4,1408]{1,0:T(4,128)S(1)}, u32[]{:S(2)}, u32[]{:S(2)}) collective-permute-start(s32[4,1408]{1,0:T(4,128)S(1)} %combine.1.rest_0_), channel_id=1, source_target_pairs={{0,8},{4,12},{8,0},{12,4},{1,9},{5,13},{9,1},{13,5},{2,10},{6,14},... | collective-permute-start | bytes 67592 | tf_op jit(solution)/shard_map/ppermute | solution.py:317

commit v8 on v6

--- a/solution.py
+++ b/solution.py
@@ -187,8 +187,7 @@
     rows_each = blk_count * rows_own
     coded = encode(green)
     for place, sent_ref in enumerate(sent_refs):
-        rows = coded if place else green
-        sent_ref[...] = rows[place * rows_each : (place + 1) * rows_each]
+        sent_ref[...] = coded[place * rows_each : (place + 1) * rows_each]
 
 
 def combine_kernel(sizes, *refs):
@@ -196,8 +195,18 @@
     blk_index = lax.axis_index("blk")
     parts = walk_count * sub_count
     part_refs, whole_refs, row_ref = refs[:parts], refs[parts:-1], refs[-1]
-    total = part_refs[0][...] + sum(decode(part_ref[...]) for part_ref in part_refs[1:])
-    coded = encode(total)
+    half = part_refs[0].shape[1] - lanes
+
+    exponents = [part_ref[:, half:] for part_ref in part_refs]
+    exponent = functools.reduce(jnp.maximum, exponents) + (parts - 1).bit_length()
+    high, low = 0.5, 0.5
+    for part_ref, part_exponent in zip(part_refs, exponents):
+        scale = jnp.exp2((part_exponent - exponent).astype(jnp.float32))[:, :1]
+        words = part_ref[:, :half]
+        high += (words >> 16).astype(jnp.float32) * scale
+        low += ((words << 16) >> 16).astype(jnp.float32) * scale
+    high, low = jnp.floor(high).astype(jnp.int32), jnp.floor(low).astype(jnp.int32)
+    coded = jnp.concatenate([(high << 16) | (low & 0xFFFF), exponent], axis=1)
     if len(whole_refs) == 1:
         whole_refs[0][...] = coded
         return
@@ -333,10 +342,8 @@
     coded = columns // 2 + lanes
     sent = pl.pallas_call(
         functools.partial(transform_kernel, sizes),
-        out_shape=[
-            jax.ShapeDtypeStruct((blk_count * rows_own, coded if place else columns), jnp.int32 if place else jnp.float32)
-            for place in range(walk_count * sub_count)
-        ],
+        out_shape=[jax.ShapeDtypeStruct((blk_count * rows_own, coded), jnp.int32)]
+        * (walk_count * sub_count),
         in_specs=[pl.BlockSpec(memory_space=pl.ANY)] * 2,
         out_specs=[vmem] * (walk_count * sub_count),
         scratch_shapes=[

time: 20.5 us -> 20.4 us (level)
  no operation moved by 1% of the time
where the time goes in v8:
time: 20.4 us; the launch traced here: 20.2 us
  starting transfers between devices  7.61 us (37%)
  Pallas kernels  7.02 us (34%)
  waiting for transfers between devices  5.55 us (27%)
    ppermute x6, starting transfers between devices, exchange(): arrived[i] = lax.ppermute(pieces[i], axes, route)  7.61 us
    ppermute x6, waiting for transfers between devices, exchange(): arrived[i] = lax.ppermute(pieces[i], axes, route)  5.55 us
    pallas_call x1, Pallas kernels, local(): pl.pallas_call(functools.partial(transform_kernel, sizes), out_shape=[jax...  3.84 us
    pallas_call x3, Pallas kernels, local(): pl.pallas_call(functools.partial(accumulate_kernel, sizes, places, last),...  3.07 us
  transfers between devices with their start and end apart: 6, of which 5 were waited for; matrix products, arithmetic and copies ran while one was open for 0% of the time, Pallas kernels for 9%

profile of v8, /device:TPU:0, one launch (start us, length us, event | category | flops | bytes accessed | tf_op | source)
XLA Modules:
  0.0 20.2 jit_solution(13561531185045354836)
XLA Ops:
  0.0 0.0 copy-start
  0.0 0.0 copy-start.1
  0.0 0.0 copy-start.2
  0.0 3.8 %transform.1 = (s32[4,1408]{1,0:T(4,128)S(1)}, s32[4,1408]{1,0:T(4,128)S(1)}, s32[4,1408]{1,0:T(4,128)S(1)}, s32[4,1408]{1,0:T(4,128)S(1)}) custom-call(bf16[1,1024,2048]{2,1,0:T(8,128)(2,1)} %matrix_hbm.1, s32[1,2048]{1,0:T(1,128)} %vertex_hbm.1), custom_call_target="tpu_custom_call" | custom-call | tf_op jit(solution)/shard_map/transform/pallas_call | solution.py:343
  3.9 0.5 %collective-permute-start = (s32[4,1408]{1,0:T(4,128)S(1)}, s32[4,1408]{1,0:T(4,128)S(1)}, u32[]{:S(2)}, u32[]{:S(2)}) collective-permute-start(s32[4,1408]{1,0:T(4,128)S(1)} %get-tuple-element.10), channel_id=1, source_target_pairs={{0,1},{1,0},{2,3},{3,2},{4,5},{5,4},{6,7},{7,6},{8,9},{9,8},{10,11... | collective-permute-start | bytes 67592 | tf_op jit(solution)/shard_map/ppermute | solution.py:326
  4.4 2.6 %collective-permute-start.1 = (s32[4,1408]{1,0:T(4,128)S(1)}, s32[4,1408]{1,0:T(4,128)S(1)}, u32[]{:S(2)}, u32[]{:S(2)}) collective-permute-start(s32[4,1408]{1,0:T(4,128)S(1)} %get-tuple-element.11), channel_id=1, source_target_pairs={{0,2},{1,3},{2,0},{3,1},{4,6},{5,7},{6,4},{7,5},{8,10},{9,11},{10,... | collective-permute-start | bytes 67592 | tf_op jit(solution)/shard_map/ppermute | solution.py:326
  6.9 0.1 collective-permute-start.2
  7.0 0.0 collective-permute-done.refs_1_
  7.0 1.7 %collective-permute-done.1.refs_2_ = s32[4,1408]{1,0:T(4,128)S(1)} collective-permute-done((s32[4,1408]{1,0:T(4,128)S(1)}, s32[4,1408]{1,0:T(4,128)S(1)}, u32[]{:S(2)}, u32[]{:S(2)}) %collective-permute-start.1) | collective-permute-done | bytes 22560 | tf_op jit(solution)/shard_map/ppermute | solution.py:326
  8.7 1.4 %collective-permute-done.2.refs_3_ = s32[4,1408]{1,0:T(4,128)S(1)} collective-permute-done((s32[4,1408]{1,0:T(4,128)S(1)}, s32[4,1408]{1,0:T(4,128)S(1)}, u32[]{:S(2)}, u32[]{:S(2)}) %collective-permute-start.2) | collective-permute-done | bytes 22560 | tf_op jit(solution)/shard_map/ppermute | solution.py:326
  10.2 0.1 combine.1.rest_0_
  10.3 3.7 %collective-permute-start.3 = (s32[4,1408]{1,0:T(4,128)S(1)}, s32[4,1408]{1,0:T(4,128)S(1)}, u32[]{:S(2)}, u32[]{:S(2)}) collective-permute-start(s32[4,1408]{1,0:T(4,128)S(1)} %combine.1.rest_0_), channel_id=1, source_target_pairs={{0,12},{4,8},{8,4},{12,0},{1,13},{5,9},{9,5},{13,1},{2,14},{6,10},... | collective-permute-start | bytes 67592 | tf_op jit(solution)/shard_map/ppermute | solution.py:326
  14.0 0.0 collective-permute-start.4
  14.0 0.8 %collective-permute-start.5 = (s32[4,1408]{1,0:T(4,128)S(1)}, s32[4,1408]{1,0:T(4,128)S(1)}, u32[]{:S(2)}, u32[]{:S(2)}) collective-permute-start(s32[4,1408]{1,0:T(4,128)S(1)} %combine.1.rest_0_), channel_id=1, source_target_pairs={{0,8},{4,12},{8,0},{12,4},{1,9},{5,13},{9,1},{13,5},{2,10},{6,14},... | collective-permute-start | bytes 67592 | tf_op jit(solution)/shard_map/ppermute | solution.py:326
  14.7 1.2 %collective-permute-done.3.rest_1_ = s32[4,1408]{1,0:T(4,128)S(1)} collective-permute-done((s32[4,1408]{1,0:T(4,128)S(1)}, s32[4,1408]{1,0:T(4,128)S(1)}, u32[]{:S(2)}, u32[]{:S(2)}) %collective-permute-start.3) | collective-permute-done | bytes 22560 | tf_op jit(solution)/shard_map/ppermute | solution.py:326
  16.0 0.0 copy-done
  16.0 0.0 copy-done.1
  16.0 0.0 copy-done.2
  16.0 1.1 %accumulate.3.old_ref = f32[1,16,2560]{2,1,0:T(8,128)S(1)} custom-call(f32[1,4]{1,0:T(1,128)S(1)} %bitcast.1, s32[16,2560]{1,0:T(8,128)S(1)} %copy-done, f32[1,16,2560]{2,1,0:T(8,128)S(1)} %copy-done.1, s32[4,1408]{1,0:T(4,128)S(1)} %combine.1.rest_0_, s32[4,1408]{1,0:T(4,128)S(1)} %collective-permute-done.3.rest_1_), custom_call_target="tpu_custom_call" | custom-call | flops 81920000 | bytes 491520 | tf_op jit(solution)/shard_map/accumulate/pallas_call | solution.py:390
  17.1 0.8 %collective-permute-done.4.rest_0_ = s32[4,1408]{1,0:T(4,128)S(1)} collective-permute-done((s32[4,1408]{1,0:T(4,128)S(1)}, s32[4,1408]{1,0:T(4,128)S(1)}, u32[]{:S(2)}, u32[]{:S(2)}) %collective-permute-start.4) | collective-permute-done | bytes 22560 | tf_op jit(solution)/shard_map/ppermute | solution.py:326
  17.8 0.7 %accumulate.4.old_ref = f32[1,16,2560]{2,1,0:T(8,128)S(1)} custom-call(f32[1,4]{1,0:T(1,128)S(1)} %bitcast.2, s32[16,2560]{1,0:T(8,128)S(1)} %copy-done, f32[1,16,2560]{2,1,0:T(8,128)S(1)} %accumulate.3.old_ref, s32[4,1408]{1,0:T(4,128)S(1)} %collective-permute-done.4.rest_0_), custom_call_target="tpu_custom_call" | custom-call | flops 40960000 | bytes 491520 | tf_op jit(solution)/shard_map/accumulate/pallas_call | solution.py:390
  18.5 0.4 %collective-permute-done.5.rest_0_ = s32[4,1408]{1,0:T(4,128)S(1)} collective-permute-done((s32[4,1408]{1,0:T(4,128)S(1)}, s32[4,1408]{1,0:T(4,128)S(1)}, u32[]{:S(2)}, u32[]{:S(2)}) %collective-permute-start.5) | collective-permute-done | bytes 22560 | tf_op jit(solution)/shard_map/ppermute | solution.py:326
  18.9 1.3 %accumulate.5 = f32[1,16,2560]{2,1,0:T(8,128)} custom-call(f32[1,4]{1,0:T(1,128)S(1)} %bitcast.3, s32[16,2560]{1,0:T(8,128)S(1)} %copy-done, f32[1,16,2560]{2,1,0:T(8,128)S(1)} %accumulate.4.old_ref, s32[4,1408]{1,0:T(4,128)S(1)} %collective-permute-done.5.rest_0_), custom_call_target="tpu_custom_call" | custom-call | flops 40960000 | bytes 491520 | tf_op jit(solution)/shard_map/accumulate/pallas_call | solution.py:390
Async XLA Ops:
  0.0 16.0 %copy-start = (s32[16,2560]{1,0:T(8,128)S(1)}, s32[16,2560]{1,0:T(8,128)}, u32[]{:S(2)}) copy-start(s32[16,2560]{1,0:T(8,128)} %transfer_ref.5) | copy-start | bytes 491524
  0.0 16.0 %copy-start.1 = (f32[1,16,2560]{2,1,0:T(8,128)S(1)}, f32[1,16,2560]{2,1,0:T(8,128)}, u32[]{:S(2)}) copy-start(f32[1,16,2560]{2,1,0:T(8,128)} %old_ref.1) | copy-start | bytes 491524
  0.0 16.0 %copy-start.2 = (f32[4]{0:T(128)S(1)}, f32[4]{0:T(128)}, u32[]{:S(2)}) copy-start(f32[4]{0:T(128)} %param.7) | copy-start | bytes 52
  3.9 3.2 %collective-permute-start = (s32[4,1408]{1,0:T(4,128)S(1)}, s32[4,1408]{1,0:T(4,128)S(1)}, u32[]{:S(2)}, u32[]{:S(2)}) collective-permute-start(s32[4,1408]{1,0:T(4,128)S(1)} %get-tuple-element.10), channel_id=1, source_target_pairs={{0,1},{1,0},{2,3},{3,2},{4,5},{5,4},{6,7},{7,6},{8,9},{9,8},{10,11... | collective-permute-start | bytes 67592 | tf_op jit(solution)/shard_map/ppermute | solution.py:326
  4.4 4.3 %collective-permute-start.1 = (s32[4,1408]{1,0:T(4,128)S(1)}, s32[4,1408]{1,0:T(4,128)S(1)}, u32[]{:S(2)}, u32[]{:S(2)}) collective-permute-start(s32[4,1408]{1,0:T(4,128)S(1)} %get-tuple-element.11), channel_id=1, source_target_pairs={{0,2},{1,3},{2,0},{3,1},{4,6},{5,7},{6,4},{7,5},{8,10},{9,11},{10,... | collective-permute-start | bytes 67592 | tf_op jit(solution)/shard_map/ppermute | solution.py:326
  6.9 3.2 %collective-permute-start.2 = (s32[4,1408]{1,0:T(4,128)S(1)}, s32[4,1408]{1,0:T(4,128)S(1)}, u32[]{:S(2)}, u32[]{:S(2)}) collective-permute-start(s32[4,1408]{1,0:T(4,128)S(1)} %get-tuple-element.12), channel_id=1, source_target_pairs={{0,3},{1,2},{2,1},{3,0},{4,7},{5,6},{6,5},{7,4},{8,11},{9,10},{10,... | collective-permute-start | bytes 67592 | tf_op jit(solution)/shard_map/ppermute | solution.py:326
  10.3 5.7 %collective-permute-start.3 = (s32[4,1408]{1,0:T(4,128)S(1)}, s32[4,1408]{1,0:T(4,128)S(1)}, u32[]{:S(2)}, u32[]{:S(2)}) collective-permute-start(s32[4,1408]{1,0:T(4,128)S(1)} %combine.1.rest_0_), channel_id=1, source_target_pairs={{0,12},{4,8},{8,4},{12,0},{1,13},{5,9},{9,5},{13,1},{2,14},{6,10},... | collective-permute-start | bytes 67592 | tf_op jit(solution)/shard_map/ppermute | solution.py:326
  14.0 3.9 %collective-permute-start.4 = (s32[4,1408]{1,0:T(4,128)S(1)}, s32[4,1408]{1,0:T(4,128)S(1)}, u32[]{:S(2)}, u32[]{:S(2)}) collective-permute-start(s32[4,1408]{1,0:T(4,128)S(1)} %combine.1.rest_0_), channel_id=1, source_target_pairs={{0,4},{4,0},{8,12},{12,8},{1,5},{5,1},{9,13},{13,9},{2,6},{6,2},{1... | collective-permute-start | bytes 67592 | tf_op jit(solution)/shard_map/ppermute | solution.py:326
  14.0 4.9 %collective-permute-start.5 = (s32[4,1408]{1,0:T(4,128)S(1)}, s32[4,1408]{1,0:T(4,128)S(1)}, u32[]{:S(2)}, u32[]{:S(2)}) collective-permute-start(s32[4,1408]{1,0:T(4,128)S(1)} %combine.1.rest_0_), channel_id=1, source_target_pairs={{0,8},{4,12},{8,0},{12,4},{1,9},{5,13},{9,1},{13,5},{2,10},{6,14},... | collective-permute-start | bytes 67592 | tf_op jit(solution)/shard_map/ppermute | solution.py:326

commit v9 on v8

--- a/solution.py
+++ b/solution.py
@@ -124,7 +124,7 @@
 
 
 def transform_kernel(sizes, matrix_hbm, vertex_hbm, *rest):
-    *sent_refs, matrix_ref, vertex_ref, left_ref, early_ref, middle_ref, late_ref, weight_ref, matrix_sem, vertex_sem = rest
+    *sent_refs, matrix_ref, vertex_ref, left_ref, early_ref, late_ref, weight_ref, matrix_sem, vertex_sem = rest
     blk_count, walk_count, sub_count, rows_own = sizes
     walk_index = lax.axis_index("walk")
     sub_index = lax.axis_index("sub")
@@ -170,7 +170,7 @@
             left_product - high.astype(jnp.float32)
         ).astype(jnp.bfloat16)
     green, start = 0.0, 0
-    for table_ref in (early_ref, middle_ref, late_ref):
+    for table_ref in (early_ref, late_ref):
         size = table_ref.shape[1]
         if table_ref is not early_ref:
             for tile in range(0, size, lanes):
@@ -337,8 +337,7 @@
     sizes = (blk_count, walk_count, sub_count, rows_own)
     vmem = pl.BlockSpec(memory_space=pltpu.VMEM)
     vertices_local = vertices // sub_count
-    early = vertices_local // (4 * lanes) * 2 * lanes
-    middle = early // 2
+    early = 3 * vertices_local // (8 * lanes) * 2 * lanes
     coded = columns // 2 + lanes
     sent = pl.pallas_call(
         functools.partial(transform_kernel, sizes),
@@ -351,8 +350,7 @@
             pltpu.VMEM((1, vertices), jnp.int32),
             pltpu.VMEM((devices * rows_own, rows_local), jnp.bfloat16),
             pltpu.VMEM((columns, early), jnp.bfloat16),
-            pltpu.VMEM((columns, middle), jnp.bfloat16),
-            pltpu.VMEM((columns, vertices_local - early - middle), jnp.bfloat16),
+            pltpu.VMEM((columns, vertices_local - early), jnp.bfloat16),
             pltpu.VMEM((2 * devices * rows_own, vertices_local), jnp.bfloat16),
             pltpu.SemaphoreType.DMA,
             pltpu.SemaphoreType.DMA,

time: 20.4 us -> 20.7 us (1.015)
  Pallas kernels: 7.02 us -> 7.37 us
    pallas_call x1, Pallas kernels: 3.84 us -> 4.19 us  [local(): pl.pallas_call(functools.partial(transform_kernel, sizes), out_shape=[jax...]
where the time goes in v9:
time: 20.7 us; the launch traced here: 20.6 us
  starting transfers between devices  7.61 us (37%)
  Pallas kernels  7.37 us (36%)
  waiting for transfers between devices  5.55 us (27%)
    ppermute x6, starting transfers between devices, exchange(): arrived[i] = lax.ppermute(pieces[i], axes, route)  7.61 us
    ppermute x6, waiting for transfers between devices, exchange(): arrived[i] = lax.ppermute(pieces[i], axes, route)  5.55 us
    pallas_call x1, Pallas kernels, local(): pl.pallas_call(functools.partial(transform_kernel, sizes), out_shape=[jax...  4.19 us
    pallas_call x3, Pallas kernels, local(): pl.pallas_call(functools.partial(accumulate_kernel, sizes, places, last),...  3.07 us
  transfers between devices with their start and end apart: 6, of which 5 were waited for; matrix products, arithmetic and copies ran while one was open for 0% of the time, Pallas kernels for 9%

profile of v9, /device:TPU:0, one launch (start us, length us, event | category | flops | bytes accessed | tf_op | source)
XLA Modules:
  0.0 20.6 jit_solution(15789156367053743507)
XLA Ops:
  0.0 0.0 copy-start
  0.0 0.0 copy-start.1
  0.0 0.0 copy-start.2
  0.0 4.2 %transform.1 = (s32[4,1408]{1,0:T(4,128)S(1)}, s32[4,1408]{1,0:T(4,128)S(1)}, s32[4,1408]{1,0:T(4,128)S(1)}, s32[4,1408]{1,0:T(4,128)S(1)}) custom-call(bf16[1,1024,2048]{2,1,0:T(8,128)(2,1)} %matrix_hbm.1, s32[1,2048]{1,0:T(1,128)} %vertex_hbm.1), custom_call_target="tpu_custom_call" | custom-call | tf_op jit(solution)/shard_map/transform/pallas_call | solution.py:342
  4.2 0.5 %collective-permute-start = (s32[4,1408]{1,0:T(4,128)S(1)}, s32[4,1408]{1,0:T(4,128)S(1)}, u32[]{:S(2)}, u32[]{:S(2)}) collective-permute-start(s32[4,1408]{1,0:T(4,128)S(1)} %get-tuple-element.10), channel_id=1, source_target_pairs={{0,1},{1,0},{2,3},{3,2},{4,5},{5,4},{6,7},{7,6},{8,9},{9,8},{10,11... | collective-permute-start | bytes 67592 | tf_op jit(solution)/shard_map/ppermute | solution.py:326
  4.7 2.6 %collective-permute-start.1 = (s32[4,1408]{1,0:T(4,128)S(1)}, s32[4,1408]{1,0:T(4,128)S(1)}, u32[]{:S(2)}, u32[]{:S(2)}) collective-permute-start(s32[4,1408]{1,0:T(4,128)S(1)} %get-tuple-element.11), channel_id=1, source_target_pairs={{0,2},{1,3},{2,0},{3,1},{4,6},{5,7},{6,4},{7,5},{8,10},{9,11},{10,... | collective-permute-start | bytes 67592 | tf_op jit(solution)/shard_map/ppermute | solution.py:326
  7.3 0.1 collective-permute-start.2
  7.4 0.0 collective-permute-done.refs_1_
  7.4 1.7 %collective-permute-done.1.refs_2_ = s32[4,1408]{1,0:T(4,128)S(1)} collective-permute-done((s32[4,1408]{1,0:T(4,128)S(1)}, s32[4,1408]{1,0:T(4,128)S(1)}, u32[]{:S(2)}, u32[]{:S(2)}) %collective-permute-start.1) | collective-permute-done | bytes 22560 | tf_op jit(solution)/shard_map/ppermute | solution.py:326
  9.1 1.4 %collective-permute-done.2.refs_3_ = s32[4,1408]{1,0:T(4,128)S(1)} collective-permute-done((s32[4,1408]{1,0:T(4,128)S(1)}, s32[4,1408]{1,0:T(4,128)S(1)}, u32[]{:S(2)}, u32[]{:S(2)}) %collective-permute-start.2) | collective-permute-done | bytes 22560 | tf_op jit(solution)/shard_map/ppermute | solution.py:326
  10.5 0.1 combine.1.rest_0_
  10.6 3.7 %collective-permute-start.3 = (s32[4,1408]{1,0:T(4,128)S(1)}, s32[4,1408]{1,0:T(4,128)S(1)}, u32[]{:S(2)}, u32[]{:S(2)}) collective-permute-start(s32[4,1408]{1,0:T(4,128)S(1)} %combine.1.rest_0_), channel_id=1, source_target_pairs={{0,12},{4,8},{8,4},{12,0},{1,13},{5,9},{9,5},{13,1},{2,14},{6,10},... | collective-permute-start | bytes 67592 | tf_op jit(solution)/shard_map/ppermute | solution.py:326
  14.3 0.0 collective-permute-start.4
  14.3 0.8 %collective-permute-start.5 = (s32[4,1408]{1,0:T(4,128)S(1)}, s32[4,1408]{1,0:T(4,128)S(1)}, u32[]{:S(2)}, u32[]{:S(2)}) collective-permute-start(s32[4,1408]{1,0:T(4,128)S(1)} %combine.1.rest_0_), channel_id=1, source_target_pairs={{0,8},{4,12},{8,0},{12,4},{1,9},{5,13},{9,1},{13,5},{2,10},{6,14},... | collective-permute-start | bytes 67592 | tf_op jit(solution)/shard_map/ppermute | solution.py:326
  15.1 1.2 %collective-permute-done.3.rest_1_ = s32[4,1408]{1,0:T(4,128)S(1)} collective-permute-done((s32[4,1408]{1,0:T(4,128)S(1)}, s32[4,1408]{1,0:T(4,128)S(1)}, u32[]{:S(2)}, u32[]{:S(2)}) %collective-permute-start.3) | collective-permute-done | bytes 22560 | tf_op jit(solution)/shard_map/ppermute | solution.py:326
  16.3 0.0 copy-done
  16.3 0.0 copy-done.1
  16.3 0.0 copy-done.2
  16.3 1.1 %accumulate.3.old_ref = f32[1,16,2560]{2,1,0:T(8,128)S(1)} custom-call(f32[1,4]{1,0:T(1,128)S(1)} %bitcast.1, s32[16,2560]{1,0:T(8,128)S(1)} %copy-done, f32[1,16,2560]{2,1,0:T(8,128)S(1)} %copy-done.1, s32[4,1408]{1,0:T(4,128)S(1)} %combine.1.rest_0_, s32[4,1408]{1,0:T(4,128)S(1)} %collective-permute-done.3.rest_1_), custom_call_target="tpu_custom_call" | custom-call | flops 81920000 | bytes 491520 | tf_op jit(solution)/shard_map/accumulate/pallas_call | solution.py:388
  17.4 0.8 %collective-permute-done.4.rest_0_ = s32[4,1408]{1,0:T(4,128)S(1)} collective-permute-done((s32[4,1408]{1,0:T(4,128)S(1)}, s32[4,1408]{1,0:T(4,128)S(1)}, u32[]{:S(2)}, u32[]{:S(2)}) %collective-permute-start.4) | collective-permute-done | bytes 22560 | tf_op jit(solution)/shard_map/ppermute | solution.py:326
  18.2 0.7 %accumulate.4.old_ref = f32[1,16,2560]{2,1,0:T(8,128)S(1)} custom-call(f32[1,4]{1,0:T(1,128)S(1)} %bitcast.2, s32[16,2560]{1,0:T(8,128)S(1)} %copy-done, f32[1,16,2560]{2,1,0:T(8,128)S(1)} %accumulate.3.old_ref, s32[4,1408]{1,0:T(4,128)S(1)} %collective-permute-done.4.rest_0_), custom_call_target="tpu_custom_call" | custom-call | flops 40960000 | bytes 491520 | tf_op jit(solution)/shard_map/accumulate/pallas_call | solution.py:388
  18.8 0.4 %collective-permute-done.5.rest_0_ = s32[4,1408]{1,0:T(4,128)S(1)} collective-permute-done((s32[4,1408]{1,0:T(4,128)S(1)}, s32[4,1408]{1,0:T(4,128)S(1)}, u32[]{:S(2)}, u32[]{:S(2)}) %collective-permute-start.5) | collective-permute-done | bytes 22560 | tf_op jit(solution)/shard_map/ppermute | solution.py:326
  19.2 1.3 %accumulate.5 = f32[1,16,2560]{2,1,0:T(8,128)} custom-call(f32[1,4]{1,0:T(1,128)S(1)} %bitcast.3, s32[16,2560]{1,0:T(8,128)S(1)} %copy-done, f32[1,16,2560]{2,1,0:T(8,128)S(1)} %accumulate.4.old_ref, s32[4,1408]{1,0:T(4,128)S(1)} %collective-permute-done.5.rest_0_), custom_call_target="tpu_custom_call" | custom-call | flops 40960000 | bytes 491520 | tf_op jit(solution)/shard_map/accumulate/pallas_call | solution.py:388
Async XLA Ops:
  0.0 16.3 %copy-start = (s32[16,2560]{1,0:T(8,128)S(1)}, s32[16,2560]{1,0:T(8,128)}, u32[]{:S(2)}) copy-start(s32[16,2560]{1,0:T(8,128)} %transfer_ref.5) | copy-start | bytes 491524
  0.0 16.3 %copy-start.1 = (f32[1,16,2560]{2,1,0:T(8,128)S(1)}, f32[1,16,2560]{2,1,0:T(8,128)}, u32[]{:S(2)}) copy-start(f32[1,16,2560]{2,1,0:T(8,128)} %old_ref.1) | copy-start | bytes 491524
  0.0 16.3 %copy-start.2 = (f32[4]{0:T(128)S(1)}, f32[4]{0:T(128)}, u32[]{:S(2)}) copy-start(f32[4]{0:T(128)} %param.7) | copy-start | bytes 52
  4.2 3.2 %collective-permute-start = (s32[4,1408]{1,0:T(4,128)S(1)}, s32[4,1408]{1,0:T(4,128)S(1)}, u32[]{:S(2)}, u32[]{:S(2)}) collective-permute-start(s32[4,1408]{1,0:T(4,128)S(1)} %get-tuple-element.10), channel_id=1, source_target_pairs={{0,1},{1,0},{2,3},{3,2},{4,5},{5,4},{6,7},{7,6},{8,9},{9,8},{10,11... | collective-permute-start | bytes 67592 | tf_op jit(solution)/shard_map/ppermute | solution.py:326
  4.7 4.3 %collective-permute-start.1 = (s32[4,1408]{1,0:T(4,128)S(1)}, s32[4,1408]{1,0:T(4,128)S(1)}, u32[]{:S(2)}, u32[]{:S(2)}) collective-permute-start(s32[4,1408]{1,0:T(4,128)S(1)} %get-tuple-element.11), channel_id=1, source_target_pairs={{0,2},{1,3},{2,0},{3,1},{4,6},{5,7},{6,4},{7,5},{8,10},{9,11},{10,... | collective-permute-start | bytes 67592 | tf_op jit(solution)/shard_map/ppermute | solution.py:326
  7.3 3.2 %collective-permute-start.2 = (s32[4,1408]{1,0:T(4,128)S(1)}, s32[4,1408]{1,0:T(4,128)S(1)}, u32[]{:S(2)}, u32[]{:S(2)}) collective-permute-start(s32[4,1408]{1,0:T(4,128)S(1)} %get-tuple-element.12), channel_id=1, source_target_pairs={{0,3},{1,2},{2,1},{3,0},{4,7},{5,6},{6,5},{7,4},{8,11},{9,10},{10,... | collective-permute-start | bytes 67592 | tf_op jit(solution)/shard_map/ppermute | solution.py:326
  10.6 5.7 %collective-permute-start.3 = (s32[4,1408]{1,0:T(4,128)S(1)}, s32[4,1408]{1,0:T(4,128)S(1)}, u32[]{:S(2)}, u32[]{:S(2)}) collective-permute-start(s32[4,1408]{1,0:T(4,128)S(1)} %combine.1.rest_0_), channel_id=1, source_target_pairs={{0,12},{4,8},{8,4},{12,0},{1,13},{5,9},{9,5},{13,1},{2,14},{6,10},... | collective-permute-start | bytes 67592 | tf_op jit(solution)/shard_map/ppermute | solution.py:326
  14.3 3.9 %collective-permute-start.4 = (s32[4,1408]{1,0:T(4,128)S(1)}, s32[4,1408]{1,0:T(4,128)S(1)}, u32[]{:S(2)}, u32[]{:S(2)}) collective-permute-start(s32[4,1408]{1,0:T(4,128)S(1)} %combine.1.rest_0_), channel_id=1, source_target_pairs={{0,4},{4,0},{8,12},{12,8},{1,5},{5,1},{9,13},{13,9},{2,6},{6,2},{1... | collective-permute-start | bytes 67592 | tf_op jit(solution)/shard_map/ppermute | solution.py:326
  14.3 4.9 %collective-permute-start.5 = (s32[4,1408]{1,0:T(4,128)S(1)}, s32[4,1408]{1,0:T(4,128)S(1)}, u32[]{:S(2)}, u32[]{:S(2)}) collective-permute-start(s32[4,1408]{1,0:T(4,128)S(1)} %combine.1.rest_0_), channel_id=1, source_target_pairs={{0,8},{4,12},{8,0},{12,4},{1,9},{5,13},{9,1},{13,5},{2,10},{6,14},... | collective-permute-start | bytes 67592 | tf_op jit(solution)/shard_map/ppermute | solution.py:326

commit v10 on v9

--- a/solution.py
+++ b/solution.py
@@ -337,7 +337,7 @@
     sizes = (blk_count, walk_count, sub_count, rows_own)
     vmem = pl.BlockSpec(memory_space=pltpu.VMEM)
     vertices_local = vertices // sub_count
-    early = 3 * vertices_local // (8 * lanes) * 2 * lanes
+    early = vertices_local // (4 * lanes) * 2 * lanes
     coded = columns // 2 + lanes
     sent = pl.pallas_call(
         functools.partial(transform_kernel, sizes),

time: 20.7 us -> 20.3 us (0.981)
  Pallas kernels: 7.37 us -> 7 us
    pallas_call x1, Pallas kernels: 4.19 us -> 3.82 us  [local(): pl.pallas_call(functools.partial(transform_kernel, sizes), out_shape=[jax...]
where the time goes in v10:
time: 20.3 us; the launch traced here: 20.2 us
  starting transfers between devices  7.61 us (37%)
  Pallas kernels  7 us (34%)
  waiting for transfers between devices  5.55 us (27%)
    ppermute x6, starting transfers between devices, exchange(): arrived[i] = lax.ppermute(pieces[i], axes, route)  7.61 us
    ppermute x6, waiting for transfers between devices, exchange(): arrived[i] = lax.ppermute(pieces[i], axes, route)  5.55 us
    pallas_call x1, Pallas kernels, local(): pl.pallas_call(functools.partial(transform_kernel, sizes), out_shape=[jax...  3.82 us
    pallas_call x3, Pallas kernels, local(): pl.pallas_call(functools.partial(accumulate_kernel, sizes, places, last),...  3.07 us
  transfers between devices with their start and end apart: 6, of which 5 were waited for; matrix products, arithmetic and copies ran while one was open for 0% of the time, Pallas kernels for 9%

profile of v10, /device:TPU:0, one launch (start us, length us, event | category | flops | bytes accessed | tf_op | source)
XLA Modules:
  0.0 20.2 jit_solution(16773816240351594929)
XLA Ops:
  0.0 0.0 copy-start
  0.0 0.0 copy-start.1
  0.0 0.0 copy-start.2
  0.0 3.8 %transform.1 = (s32[4,1408]{1,0:T(4,128)S(1)}, s32[4,1408]{1,0:T(4,128)S(1)}, s32[4,1408]{1,0:T(4,128)S(1)}, s32[4,1408]{1,0:T(4,128)S(1)}) custom-call(bf16[1,1024,2048]{2,1,0:T(8,128)(2,1)} %matrix_hbm.1, s32[1,2048]{1,0:T(1,128)} %vertex_hbm.1), custom_call_target="tpu_custom_call" | custom-call | tf_op jit(solution)/shard_map/transform/pallas_call | solution.py:342
  3.8 0.5 %collective-permute-start = (s32[4,1408]{1,0:T(4,128)S(1)}, s32[4,1408]{1,0:T(4,128)S(1)}, u32[]{:S(2)}, u32[]{:S(2)}) collective-permute-start(s32[4,1408]{1,0:T(4,128)S(1)} %get-tuple-element.10), channel_id=1, source_target_pairs={{0,1},{1,0},{2,3},{3,2},{4,5},{5,4},{6,7},{7,6},{8,9},{9,8},{10,11... | collective-permute-start | bytes 67592 | tf_op jit(solution)/shard_map/ppermute | solution.py:326
  4.4 2.6 %collective-permute-start.1 = (s32[4,1408]{1,0:T(4,128)S(1)}, s32[4,1408]{1,0:T(4,128)S(1)}, u32[]{:S(2)}, u32[]{:S(2)}) collective-permute-start(s32[4,1408]{1,0:T(4,128)S(1)} %get-tuple-element.11), channel_id=1, source_target_pairs={{0,2},{1,3},{2,0},{3,1},{4,6},{5,7},{6,4},{7,5},{8,10},{9,11},{10,... | collective-permute-start | bytes 67592 | tf_op jit(solution)/shard_map/ppermute | solution.py:326
  6.9 0.1 collective-permute-start.2
  7.0 0.0 collective-permute-done.refs_1_
  7.0 1.7 %collective-permute-done.1.refs_2_ = s32[4,1408]{1,0:T(4,128)S(1)} collective-permute-done((s32[4,1408]{1,0:T(4,128)S(1)}, s32[4,1408]{1,0:T(4,128)S(1)}, u32[]{:S(2)}, u32[]{:S(2)}) %collective-permute-start.1) | collective-permute-done | bytes 22560 | tf_op jit(solution)/shard_map/ppermute | solution.py:326
  8.7 1.4 %collective-permute-done.2.refs_3_ = s32[4,1408]{1,0:T(4,128)S(1)} collective-permute-done((s32[4,1408]{1,0:T(4,128)S(1)}, s32[4,1408]{1,0:T(4,128)S(1)}, u32[]{:S(2)}, u32[]{:S(2)}) %collective-permute-start.2) | collective-permute-done | bytes 22560 | tf_op jit(solution)/shard_map/ppermute | solution.py:326
  10.2 0.1 combine.1.rest_0_
  10.3 3.7 %collective-permute-start.3 = (s32[4,1408]{1,0:T(4,128)S(1)}, s32[4,1408]{1,0:T(4,128)S(1)}, u32[]{:S(2)}, u32[]{:S(2)}) collective-permute-start(s32[4,1408]{1,0:T(4,128)S(1)} %combine.1.rest_0_), channel_id=1, source_target_pairs={{0,12},{4,8},{8,4},{12,0},{1,13},{5,9},{9,5},{13,1},{2,14},{6,10},... | collective-permute-start | bytes 67592 | tf_op jit(solution)/shard_map/ppermute | solution.py:326
  13.9 0.0 collective-permute-start.4
  13.9 0.8 %collective-permute-start.5 = (s32[4,1408]{1,0:T(4,128)S(1)}, s32[4,1408]{1,0:T(4,128)S(1)}, u32[]{:S(2)}, u32[]{:S(2)}) collective-permute-start(s32[4,1408]{1,0:T(4,128)S(1)} %combine.1.rest_0_), channel_id=1, source_target_pairs={{0,8},{4,12},{8,0},{12,4},{1,9},{5,13},{9,1},{13,5},{2,10},{6,14},... | collective-permute-start | bytes 67592 | tf_op jit(solution)/shard_map/ppermute | solution.py:326
  14.7 1.2 %collective-permute-done.3.rest_1_ = s32[4,1408]{1,0:T(4,128)S(1)} collective-permute-done((s32[4,1408]{1,0:T(4,128)S(1)}, s32[4,1408]{1,0:T(4,128)S(1)}, u32[]{:S(2)}, u32[]{:S(2)}) %collective-permute-start.3) | collective-permute-done | bytes 22560 | tf_op jit(solution)/shard_map/ppermute | solution.py:326
  15.9 0.0 copy-done
  15.9 0.0 copy-done.1
  15.9 0.0 copy-done.2
  15.9 1.1 %accumulate.3.old_ref = f32[1,16,2560]{2,1,0:T(8,128)S(1)} custom-call(f32[1,4]{1,0:T(1,128)S(1)} %bitcast.1, s32[16,2560]{1,0:T(8,128)S(1)} %copy-done, f32[1,16,2560]{2,1,0:T(8,128)S(1)} %copy-done.1, s32[4,1408]{1,0:T(4,128)S(1)} %combine.1.rest_0_, s32[4,1408]{1,0:T(4,128)S(1)} %collective-permute-done.3.rest_1_), custom_call_target="tpu_custom_call" | custom-call | flops 81920000 | bytes 491520 | tf_op jit(solution)/shard_map/accumulate/pallas_call | solution.py:388
  17.0 0.8 %collective-permute-done.4.rest_0_ = s32[4,1408]{1,0:T(4,128)S(1)} collective-permute-done((s32[4,1408]{1,0:T(4,128)S(1)}, s32[4,1408]{1,0:T(4,128)S(1)}, u32[]{:S(2)}, u32[]{:S(2)}) %collective-permute-start.4) | collective-permute-done | bytes 22560 | tf_op jit(solution)/shard_map/ppermute | solution.py:326
  17.8 0.7 %accumulate.4.old_ref = f32[1,16,2560]{2,1,0:T(8,128)S(1)} custom-call(f32[1,4]{1,0:T(1,128)S(1)} %bitcast.2, s32[16,2560]{1,0:T(8,128)S(1)} %copy-done, f32[1,16,2560]{2,1,0:T(8,128)S(1)} %accumulate.3.old_ref, s32[4,1408]{1,0:T(4,128)S(1)} %collective-permute-done.4.rest_0_), custom_call_target="tpu_custom_call" | custom-call | flops 40960000 | bytes 491520 | tf_op jit(solution)/shard_map/accumulate/pallas_call | solution.py:388
  18.5 0.4 %collective-permute-done.5.rest_0_ = s32[4,1408]{1,0:T(4,128)S(1)} collective-permute-done((s32[4,1408]{1,0:T(4,128)S(1)}, s32[4,1408]{1,0:T(4,128)S(1)}, u32[]{:S(2)}, u32[]{:S(2)}) %collective-permute-start.5) | collective-permute-done | bytes 22560 | tf_op jit(solution)/shard_map/ppermute | solution.py:326
  18.9 1.3 %accumulate.5 = f32[1,16,2560]{2,1,0:T(8,128)} custom-call(f32[1,4]{1,0:T(1,128)S(1)} %bitcast.3, s32[16,2560]{1,0:T(8,128)S(1)} %copy-done, f32[1,16,2560]{2,1,0:T(8,128)S(1)} %accumulate.4.old_ref, s32[4,1408]{1,0:T(4,128)S(1)} %collective-permute-done.5.rest_0_), custom_call_target="tpu_custom_call" | custom-call | flops 40960000 | bytes 491520 | tf_op jit(solution)/shard_map/accumulate/pallas_call | solution.py:388
Async XLA Ops:
  0.0 15.9 %copy-start = (s32[16,2560]{1,0:T(8,128)S(1)}, s32[16,2560]{1,0:T(8,128)}, u32[]{:S(2)}) copy-start(s32[16,2560]{1,0:T(8,128)} %transfer_ref.5) | copy-start | bytes 491524
  0.0 15.9 %copy-start.1 = (f32[1,16,2560]{2,1,0:T(8,128)S(1)}, f32[1,16,2560]{2,1,0:T(8,128)}, u32[]{:S(2)}) copy-start(f32[1,16,2560]{2,1,0:T(8,128)} %old_ref.1) | copy-start | bytes 491524
  0.0 15.9 %copy-start.2 = (f32[4]{0:T(128)S(1)}, f32[4]{0:T(128)}, u32[]{:S(2)}) copy-start(f32[4]{0:T(128)} %param.7) | copy-start | bytes 52
  3.8 3.2 %collective-permute-start = (s32[4,1408]{1,0:T(4,128)S(1)}, s32[4,1408]{1,0:T(4,128)S(1)}, u32[]{:S(2)}, u32[]{:S(2)}) collective-permute-start(s32[4,1408]{1,0:T(4,128)S(1)} %get-tuple-element.10), channel_id=1, source_target_pairs={{0,1},{1,0},{2,3},{3,2},{4,5},{5,4},{6,7},{7,6},{8,9},{9,8},{10,11... | collective-permute-start | bytes 67592 | tf_op jit(solution)/shard_map/ppermute | solution.py:326
  4.4 4.3 %collective-permute-start.1 = (s32[4,1408]{1,0:T(4,128)S(1)}, s32[4,1408]{1,0:T(4,128)S(1)}, u32[]{:S(2)}, u32[]{:S(2)}) collective-permute-start(s32[4,1408]{1,0:T(4,128)S(1)} %get-tuple-element.11), channel_id=1, source_target_pairs={{0,2},{1,3},{2,0},{3,1},{4,6},{5,7},{6,4},{7,5},{8,10},{9,11},{10,... | collective-permute-start | bytes 67592 | tf_op jit(solution)/shard_map/ppermute | solution.py:326
  6.9 3.2 %collective-permute-start.2 = (s32[4,1408]{1,0:T(4,128)S(1)}, s32[4,1408]{1,0:T(4,128)S(1)}, u32[]{:S(2)}, u32[]{:S(2)}) collective-permute-start(s32[4,1408]{1,0:T(4,128)S(1)} %get-tuple-element.12), channel_id=1, source_target_pairs={{0,3},{1,2},{2,1},{3,0},{4,7},{5,6},{6,5},{7,4},{8,11},{9,10},{10,... | collective-permute-start | bytes 67592 | tf_op jit(solution)/shard_map/ppermute | solution.py:326
  10.3 5.7 %collective-permute-start.3 = (s32[4,1408]{1,0:T(4,128)S(1)}, s32[4,1408]{1,0:T(4,128)S(1)}, u32[]{:S(2)}, u32[]{:S(2)}) collective-permute-start(s32[4,1408]{1,0:T(4,128)S(1)} %combine.1.rest_0_), channel_id=1, source_target_pairs={{0,12},{4,8},{8,4},{12,0},{1,13},{5,9},{9,5},{13,1},{2,14},{6,10},... | collective-permute-start | bytes 67592 | tf_op jit(solution)/shard_map/ppermute | solution.py:326
  13.9 3.9 %collective-permute-start.4 = (s32[4,1408]{1,0:T(4,128)S(1)}, s32[4,1408]{1,0:T(4,128)S(1)}, u32[]{:S(2)}, u32[]{:S(2)}) collective-permute-start(s32[4,1408]{1,0:T(4,128)S(1)} %combine.1.rest_0_), channel_id=1, source_target_pairs={{0,4},{4,0},{8,12},{12,8},{1,5},{5,1},{9,13},{13,9},{2,6},{6,2},{1... | collective-permute-start | bytes 67592 | tf_op jit(solution)/shard_map/ppermute | solution.py:326
  13.9 4.9 %collective-permute-start.5 = (s32[4,1408]{1,0:T(4,128)S(1)}, s32[4,1408]{1,0:T(4,128)S(1)}, u32[]{:S(2)}, u32[]{:S(2)}) collective-permute-start(s32[4,1408]{1,0:T(4,128)S(1)} %combine.1.rest_0_), channel_id=1, source_target_pairs={{0,8},{4,12},{8,0},{12,4},{1,9},{5,13},{9,1},{13,5},{2,10},{6,14},... | collective-permute-start | bytes 67592 | tf_op jit(solution)/shard_map/ppermute | solution.py:326

commit v11 on v10

--- a/solution.py
+++ b/solution.py
@@ -159,29 +159,30 @@
         make_table(vertex_ref, early_ref, first + step * lanes, step * lanes)
 
     matrix_copy.wait()
-    chunk = 4 * lanes
-    for start in range(0, vertices_local, chunk):
+    late = vertices_local - early
+    tiles = list(range(0, late, lanes))
+    green = 0.0
+    for start, table_ref, beside in (
+        (0, early_ref, tiles[: len(tiles) // 2]),
+        (early, late_ref, tiles[len(tiles) // 2 :]),
+    ):
+        size = table_ref.shape[1]
         left_product = jnp.dot(
-            left_ref[...], matrix_ref[:, start : start + chunk], preferred_element_type=jnp.float32
+            left_ref[...], matrix_ref[:, start : start + size], preferred_element_type=jnp.float32
         )
+        for tile in beside:
+            make_table(vertex_ref, late_ref, first + early + tile, tile)
         high = left_product.astype(jnp.bfloat16)
-        weight_ref[:window_rows, start : start + chunk] = high
-        weight_ref[window_rows:, start : start + chunk] = (
+        weight_ref[:window_rows, start : start + size] = high
+        weight_ref[window_rows:, start : start + size] = (
             left_product - high.astype(jnp.float32)
         ).astype(jnp.bfloat16)
-    green, start = 0.0, 0
-    for table_ref in (early_ref, late_ref):
-        size = table_ref.shape[1]
-        if table_ref is not early_ref:
-            for tile in range(0, size, lanes):
-                make_table(vertex_ref, table_ref, first + start + tile, tile)
         green += lax.dot_general(
             table_ref[...],
             weight_ref[:, start : start + size],
             (((1,), (1,)), ((), ())),
             preferred_element_type=jnp.float32,
         )
-        start += size
     green = green.T
     green = green[:window_rows] + green[window_rows:]
     rows_each = blk_count * rows_own

time: 20.3 us -> 20.3 us (level)
  no operation moved by 1% of the time
where the time goes in v11:
time: 20.3 us; the launch traced here: 20.2 us
  starting transfers between devices  7.61 us (37%)
  Pallas kernels  7 us (34%)
  waiting for transfers between devices  5.55 us (27%)
    ppermute x6, starting transfers between devices, exchange(): arrived[i] = lax.ppermute(pieces[i], axes, route)  7.61 us
    ppermute x6, waiting for transfers between devices, exchange(): arrived[i] = lax.ppermute(pieces[i], axes, route)  5.55 us
    pallas_call x1, Pallas kernels, local(): pl.pallas_call(functools.partial(transform_kernel, sizes), out_shape=[jax...  3.82 us
    pallas_call x3, Pallas kernels, local(): pl.pallas_call(functools.partial(accumulate_kernel, sizes, places, last),...  3.07 us
  transfers between devices with their start and end apart: 6, of which 5 were waited for; matrix products, arithmetic and copies ran while one was open for 0% of the time, Pallas kernels for 9%

profile of v11, /device:TPU:0, one launch (start us, length us, event | category | flops | bytes accessed | tf_op | source)
XLA Modules:
  0.0 20.2 jit_solution(16773816240351594929)
XLA Ops:
  0.0 0.0 copy-start
  0.0 0.0 copy-start.1
  0.0 0.0 copy-start.2
  0.0 3.8 %transform.1 = (s32[4,1408]{1,0:T(4,128)S(1)}, s32[4,1408]{1,0:T(4,128)S(1)}, s32[4,1408]{1,0:T(4,128)S(1)}, s32[4,1408]{1,0:T(4,128)S(1)}) custom-call(bf16[1,1024,2048]{2,1,0:T(8,128)(2,1)} %matrix_hbm.1, s32[1,2048]{1,0:T(1,128)} %vertex_hbm.1), custom_call_target="tpu_custom_call" | custom-call | tf_op jit(solution)/shard_map/transform/pallas_call | solution.py:343
  3.8 0.5 %collective-permute-start = (s32[4,1408]{1,0:T(4,128)S(1)}, s32[4,1408]{1,0:T(4,128)S(1)}, u32[]{:S(2)}, u32[]{:S(2)}) collective-permute-start(s32[4,1408]{1,0:T(4,128)S(1)} %get-tuple-element.10), channel_id=1, source_target_pairs={{0,1},{1,0},{2,3},{3,2},{4,5},{5,4},{6,7},{7,6},{8,9},{9,8},{10,11... | collective-permute-start | bytes 67592 | tf_op jit(solution)/shard_map/ppermute | solution.py:327
  4.4 2.6 %collective-permute-start.1 = (s32[4,1408]{1,0:T(4,128)S(1)}, s32[4,1408]{1,0:T(4,128)S(1)}, u32[]{:S(2)}, u32[]{:S(2)}) collective-permute-start(s32[4,1408]{1,0:T(4,128)S(1)} %get-tuple-element.11), channel_id=1, source_target_pairs={{0,2},{1,3},{2,0},{3,1},{4,6},{5,7},{6,4},{7,5},{8,10},{9,11},{10,... | collective-permute-start | bytes 67592 | tf_op jit(solution)/shard_map/ppermute | solution.py:327
  6.9 0.1 collective-permute-start.2
  7.0 0.0 collective-permute-done.refs_1_
  7.0 1.7 %collective-permute-done.1.refs_2_ = s32[4,1408]{1,0:T(4,128)S(1)} collective-permute-done((s32[4,1408]{1,0:T(4,128)S(1)}, s32[4,1408]{1,0:T(4,128)S(1)}, u32[]{:S(2)}, u32[]{:S(2)}) %collective-permute-start.1) | collective-permute-done | bytes 22560 | tf_op jit(solution)/shard_map/ppermute | solution.py:327
  8.7 1.4 %collective-permute-done.2.refs_3_ = s32[4,1408]{1,0:T(4,128)S(1)} collective-permute-done((s32[4,1408]{1,0:T(4,128)S(1)}, s32[4,1408]{1,0:T(4,128)S(1)}, u32[]{:S(2)}, u32[]{:S(2)}) %collective-permute-start.2) | collective-permute-done | bytes 22560 | tf_op jit(solution)/shard_map/ppermute | solution.py:327
  10.2 0.1 combine.1.rest_0_
  10.3 3.7 %collective-permute-start.3 = (s32[4,1408]{1,0:T(4,128)S(1)}, s32[4,1408]{1,0:T(4,128)S(1)}, u32[]{:S(2)}, u32[]{:S(2)}) collective-permute-start(s32[4,1408]{1,0:T(4,128)S(1)} %combine.1.rest_0_), channel_id=1, source_target_pairs={{0,12},{4,8},{8,4},{12,0},{1,13},{5,9},{9,5},{13,1},{2,14},{6,10},... | collective-permute-start | bytes 67592 | tf_op jit(solution)/shard_map/ppermute | solution.py:327
  13.9 0.0 collective-permute-start.4
  13.9 0.8 %collective-permute-start.5 = (s32[4,1408]{1,0:T(4,128)S(1)}, s32[4,1408]{1,0:T(4,128)S(1)}, u32[]{:S(2)}, u32[]{:S(2)}) collective-permute-start(s32[4,1408]{1,0:T(4,128)S(1)} %combine.1.rest_0_), channel_id=1, source_target_pairs={{0,8},{4,12},{8,0},{12,4},{1,9},{5,13},{9,1},{13,5},{2,10},{6,14},... | collective-permute-start | bytes 67592 | tf_op jit(solution)/shard_map/ppermute | solution.py:327
  14.7 1.2 %collective-permute-done.3.rest_1_ = s32[4,1408]{1,0:T(4,128)S(1)} collective-permute-done((s32[4,1408]{1,0:T(4,128)S(1)}, s32[4,1408]{1,0:T(4,128)S(1)}, u32[]{:S(2)}, u32[]{:S(2)}) %collective-permute-start.3) | collective-permute-done | bytes 22560 | tf_op jit(solution)/shard_map/ppermute | solution.py:327
  15.9 0.0 copy-done
  15.9 0.0 copy-done.1
  15.9 0.0 copy-done.2
  15.9 1.1 %accumulate.3.old_ref = f32[1,16,2560]{2,1,0:T(8,128)S(1)} custom-call(f32[1,4]{1,0:T(1,128)S(1)} %bitcast.1, s32[16,2560]{1,0:T(8,128)S(1)} %copy-done, f32[1,16,2560]{2,1,0:T(8,128)S(1)} %copy-done.1, s32[4,1408]{1,0:T(4,128)S(1)} %combine.1.rest_0_, s32[4,1408]{1,0:T(4,128)S(1)} %collective-permute-done.3.rest_1_), custom_call_target="tpu_custom_call" | custom-call | flops 81920000 | bytes 491520 | tf_op jit(solution)/shard_map/accumulate/pallas_call | solution.py:389
  17.0 0.8 %collective-permute-done.4.rest_0_ = s32[4,1408]{1,0:T(4,128)S(1)} collective-permute-done((s32[4,1408]{1,0:T(4,128)S(1)}, s32[4,1408]{1,0:T(4,128)S(1)}, u32[]{:S(2)}, u32[]{:S(2)}) %collective-permute-start.4) | collective-permute-done | bytes 22560 | tf_op jit(solution)/shard_map/ppermute | solution.py:327
  17.8 0.7 %accumulate.4.old_ref = f32[1,16,2560]{2,1,0:T(8,128)S(1)} custom-call(f32[1,4]{1,0:T(1,128)S(1)} %bitcast.2, s32[16,2560]{1,0:T(8,128)S(1)} %copy-done, f32[1,16,2560]{2,1,0:T(8,128)S(1)} %accumulate.3.old_ref, s32[4,1408]{1,0:T(4,128)S(1)} %collective-permute-done.4.rest_0_), custom_call_target="tpu_custom_call" | custom-call | flops 40960000 | bytes 491520 | tf_op jit(solution)/shard_map/accumulate/pallas_call | solution.py:389
  18.5 0.4 %collective-permute-done.5.rest_0_ = s32[4,1408]{1,0:T(4,128)S(1)} collective-permute-done((s32[4,1408]{1,0:T(4,128)S(1)}, s32[4,1408]{1,0:T(4,128)S(1)}, u32[]{:S(2)}, u32[]{:S(2)}) %collective-permute-start.5) | collective-permute-done | bytes 22560 | tf_op jit(solution)/shard_map/ppermute | solution.py:327
  18.9 1.3 %accumulate.5 = f32[1,16,2560]{2,1,0:T(8,128)} custom-call(f32[1,4]{1,0:T(1,128)S(1)} %bitcast.3, s32[16,2560]{1,0:T(8,128)S(1)} %copy-done, f32[1,16,2560]{2,1,0:T(8,128)S(1)} %accumulate.4.old_ref, s32[4,1408]{1,0:T(4,128)S(1)} %collective-permute-done.5.rest_0_), custom_call_target="tpu_custom_call" | custom-call | flops 40960000 | bytes 491520 | tf_op jit(solution)/shard_map/accumulate/pallas_call | solution.py:389
Async XLA Ops:
  0.0 15.9 %copy-start = (s32[16,2560]{1,0:T(8,128)S(1)}, s32[16,2560]{1,0:T(8,128)}, u32[]{:S(2)}) copy-start(s32[16,2560]{1,0:T(8,128)} %transfer_ref.5) | copy-start | bytes 491524
  0.0 15.9 %copy-start.1 = (f32[1,16,2560]{2,1,0:T(8,128)S(1)}, f32[1,16,2560]{2,1,0:T(8,128)}, u32[]{:S(2)}) copy-start(f32[1,16,2560]{2,1,0:T(8,128)} %old_ref.1) | copy-start | bytes 491524
  0.0 15.9 %copy-start.2 = (f32[4]{0:T(128)S(1)}, f32[4]{0:T(128)}, u32[]{:S(2)}) copy-start(f32[4]{0:T(128)} %param.7) | copy-start | bytes 52
  3.8 3.2 %collective-permute-start = (s32[4,1408]{1,0:T(4,128)S(1)}, s32[4,1408]{1,0:T(4,128)S(1)}, u32[]{:S(2)}, u32[]{:S(2)}) collective-permute-start(s32[4,1408]{1,0:T(4,128)S(1)} %get-tuple-element.10), channel_id=1, source_target_pairs={{0,1},{1,0},{2,3},{3,2},{4,5},{5,4},{6,7},{7,6},{8,9},{9,8},{10,11... | collective-permute-start | bytes 67592 | tf_op jit(solution)/shard_map/ppermute | solution.py:327
  4.4 4.3 %collective-permute-start.1 = (s32[4,1408]{1,0:T(4,128)S(1)}, s32[4,1408]{1,0:T(4,128)S(1)}, u32[]{:S(2)}, u32[]{:S(2)}) collective-permute-start(s32[4,1408]{1,0:T(4,128)S(1)} %get-tuple-element.11), channel_id=1, source_target_pairs={{0,2},{1,3},{2,0},{3,1},{4,6},{5,7},{6,4},{7,5},{8,10},{9,11},{10,... | collective-permute-start | bytes 67592 | tf_op jit(solution)/shard_map/ppermute | solution.py:327
  6.9 3.2 %collective-permute-start.2 = (s32[4,1408]{1,0:T(4,128)S(1)}, s32[4,1408]{1,0:T(4,128)S(1)}, u32[]{:S(2)}, u32[]{:S(2)}) collective-permute-start(s32[4,1408]{1,0:T(4,128)S(1)} %get-tuple-element.12), channel_id=1, source_target_pairs={{0,3},{1,2},{2,1},{3,0},{4,7},{5,6},{6,5},{7,4},{8,11},{9,10},{10,... | collective-permute-start | bytes 67592 | tf_op jit(solution)/shard_map/ppermute | solution.py:327
  10.3 5.7 %collective-permute-start.3 = (s32[4,1408]{1,0:T(4,128)S(1)}, s32[4,1408]{1,0:T(4,128)S(1)}, u32[]{:S(2)}, u32[]{:S(2)}) collective-permute-start(s32[4,1408]{1,0:T(4,128)S(1)} %combine.1.rest_0_), channel_id=1, source_target_pairs={{0,12},{4,8},{8,4},{12,0},{1,13},{5,9},{9,5},{13,1},{2,14},{6,10},... | collective-permute-start | bytes 67592 | tf_op jit(solution)/shard_map/ppermute | solution.py:327
  13.9 3.9 %collective-permute-start.4 = (s32[4,1408]{1,0:T(4,128)S(1)}, s32[4,1408]{1,0:T(4,128)S(1)}, u32[]{:S(2)}, u32[]{:S(2)}) collective-permute-start(s32[4,1408]{1,0:T(4,128)S(1)} %combine.1.rest_0_), channel_id=1, source_target_pairs={{0,4},{4,0},{8,12},{12,8},{1,5},{5,1},{9,13},{13,9},{2,6},{6,2},{1... | collective-permute-start | bytes 67592 | tf_op jit(solution)/shard_map/ppermute | solution.py:327
  13.9 4.9 %collective-permute-start.5 = (s32[4,1408]{1,0:T(4,128)S(1)}, s32[4,1408]{1,0:T(4,128)S(1)}, u32[]{:S(2)}, u32[]{:S(2)}) collective-permute-start(s32[4,1408]{1,0:T(4,128)S(1)} %combine.1.rest_0_), channel_id=1, source_target_pairs={{0,8},{4,12},{8,0},{12,4},{1,9},{5,13},{9,1},{13,5},{2,10},{6,14},... | collective-permute-start | bytes 67592 | tf_op jit(solution)/shard_map/ppermute | solution.py:327
